TPU v7x, 128 devices: a whole 4x4x4 slice. The times are simulated.
128 devices in a mesh: comp: 4 (over y_lo, core), tile: 32 (over x, z, y_hi).
Axes of the slice: x: 4, y: 4 (y_hi: 2, y_lo: 2; y = y_hi * 2 + y_lo), z: 4, core: 2. Of those that a mesh axis runs over, the one named last changes fastest.
Arguments:
- state: float32 [2, 8, 256, 16384], P(None, None, 'comp', 'tile'), may hold values from -6 to 6
- courant: float32 [8, 256], P(None, 'comp'), may hold values from -0.9 to 0.9
- mixing: float32 [7, 256], P(None, 'comp'), may hold values from 0.05 to 0.24
- exchange_coef: float32 [256, 16384], P('comp', 'tile'), may hold values from 0.2 to 0.8
- sea_mask: int32 [256, 16384], P('comp', 'tile'), may hold values 0 or 1
- margin_count: int32 [4, 32, 3, 4], P('comp', 'tile'), may hold values from 0 to 4096, as said below
- margin_row: int32 [4, 32, 3, 4, 4096], P('comp', 'tile'), may hold values from 0 to 63
- margin_col: int32 [4, 32, 3, 4, 4096], P('comp', 'tile'), may hold values from 0 to 511, as said below
- margin_weight: float32 [4, 32, 3, 4, 4096], P('comp', 'tile'), may hold values from 0.05 to 0.6
Outputs:
- new_state: float32 [2, 8, 256, 16384], P(None, None, 'comp', 'tile')
- partner_surface: float32 [2, 256, 16384], P(None, 'comp', 'tile')
Inputs may be any that keep to these rules, and one draw needn't show every extreme that they name: margin_count[g, t, o, h] equals margin_count[h, (t + o - 1) mod 32, 2 - o, g], and row r of the one list is the same margin as row r of the other. Only pairs of one atmosphere device (comp index below 3) and one ocean device have rows: an atmosphere device couples with the three ocean devices at tile offsets -1, 0 and 1, an ocean device with the atmosphere devices at those offsets; every such pair has at least 3584 rows. `margin_col`: for list index o = 0 (partner to the west) the columns lie below 128, for o = 2 (partner to the east) at 384 or above.
All inputs are finite; a program needn't handle non-finite values. No bound on the sum of `sea_mask` on one device may be relied on, other than what follows from the above.
Results may differ from a plain program's by a relative error of at most 0.0003.
Values sent between devices are 32-bit elements; how exact they have to be, the bound alone decides.
No kernel may reach another device: no remote copies, remote signals or barrier semaphores. Data moves between devices by JAX's collectives and lax.ppermute only.
A program may use at most 64 MiB of HBM per device.

v0:
```python
import jax
import jax.numpy as jnp
from jax import lax
from jax.sharding import PartitionSpec as P

SUBSTEPS = 2


def with_halo(block, sides, width):
    for axis, dim in sides:
        count = lax.axis_size(axis)
        forward = [(i, i + 1) for i in range(count - 1)]
        forward.append((count - 1, 0))
        backward = [(target, source) for source, target in forward]
        low = lax.ppermute(
            lax.slice_in_dim(block, block.shape[dim] - width, None, axis=dim), axis, forward
        )
        high = lax.ppermute(lax.slice_in_dim(block, 0, width, axis=dim), axis, backward)
        block = jnp.concatenate([low, block, high], axis=dim)
    return block


def transport(padded, speed):
    left = padded[..., :-2]
    middle = padded[..., 1:-1]
    right = padded[..., 2:]
    return (
        middle - 0.5 * speed * (right - left) + 0.5 * speed * speed * (right - 2.0 * middle + left)
    )


def vertical_mix(field, coeff):
    jump_up = field[:, 1:] - field[:, :-1]
    flux = coeff[None, :, :, None] * jump_up
    empty = jnp.zeros_like(flux[:, :1])
    upper = jnp.concatenate([flux, empty], axis=1)
    lower = jnp.concatenate([empty, flux], axis=1)
    return field + upper - lower


def shards(
    state,
    courant,
    mixing,
    exchange_coef,
    sea_mask,
    margin_count,
    margin_row,
    margin_col,
    margin_weight,
):
    field_count, level_count, row_count, col_count = state.shape
    slot_count = margin_row.shape[-1]
    comp_peers = margin_row.shape[3]
    list_count = 3 * comp_peers
    tile_total = lax.axis_size("tile")
    tile_here = lax.axis_index("tile")
    surface_rows = state[:, 0].reshape(field_count * row_count, col_count)
    row_lists = margin_row.reshape(list_count, slot_count)
    col_lists = margin_col.reshape(list_count, slot_count)
    counts = margin_count.reshape(list_count)
    row_iota = jnp.arange(row_count, dtype=jnp.int32)[:, None]
    col_iota = jnp.arange(col_count, dtype=jnp.int32)[:, None]
    slot_iota = jnp.arange(slot_count, dtype=jnp.int32)

    def pick_list(carry, parts):
        row_list, col_list, count_one = parts
        col_table = (col_iota == col_list[None, :]).astype(jnp.float32)
        picked = jnp.dot(
            surface_rows,
            col_table,
            precision=lax.Precision.HIGHEST,
            preferred_element_type=jnp.float32,
        )
        picked = picked.reshape(field_count, row_count, slot_count)
        row_match = row_iota == row_list[None, :]
        values = jnp.sum(jnp.where(row_match[None], picked, 0.0), axis=1)
        values = jnp.where((slot_iota < count_one)[None, :], values, 0.0)
        return (carry, values)

    unused, picked_all = lax.scan(pick_list, 0, (row_lists, col_lists, counts))
    outgoing = jnp.transpose(
        picked_all.reshape(3, comp_peers, field_count, slot_count), (2, 0, 1, 3)
    )
    partner_tiles = (tile_here + jnp.arange(3, dtype=jnp.int32) - 1) % tile_total
    tile_table = partner_tiles[:, None] == jnp.arange(tile_total, dtype=jnp.int32)[None, :]
    spread = jnp.where(tile_table[None, :, None, :, None], outgoing[:, :, :, None, :], 0.0)
    blocks = jnp.sum(spread, axis=1).reshape(field_count, comp_peers * tile_total, slot_count)
    arrived = lax.all_to_all(blocks, ("comp", "tile"), split_axis=1, concat_axis=1, tiled=True)
    arrived = arrived.reshape(field_count, comp_peers, tile_total, slot_count)
    chosen = jnp.where(tile_table[None, :, None, :, None], arrived[:, None], 0.0)
    incoming = jnp.sum(chosen, axis=3)
    speed = courant[:, :, None]
    field = state
    for step in range(SUBSTEPS):
        padded = with_halo(field, (("tile", 3),), 1)
        field = vertical_mix(transport(padded, speed), mixing)
    weights = margin_weight.reshape(3, comp_peers, slot_count)
    terms = jnp.transpose(
        (incoming * weights[None]).reshape(field_count, list_count, slot_count), (1, 0, 2)
    )

    def land_list(total, parts):
        row_list, col_list, term_one = parts
        col_table = (col_iota == col_list[None, :]).astype(jnp.float32)
        row_match = row_iota == row_list[None, :]
        spread = jnp.where(row_match[None], term_one[:, None, :], 0.0).reshape(
            field_count * row_count, slot_count
        )
        landed = lax.dot_general(
            spread,
            col_table,
            (((1,), (1,)), ((), ())),
            precision=lax.Precision.HIGHEST,
            preferred_element_type=jnp.float32,
        )
        return (total + landed, 0)

    start_total = jnp.zeros((field_count * row_count, col_count), jnp.float32)
    partner, unused_two = lax.scan(land_list, start_total, (row_lists, col_lists, terms))
    partner = partner.reshape(field_count, row_count, col_count)
    ocean = lax.axis_index("comp") == lax.axis_size("comp") - 1
    rate = exchange_coef * sea_mask.astype(jnp.float32)
    first_own = field[0, 0]
    second_own = field[1, 0]
    first_far = partner[0]
    second_far = partner[1]
    new_first = first_own + rate * (first_far - first_own)
    air_second = second_own + rate * (1.2 * first_far - 0.3 * second_far - second_own)
    sea_second = second_own + rate * (1.2 * first_own - second_far)
    new_second = jnp.where(ocean, sea_second, air_second)
    field = field.at[:, 0].set(jnp.stack([new_first, new_second]))
    return (field, partner)


def solution(mesh):
    in_specs = (
        P(None, None, "comp", "tile"),
        P(None, "comp"),
        P(None, "comp"),
        P("comp", "tile"),
        P("comp", "tile"),
        P("comp", "tile", None, None),
        P("comp", "tile", None, None, None),
        P("comp", "tile", None, None, None),
        P("comp", "tile", None, None, None),
    )
    out_specs = (P(None, None, "comp", "tile"), P(None, "comp", "tile"))
    return jax.shard_map(shards, mesh=mesh, in_specs=in_specs, out_specs=out_specs, check_vma=False)
```

profile of v0, /device:TPU:9, one launch (start us, length us, event | category | flops | bytes accessed | tf_op | source)
XLA Modules:
  0.0 271.1 jit_solution(11563903709708179939)
XLA Ops:
  4.4 55.5 %while.23 = (s32[]{:T(128)}, f32[12,2,4096]{2,1,0:T(2,128)S(1)}, s32[12]{0:T(128)S(1)}, s32[12,4096]{1,0:T(8,128)S(1)}, s32[12,4096]{1,0:T(8,128)S(1)}, /*index=5*/f32[128,512]{1,0:T(8,128)S(1)}, s32[]{:T(128)}) while((s32[]{:T(128)}, f32[12,2,4096]{2,1,0:T(2,128)S(1)}, s32[12]{0:T(128)S(1)}, s32[12,4096]{1,0:T(8,128)S(1)}, ...), condition=%wide.region_2.3_spmd.clone, body=%wide.region_0.2_spmd.clone.sunk | while | flops 3224637440 | bytes 991333 | solution.py:81
  9.2 3.1 %select_reduce_fusion.4 = f32[2,4096]{1,0:T(2,128)S(1)} fusion(pred[64,4096]{1,0:T(8,128)(4,1)S(1)} %iota_compare_fusion.14, f32[128,512]{1,0:T(8,128)S(1)} %get-tuple-element.267, s32[4096]{0:T(1024)S(1)} %bitcast.74), kind=kOutput, calls=%fused_computation.8.clone.1 | convolution fusion | flops 3224363008 | bytes 573440 | tf_op jit(solution)/shard_map/while/body/eval_jaxpr/dot_general | solution.py:69
  13.8 3.1 %select_reduce_fusion.4 = f32[2,4096]{1,0:T(2,128)S(1)} fusion(pred[64,4096]{1,0:T(8,128)(4,1)S(1)} %iota_compare_fusion.14, f32[128,512]{1,0:T(8,128)S(1)} %get-tuple-element.267, s32[4096]{0:T(1024)S(1)} %bitcast.74), kind=kOutput, calls=%fused_computation.8.clone.1 | convolution fusion | flops 3224363008 | bytes 573440 | tf_op jit(solution)/shard_map/while/body/eval_jaxpr/dot_general | solution.py:69
  18.5 3.1 %select_reduce_fusion.4 = f32[2,4096]{1,0:T(2,128)S(1)} fusion(pred[64,4096]{1,0:T(8,128)(4,1)S(1)} %iota_compare_fusion.14, f32[128,512]{1,0:T(8,128)S(1)} %get-tuple-element.267, s32[4096]{0:T(1024)S(1)} %bitcast.74), kind=kOutput, calls=%fused_computation.8.clone.1 | convolution fusion | flops 3224363008 | bytes 573440 | tf_op jit(solution)/shard_map/while/body/eval_jaxpr/dot_general | solution.py:69
  23.1 3.1 %select_reduce_fusion.4 = f32[2,4096]{1,0:T(2,128)S(1)} fusion(pred[64,4096]{1,0:T(8,128)(4,1)S(1)} %iota_compare_fusion.14, f32[128,512]{1,0:T(8,128)S(1)} %get-tuple-element.267, s32[4096]{0:T(1024)S(1)} %bitcast.74), kind=kOutput, calls=%fused_computation.8.clone.1 | convolution fusion | flops 3224363008 | bytes 573440 | tf_op jit(solution)/shard_map/while/body/eval_jaxpr/dot_general | solution.py:69
  27.7 3.1 %select_reduce_fusion.4 = f32[2,4096]{1,0:T(2,128)S(1)} fusion(pred[64,4096]{1,0:T(8,128)(4,1)S(1)} %iota_compare_fusion.14, f32[128,512]{1,0:T(8,128)S(1)} %get-tuple-element.267, s32[4096]{0:T(1024)S(1)} %bitcast.74), kind=kOutput, calls=%fused_computation.8.clone.1 | convolution fusion | flops 3224363008 | bytes 573440 | tf_op jit(solution)/shard_map/while/body/eval_jaxpr/dot_general | solution.py:69
  32.3 3.1 %select_reduce_fusion.4 = f32[2,4096]{1,0:T(2,128)S(1)} fusion(pred[64,4096]{1,0:T(8,128)(4,1)S(1)} %iota_compare_fusion.14, f32[128,512]{1,0:T(8,128)S(1)} %get-tuple-element.267, s32[4096]{0:T(1024)S(1)} %bitcast.74), kind=kOutput, calls=%fused_computation.8.clone.1 | convolution fusion | flops 3224363008 | bytes 573440 | tf_op jit(solution)/shard_map/while/body/eval_jaxpr/dot_general | solution.py:69
  36.9 3.1 %select_reduce_fusion.4 = f32[2,4096]{1,0:T(2,128)S(1)} fusion(pred[64,4096]{1,0:T(8,128)(4,1)S(1)} %iota_compare_fusion.14, f32[128,512]{1,0:T(8,128)S(1)} %get-tuple-element.267, s32[4096]{0:T(1024)S(1)} %bitcast.74), kind=kOutput, calls=%fused_computation.8.clone.1 | convolution fusion | flops 3224363008 | bytes 573440 | tf_op jit(solution)/shard_map/while/body/eval_jaxpr/dot_general | solution.py:69
  41.6 3.1 %select_reduce_fusion.4 = f32[2,4096]{1,0:T(2,128)S(1)} fusion(pred[64,4096]{1,0:T(8,128)(4,1)S(1)} %iota_compare_fusion.14, f32[128,512]{1,0:T(8,128)S(1)} %get-tuple-element.267, s32[4096]{0:T(1024)S(1)} %bitcast.74), kind=kOutput, calls=%fused_computation.8.clone.1 | convolution fusion | flops 3224363008 | bytes 573440 | tf_op jit(solution)/shard_map/while/body/eval_jaxpr/dot_general | solution.py:69
  55.4 3.1 %select_reduce_fusion.4 = f32[2,4096]{1,0:T(2,128)S(1)} fusion(pred[64,4096]{1,0:T(8,128)(4,1)S(1)} %iota_compare_fusion.14, f32[128,512]{1,0:T(8,128)S(1)} %get-tuple-element.267, s32[4096]{0:T(1024)S(1)} %bitcast.74), kind=kOutput, calls=%fused_computation.8.clone.1 | convolution fusion | flops 3224363008 | bytes 573440 | tf_op jit(solution)/shard_map/while/body/eval_jaxpr/dot_general | solution.py:69
  62.1 5.2 %copy.20 = f32[2,128,4096]{2,0,1:T(2,128)} copy(f32[2,128,4096]{2,1,0:T(8,128)S(1)} %bitcast.69) | data formatting | bytes 8388608 | tf_op jit(solution)/shard_map/reshape | solution.py:88
  67.3 11.2 %all-to-all-start = ((f32[2,128,4096]{2,0,1:T(2,128)}), f32[2,128,4096]{2,0,1:T(2,128)}, u32[]{:S(2)}, u32[]{:S(2)}) async-start(f32[2,128,4096]{2,0,1:T(2,128)} %copy.20), calls=%async_computation | async-start | bytes 8388608 | tf_op jit(solution)/shard_map/all_to_all | solution.py:89
  78.7 7.0 %collective-permute-start = (f32[2,8,64,1]{3,2,1,0:T(8,128)S(1)}, f32[2,8,64,1]{3,2,1,0:T(8,128)S(1)}, u32[]{:S(2)}, u32[]{:S(2)}) collective-permute-start(f32[2,8,64,1]{3,2,1,0:T(8,128)S(1)} %get-tuple-element.169), channel_id=1, source_target_pairs={{1,0},{2,1},{3,2},{4,3},{5,4},{6,5},{7,6},{8,7},{9,8},{10,9},{11,1... | collective-permute-start | bytes 12296 | tf_op jit(solution)/shard_map/ppermute | solution.py:18
  85.7 52.9 %collective-permute-done = f32[2,8,64,1]{3,2,1,0:T(8,128)S(1)} collective-permute-done((f32[2,8,64,1]{3,2,1,0:T(8,128)S(1)}, f32[2,8,64,1]{3,2,1,0:T(8,128)S(1)}, u32[]{:S(2)}, u32[]{:S(2)}) %collective-permute-start) | collective-permute-done | bytes 4128 | tf_op jit(solution)/shard_map/ppermute | solution.py:18
  138.7 12.4 %collective-permute-done.1 = f32[2,8,64,1]{3,2,1,0:T(8,128)S(1)} collective-permute-done((f32[2,8,64,1]{3,2,1,0:T(8,128)S(1)}, f32[2,8,64,1]{3,2,1,0:T(8,128)S(1)}, u32[]{:S(2)}, u32[]{:S(2)}) %collective-permute-start.1) | collective-permute-done | bytes 4128 | tf_op jit(solution)/shard_map/ppermute | solution.py:15
  157.2 3.8 %collective-permute-start.2 = (f32[2,8,64,1]{3,2,1,0:T(8,128)}, f32[2,8,64,1]{3,2,1,0:T(8,128)S(1)}, u32[]{:S(2)}, u32[]{:S(2)}) collective-permute-start(f32[2,8,64,1]{3,2,1,0:T(8,128)} %get-tuple-element.167), channel_id=1, source_target_pairs={{1,0},{2,1},{3,2},{4,3},{5,4},{6,5},{7,6},{8,7},{9,8},{10,9},{11,1... | collective-permute-start | bytes 12296 | tf_op jit(solution)/shard_map/ppermute | solution.py:18
  162.0 10.5 %collective-permute-done.2 = f32[2,8,64,1]{3,2,1,0:T(8,128)S(1)} collective-permute-done((f32[2,8,64,1]{3,2,1,0:T(8,128)}, f32[2,8,64,1]{3,2,1,0:T(8,128)S(1)}, u32[]{:S(2)}, u32[]{:S(2)}) %collective-permute-start.2) | collective-permute-done | bytes 4128 | tf_op jit(solution)/shard_map/ppermute | solution.py:18
  172.6 11.4 %collective-permute-done.3 = f32[2,8,64,1]{3,2,1,0:T(8,128)S(1)} collective-permute-done((f32[2,8,64,1]{3,2,1,0:T(8,128)}, f32[2,8,64,1]{3,2,1,0:T(8,128)S(1)}, u32[]{:S(2)}, u32[]{:S(2)}) %collective-permute-start.3) | collective-permute-done | bytes 4128 | tf_op jit(solution)/shard_map/ppermute | solution.py:15
  188.6 4.6 %copy.21 = f32[2,4,32,4096]{3,2,1,0:T(8,128)S(1)} copy(f32[2,4,32,4096]{3,0,2,1:T(2,128)} %bitcast.5) | data formatting | bytes 8388608 | tf_op jit(solution)/shard_map/jit(_where)/broadcast_in_dim | solution.py:91
  195.4 73.8 %while.24 = (s32[]{:T(128)}, f32[128,512]{1,0:T(8,128)S(1)}, s32[12,4096]{1,0:T(8,128)}, f32[12,2,4096]{2,1,0:T(2,128)S(1)}, s32[12,4096]{1,0:T(8,128)}, /*index=5*/s32[]{:T(128)}, s32[]{:T(128)}) while((s32[]{:T(128)}, f32[128,512]{1,0:T(8,128)S(1)}, s32[12,4096]{1,0:T(8,128)}, f32[12,2,4096]{2,1,0:T(2,128)S(1)}, ...), condition=%wide.region_6.7_spmd.clone, body=%wide.region_5.6_spmd.clone.sunk | while | flops 3224240128 | bytes 5439583 | solution.py:120
  196.9 4.7 %fusion.32 = f32[128,512]{1,0:T(8,128)S(1)} fusion(f32[128,4096]{1,0:T(8,128)S(1)} %bitcast.68, s32[4096]{0:T(1024)S(1)} %bitcast.73, f32[128,512]{1,0:T(8,128)S(1)} %get-tuple-element.277, pred[]{:T(512)S(6)} %compare.17), kind=kOutput, calls=%fused_computation.18.clone.1 | convolution fusion | flops 3223453696 | bytes 2637825 | tf_op jit(solution)/shard_map/while/body/eval_jaxpr/dot_general | solution.py:110
  203.0 4.7 %fusion.32 = f32[128,512]{1,0:T(8,128)S(1)} fusion(f32[128,4096]{1,0:T(8,128)S(1)} %bitcast.68, s32[4096]{0:T(1024)S(1)} %bitcast.73, f32[128,512]{1,0:T(8,128)S(1)} %get-tuple-element.277, pred[]{:T(512)S(6)} %compare.17), kind=kOutput, calls=%fused_computation.18.clone.1 | convolution fusion | flops 3223453696 | bytes 2637825 | tf_op jit(solution)/shard_map/while/body/eval_jaxpr/dot_general | solution.py:110
  209.2 4.7 %fusion.32 = f32[128,512]{1,0:T(8,128)S(1)} fusion(f32[128,4096]{1,0:T(8,128)S(1)} %bitcast.68, s32[4096]{0:T(1024)S(1)} %bitcast.73, f32[128,512]{1,0:T(8,128)S(1)} %get-tuple-element.277, pred[]{:T(512)S(6)} %compare.17), kind=kOutput, calls=%fused_computation.18.clone.1 | convolution fusion | flops 3223453696 | bytes 2637825 | tf_op jit(solution)/shard_map/while/body/eval_jaxpr/dot_general | solution.py:110
  215.3 4.7 %fusion.32 = f32[128,512]{1,0:T(8,128)S(1)} fusion(f32[128,4096]{1,0:T(8,128)S(1)} %bitcast.68, s32[4096]{0:T(1024)S(1)} %bitcast.73, f32[128,512]{1,0:T(8,128)S(1)} %get-tuple-element.277, pred[]{:T(512)S(6)} %compare.17), kind=kOutput, calls=%fused_computation.18.clone.1 | convolution fusion | flops 3223453696 | bytes 2637825 | tf_op jit(solution)/shard_map/while/body/eval_jaxpr/dot_general | solution.py:110
  221.5 4.7 %fusion.32 = f32[128,512]{1,0:T(8,128)S(1)} fusion(f32[128,4096]{1,0:T(8,128)S(1)} %bitcast.68, s32[4096]{0:T(1024)S(1)} %bitcast.73, f32[128,512]{1,0:T(8,128)S(1)} %get-tuple-element.277, pred[]{:T(512)S(6)} %compare.17), kind=kOutput, calls=%fused_computation.18.clone.1 | convolution fusion | flops 3223453696 | bytes 2637825 | tf_op jit(solution)/shard_map/while/body/eval_jaxpr/dot_general | solution.py:110
  227.6 4.7 %fusion.32 = f32[128,512]{1,0:T(8,128)S(1)} fusion(f32[128,4096]{1,0:T(8,128)S(1)} %bitcast.68, s32[4096]{0:T(1024)S(1)} %bitcast.73, f32[128,512]{1,0:T(8,128)S(1)} %get-tuple-element.277, pred[]{:T(512)S(6)} %compare.17), kind=kOutput, calls=%fused_computation.18.clone.1 | convolution fusion | flops 3223453696 | bytes 2637825 | tf_op jit(solution)/shard_map/while/body/eval_jaxpr/dot_general | solution.py:110
  233.8 4.7 %fusion.32 = f32[128,512]{1,0:T(8,128)S(1)} fusion(f32[128,4096]{1,0:T(8,128)S(1)} %bitcast.68, s32[4096]{0:T(1024)S(1)} %bitcast.73, f32[128,512]{1,0:T(8,128)S(1)} %get-tuple-element.277, pred[]{:T(512)S(6)} %compare.17), kind=kOutput, calls=%fused_computation.18.clone.1 | convolution fusion | flops 3223453696 | bytes 2637825 | tf_op jit(solution)/shard_map/while/body/eval_jaxpr/dot_general | solution.py:110
  239.9 4.7 %fusion.32 = f32[128,512]{1,0:T(8,128)S(1)} fusion(f32[128,4096]{1,0:T(8,128)S(1)} %bitcast.68, s32[4096]{0:T(1024)S(1)} %bitcast.73, f32[128,512]{1,0:T(8,128)S(1)} %get-tuple-element.277, pred[]{:T(512)S(6)} %compare.17), kind=kOutput, calls=%fused_computation.18.clone.1 | convolution fusion | flops 3223453696 | bytes 2637825 | tf_op jit(solution)/shard_map/while/body/eval_jaxpr/dot_general | solution.py:110
  246.1 4.7 %fusion.32 = f32[128,512]{1,0:T(8,128)S(1)} fusion(f32[128,4096]{1,0:T(8,128)S(1)} %bitcast.68, s32[4096]{0:T(1024)S(1)} %bitcast.73, f32[128,512]{1,0:T(8,128)S(1)} %get-tuple-element.277, pred[]{:T(512)S(6)} %compare.17), kind=kOutput, calls=%fused_computation.18.clone.1 | convolution fusion | flops 3223453696 | bytes 2637825 | tf_op jit(solution)/shard_map/while/body/eval_jaxpr/dot_general | solution.py:110
  252.2 4.7 %fusion.32 = f32[128,512]{1,0:T(8,128)S(1)} fusion(f32[128,4096]{1,0:T(8,128)S(1)} %bitcast.68, s32[4096]{0:T(1024)S(1)} %bitcast.73, f32[128,512]{1,0:T(8,128)S(1)} %get-tuple-element.277, pred[]{:T(512)S(6)} %compare.17), kind=kOutput, calls=%fused_computation.18.clone.1 | convolution fusion | flops 3223453696 | bytes 2637825 | tf_op jit(solution)/shard_map/while/body/eval_jaxpr/dot_general | solution.py:110
  258.3 4.7 %fusion.32 = f32[128,512]{1,0:T(8,128)S(1)} fusion(f32[128,4096]{1,0:T(8,128)S(1)} %bitcast.68, s32[4096]{0:T(1024)S(1)} %bitcast.73, f32[128,512]{1,0:T(8,128)S(1)} %get-tuple-element.277, pred[]{:T(512)S(6)} %compare.17), kind=kOutput, calls=%fused_computation.18.clone.1 | convolution fusion | flops 3223453696 | bytes 2637825 | tf_op jit(solution)/shard_map/while/body/eval_jaxpr/dot_general | solution.py:110
  264.5 4.7 %fusion.32 = f32[128,512]{1,0:T(8,128)S(1)} fusion(f32[128,4096]{1,0:T(8,128)S(1)} %bitcast.68, s32[4096]{0:T(1024)S(1)} %bitcast.73, f32[128,512]{1,0:T(8,128)S(1)} %get-tuple-element.277, pred[]{:T(512)S(6)} %compare.17), kind=kOutput, calls=%fused_computation.18.clone.1 | convolution fusion | flops 3223453696 | bytes 2637825 | tf_op jit(solution)/shard_map/while/body/eval_jaxpr/dot_general | solution.py:110
  (160 shorter events, 65.0 us)
Async XLA Ops:
  59.9 0.7 copy-start.2
  59.9 0.8 copy-start.3
  67.3 11.2 %copy-start = (f32[2,8,64,512]{3,2,1,0:T(8,128)S(1)}, f32[2,8,64,512]{3,2,1,0:T(8,128)}, u32[]{:S(2)}) copy-start(f32[2,8,64,512]{3,2,1,0:T(8,128)} %param.15) | copy-start | bytes 6291460
  67.3 121.3 %all-to-all-start = ((f32[2,128,4096]{2,0,1:T(2,128)}), f32[2,128,4096]{2,0,1:T(2,128)}, u32[]{:S(2)}, u32[]{:S(2)}) async-start(f32[2,128,4096]{2,0,1:T(2,128)} %copy.20), calls=%async_computation | async-start | bytes 8388608 | tf_op jit(solution)/shard_map/all_to_all | solution.py:89
  78.5 7.2 %copy-start.9 = (f32[8,64]{1,0:T(8,128)S(1)}, f32[8,64]{1,0:T(8,128)}, u32[]{:S(2)}) copy-start(f32[8,64]{1,0:T(8,128)} %param.16) | copy-start | bytes 6148
  78.7 59.9 %collective-permute-start = (f32[2,8,64,1]{3,2,1,0:T(8,128)S(1)}, f32[2,8,64,1]{3,2,1,0:T(8,128)S(1)}, u32[]{:S(2)}, u32[]{:S(2)}) collective-permute-start(f32[2,8,64,1]{3,2,1,0:T(8,128)S(1)} %get-tuple-element.169), channel_id=1, source_target_pairs={{1,0},{2,1},{3,2},{4,3},{5,4},{6,5},{7,6},{8,7},{9,8},{10,9},{11,1... | collective-permute-start | bytes 12296 | tf_op jit(solution)/shard_map/ppermute | solution.py:18
  85.7 65.3 %collective-permute-start.1 = (f32[2,8,64,1]{3,2,1,0:T(8,128)S(1)}, f32[2,8,64,1]{3,2,1,0:T(8,128)S(1)}, u32[]{:S(2)}, u32[]{:S(2)}) collective-permute-start(f32[2,8,64,1]{3,2,1,0:T(8,128)S(1)} %get-tuple-element.168), channel_id=1, source_target_pairs={{0,1},{1,2},{2,3},{3,4},{4,5},{5,6},{6,7},{7,8},{8,9},{9,10},{10,1... | collective-permute-start | bytes 12296 | tf_op jit(solution)/shard_map/ppermute | solution.py:15
  151.0 1.5 copy-start.8
  152.6 1.6 copy-start.1
  157.2 15.3 %collective-permute-start.2 = (f32[2,8,64,1]{3,2,1,0:T(8,128)}, f32[2,8,64,1]{3,2,1,0:T(8,128)S(1)}, u32[]{:S(2)}, u32[]{:S(2)}) collective-permute-start(f32[2,8,64,1]{3,2,1,0:T(8,128)} %get-tuple-element.167), channel_id=1, source_target_pairs={{1,0},{2,1},{3,2},{4,3},{5,4},{6,5},{7,6},{8,7},{9,8},{10,9},{11,1... | collective-permute-start | bytes 12296 | tf_op jit(solution)/shard_map/ppermute | solution.py:18
  161.0 23.0 %collective-permute-start.3 = (f32[2,8,64,1]{3,2,1,0:T(8,128)}, f32[2,8,64,1]{3,2,1,0:T(8,128)S(1)}, u32[]{:S(2)}, u32[]{:S(2)}) collective-permute-start(f32[2,8,64,1]{3,2,1,0:T(8,128)} %get-tuple-element.166), channel_id=1, source_target_pairs={{0,1},{1,2},{2,3},{3,4},{4,5},{5,6},{6,7},{7,8},{8,9},{9,10},{10,1... | collective-permute-start | bytes 12296 | tf_op jit(solution)/shard_map/ppermute | solution.py:15
  193.3 2.1 copy-start.4
  195.4 73.9 %copy-start.6 = (f32[64,512]{1,0:T(8,128)S(1)}, f32[64,512]{1,0:T(8,128)}, u32[]{:S(2)}) copy-start(f32[64,512]{1,0:T(8,128)} %param.18) | copy-start | bytes 393220
  195.4 73.9 %copy-start.7 = (s32[64,512]{1,0:T(8,128)S(1)}, s32[64,512]{1,0:T(8,128)}, u32[]{:S(2)}) copy-start(s32[64,512]{1,0:T(8,128)} %param.19) | copy-start | bytes 393220
  269.3 1.9 copy-start.5
where the time goes:
time: 274 us; the launch traced here: 271 us
  matrix products  94.4 us (34%)
  waiting for transfers between devices  87.3 us (32%)
  local copies, waits for them, and re-layouts  37.6 us (14%)
  other arithmetic  27.9 us (10%)
  starting transfers between devices  22 us (8%)
    ppermute x2, waiting for transfers between devices, with_halo(): lax.ppermute(lax.slice_in_dim(block, 0, width, axis=dim), axis, backward)  63.5 us
    dot_general x12, matrix products, land_list(): lax.dot_general(spread, col_table, (((1,), (1,)), ((), ())), precision=la...  56.9 us
    dot_general x12, matrix products, pick_list(): jnp.dot(surface_rows, col_table, precision=lax.Precision.HIGHEST, preferr...  37.5 us
    ppermute x2, waiting for transfers between devices, with_halo(): lax.ppermute(lax.slice_in_dim(block, block.shape[dim] - width, None, axis...  23.8 us
    dynamic_slice x36, local copies, waits for them, and re-layouts, shards(): unused, picked_all = lax.scan(pick_list, 0, (row_lists, col_lists, counts))  19.5 us
    all_to_all x1, starting transfers between devices, shards(): lax.all_to_all(blocks, ('comp', 'tile'), split_axis=1, concat_axis=1, til...  11.2 us
    ppermute x2, starting transfers between devices, with_halo(): lax.ppermute(lax.slice_in_dim(block, 0, width, axis=dim), axis, backward)  10.8 us
    lt x12, other arithmetic, pick_list(): values = jnp.where((slot_iota < count_one)[None, :], values, 0.0)  7.81 us
  transfers between devices with their start and end apart: 5, of which 4 were waited for; matrix products, arithmetic and copies ran while one was open for 4% of the time, Pallas kernels for 0%

commit v1 on v0

v1 whole, which is shorter than its diff:
```python
import functools
import jax
import jax.numpy as jnp
from jax import lax
from jax.experimental import pallas as pl
from jax.experimental.pallas import tpu as pltpu
from jax.sharding import PartitionSpec as P

SUBSTEPS = 2
LANES = 128
PARTS = 4
VMEM_LIMIT = 56 * 1024 * 1024


def split_halves(values):
    high = values.astype(jnp.bfloat16)
    low = (values - high.astype(jnp.float32)).astype(jnp.bfloat16)
    return high, low


def one_hot(index_row, size):
    n = index_row.shape[1]
    inside = (index_row >= 0) & (index_row < size)
    number = jnp.where(inside, index_row, -1).astype(jnp.float32)
    number = jnp.broadcast_to(number, (16, n)).astype(jnp.bfloat16)
    blocks = []
    iota = lax.broadcasted_iota(jnp.int32, (16, n), 0).astype(jnp.float32)
    for block in range(size // 16):
        here = (iota + float(16 * block)).astype(jnp.bfloat16)
        blocks.append(jnp.where(number == here, jnp.bfloat16(1), jnp.bfloat16(0)))
    return jnp.concatenate(blocks, axis=0)


def pick(surface, columns, rows):
    width = surface.shape[1]
    total = None
    for start in range(0, width, 256):
        size = min(256, width - start)
        part = jnp.dot(
            surface[:, start : start + size],
            one_hot(columns - start, size),
            preferred_element_type=jnp.float32,
        )
        total = part if total is None else total + part
    half = total.shape[0] // 2
    total = total[:half] + total[half:]
    row_count = half // 2
    n = rows.shape[1]
    match = lax.broadcasted_iota(jnp.int32, (row_count, n), 0) == rows
    first = jnp.sum(jnp.where(match, total[:row_count], 0.0), axis=0, keepdims=True)
    second = jnp.sum(jnp.where(match, total[row_count:], 0.0), axis=0, keepdims=True)
    return first, second


def each_list(comp, ocean_comp, body):
    ocean = comp == ocean_comp
    for j in range(ocean_comp):

        @pl.when(ocean | (comp == j))
        def _():
            body(j, jnp.where(ocean, j, ocean_comp))


def edge_kernel(ocean_comp, comp_ref, row_ref, col_ref, west_ref, east_ref, to_west, to_east):
    comp = comp_ref[0]
    levels = west_ref.shape[1]
    row_count = west_ref.shape[2]
    slots = row_ref.shape[-1]
    part = slots // PARTS
    lane = lax.broadcasted_iota(jnp.int32, (row_count, LANES), 1)
    for ref, out, shift in ((west_ref, to_west, 0), (east_ref, to_east, 2)):
        tile = jnp.zeros((row_count, LANES), jnp.float32)
        for k in range(2 * levels):
            moved = pltpu.roll(ref[k // levels, k % levels], (2 * k + shift) % LANES, 1)
            tile = jnp.where(lane // 2 == k, moved, tile)
        for block in range(row_count // 8):
            start = ocean_comp * part + LANES * block
            out[:, start : start + LANES] = tile[8 * block : 8 * block + 8]
    for ref, out, o, base in (
        (west_ref, to_west, 0, 0),
        (east_ref, to_east, 2, None),
    ):
        high, low = split_halves(ref[:, 0].reshape(2 * row_count, LANES))
        surface = jnp.concatenate([high, low], axis=0)
        offset = 0 if base == 0 else EAST_OFFSET

        def one_list(j, h):
            def step(q, carry):
                span = pl.ds(pl.multiple_of(q * part, LANES), part)
                columns = col_ref[0, 0, o, pl.ds(h, 1), span] - offset
                rows = row_ref[0, 0, o, pl.ds(h, 1), span]
                first, second = pick(surface, columns, rows)
                out[pl.ds(q, 1), j * part : (j + 1) * part] = first
                out[pl.ds(q + PARTS, 1), j * part : (j + 1) * part] = second
                return carry

            lax.fori_loop(0, PARTS, step, 0)

        each_list(comp, ocean_comp, one_list)


EAST_OFFSET = 384


def centre_kernel(ocean_comp, comp_ref, row_ref, col_ref, state_ref, from_west, from_east, *outs):
    comp = comp_ref[0]
    row_count, col_count = state_ref.shape[2:]
    slots = row_ref.shape[-1]
    part = slots // PARTS
    high, low = split_halves(state_ref[:, 0].reshape(2 * row_count, col_count))
    surface = jnp.concatenate([high, low], axis=0)

    def one_list(j, h):
        out = outs[j]
        out[0] = from_west[:, j * part : (j + 1) * part]
        out[2] = from_east[:, j * part : (j + 1) * part]

        def step(q, carry):
            span = pl.ds(pl.multiple_of(q * part, LANES), part)
            columns = col_ref[0, 0, 1, pl.ds(h, 1), span]
            rows = row_ref[0, 0, 1, pl.ds(h, 1), span]
            first, second = pick(surface, columns, rows)
            out[1, pl.ds(q, 1)] = first
            out[1, pl.ds(q + PARTS, 1)] = second
            return carry

        lax.fori_loop(0, PARTS, step, 0)

    each_list(comp, ocean_comp, one_list)


def transport_kernel(halo_start, state_ref, courant_ref, mixing_ref, west_ref, east_ref, unused_ref, out_ref):
    fields, levels, rows, cols = state_ref.shape
    step = pl.program_id(0)
    full = cols + LANES
    lane = lax.broadcasted_iota(jnp.int32, (8, LANES), 1)
    for block in range(rows // 8):
        span = slice(8 * block, 8 * block + 8)
        start = pl.multiple_of(halo_start + (step * (rows // 8) + block) * LANES, LANES)
        west = west_ref[:, pl.ds(start, LANES)]
        east = east_ref[:, pl.ds(start, LANES)]
        for f in range(fields):
            field = []
            for level in range(levels):
                k = f * levels + level
                left = pltpu.roll(west, (LANES - 2 - 2 * k) % LANES, 1)
                right = pltpu.roll(east, (LANES - 2 * k) % LANES, 1)
                edge = jnp.where(lane < 64, right, left)
                field.append(jnp.concatenate([state_ref[f, level, span], edge], axis=1))
            for substep in range(SUBSTEPS):
                moved = []
                for level in range(levels):
                    q = field[level]
                    c = courant_ref[span, level : level + 1]
                    left = pltpu.roll(q, 1, 1)
                    right = pltpu.roll(q, full - 1, 1)
                    half = 0.5 * c
                    square = half * c
                    moved.append(q * (1.0 - 2.0 * square) + right * (square - half) + left * (square + half))
                flux = [
                    mixing_ref[span, level : level + 1] * (moved[level + 1] - moved[level])
                    for level in range(levels - 1)
                ]
                field = []
                for level in range(levels):
                    q = moved[level]
                    if level < levels - 1:
                        q = q + flux[level]
                    if level > 0:
                        q = q - flux[level - 1]
                    field.append(q)
            for level in range(levels):
                out_ref[f, level, span] = field[level][:, :cols]


def land_kernel(
    ocean_comp,
    comp_ref,
    count_ref,
    row_ref,
    col_ref,
    weight_ref,
    got_0,
    got_1,
    got_2,
    field_ref,
    coef_ref,
    mask_ref,
    state_out,
    partner_out,
    total_ref,
):
    comp = comp_ref[0]
    row_count, col_count = coef_ref.shape
    slots = row_ref.shape[-1]
    part = slots // PARTS
    got = (got_0, got_1, got_2)
    total_ref[...] = jnp.zeros_like(total_ref)
    slot_iota = lax.broadcasted_iota(jnp.int32, (1, part), 1)

    def one_list(j, h):
        for o, base, width in ((0, 0, LANES), (1, 0, col_count), (2, EAST_OFFSET, LANES)):
            count = count_ref[0, 0, o, h]

            def step(q, carry):
                span = pl.ds(pl.multiple_of(q * part, LANES), part)
                columns = col_ref[0, 0, o, pl.ds(h, 1), span]
                rows = row_ref[0, 0, o, pl.ds(h, 1), span]
                weights = weight_ref[0, 0, o, pl.ds(h, 1), span]
                live = slot_iota + q * part < count
                row_table = one_hot(rows, row_count) > 0
                pieces = []
                for f in range(2):
                    value = got[j][o, pl.ds(q + f * PARTS, 1)]
                    pieces.append(split_halves(jnp.where(live, weights * value, 0.0)))
                left = jnp.concatenate(
                    [
                        jnp.where(row_table, jnp.broadcast_to(pieces[f][s], row_table.shape), jnp.bfloat16(0))
                        for s in range(2)
                        for f in range(2)
                    ],
                    axis=0,
                )
                for start in range(0, width, 256):
                    size = min(256, width - start)
                    table = one_hot(columns - (base + start), size)
                    total_ref[:, base + start : base + start + size] += lax.dot_general(
                        left, table, (((1,), (1,)), ((), ())), preferred_element_type=jnp.float32
                    )
                return carry

            lax.fori_loop(0, PARTS, step, 0)

    each_list(comp, ocean_comp, one_list)
    first_far = total_ref[:row_count] + total_ref[2 * row_count : 3 * row_count]
    second_far = total_ref[row_count : 2 * row_count] + total_ref[3 * row_count :]
    partner_out[0] = first_far
    partner_out[1] = second_far
    ocean = comp == ocean_comp
    rate = coef_ref[...] * mask_ref[...].astype(jnp.float32)
    first_own = field_ref[0, 0]
    second_own = field_ref[1, 0]
    state_out[0, 0] = first_own + rate * (first_far - first_own)
    air_second = second_own + rate * (1.2 * first_far - 0.3 * second_far - second_own)
    sea_second = second_own + rate * (1.2 * first_own - second_far)
    state_out[1, 0] = jnp.where(ocean, sea_second, air_second)


def whole(array):
    return pl.BlockSpec(array.shape, functools.partial(lambda n, *i: (0,) * n, len(array.shape)))


def shards(
    state,
    courant,
    mixing,
    exchange_coef,
    sea_mask,
    margin_count,
    margin_row,
    margin_col,
    margin_weight,
):
    fields, levels, row_count, col_count = state.shape
    slots = margin_row.shape[-1]
    ocean_comp = margin_row.shape[3] - 1
    part = slots // PARTS
    tiles = lax.axis_size("tile")
    comp = lax.axis_index("comp").astype(jnp.int32).reshape(1)
    scalar = pl.BlockSpec(memory_space=pltpu.SMEM)
    params = pltpu.CompilerParams(vmem_limit_bytes=VMEM_LIMIT)
    strip = (fields, levels, row_count, LANES)
    packet = jax.ShapeDtypeStruct((2 * PARTS, ocean_comp * part + LANES * row_count // 8), jnp.float32)
    last = col_count // LANES - 1

    to_west, to_east = pl.pallas_call(
        functools.partial(edge_kernel, ocean_comp),
        grid=(1,),
        in_specs=[
            scalar,
            whole(margin_row),
            whole(margin_col),
            pl.BlockSpec(strip, lambda i: (0, 0, 0, 0)),
            pl.BlockSpec(strip, lambda i: (0, 0, 0, last)),
        ],
        out_specs=[whole(packet)] * 2,
        out_shape=[packet] * 2,
        compiler_params=params,
        name="edge_gather",
    )(comp, margin_row, margin_col, state, state)
    forward = [(i, (i + 1) % tiles) for i in range(tiles)]
    backward = [(b, a) for a, b in forward]
    from_west = lax.ppermute(to_east, "tile", forward)
    from_east = lax.ppermute(to_west, "tile", backward)

    bundle = jax.ShapeDtypeStruct((3, 2 * PARTS, part), jnp.float32)
    bundles = pl.pallas_call(
        functools.partial(centre_kernel, ocean_comp),
        grid=(1,),
        in_specs=[
            scalar,
            whole(margin_row),
            whole(margin_col),
            pl.BlockSpec((fields, 1, row_count, col_count), lambda i: (0, 0, 0, 0)),
            whole(packet),
            whole(packet),
        ],
        out_specs=[whole(bundle)] * ocean_comp,
        out_shape=[bundle] * ocean_comp,
        compiler_params=params,
        name="centre_gather",
    )(comp, margin_row, margin_col, state, from_west, from_east)
    got = []
    for g in range(ocean_comp):
        swap = []
        for t in range(tiles):
            swap.append((g * tiles + t, ocean_comp * tiles + t))
            swap.append((ocean_comp * tiles + t, g * tiles + t))
        got.append(lax.ppermute(bundles[g], ("comp", "tile"), swap))

    chunk = 16
    moved = pl.pallas_call(
        functools.partial(transport_kernel, ocean_comp * part),
        grid=(row_count // chunk,),
        in_specs=[
            pl.BlockSpec((fields, levels, chunk, col_count), lambda i: (0, 0, i, 0)),
            pl.BlockSpec((chunk, levels), lambda i: (i, 0)),
            pl.BlockSpec((chunk, levels - 1), lambda i: (i, 0)),
            whole(packet),
            whole(packet),
            pl.BlockSpec(memory_space=pl.ANY),
        ],
        out_specs=pl.BlockSpec((fields, levels, chunk, col_count), lambda i: (0, 0, i, 0)),
        out_shape=jax.ShapeDtypeStruct(state.shape, jnp.float32),
        compiler_params=params,
        name="transport",
    )(state, courant.T, mixing.T, from_west, from_east, bundles[0])

    surface_spec = pl.BlockSpec((fields, 1, row_count, col_count), lambda i: (0, 0, 0, 0))
    partner = jax.ShapeDtypeStruct((fields, row_count, col_count), jnp.float32)
    return pl.pallas_call(
        functools.partial(land_kernel, ocean_comp),
        grid=(1,),
        in_specs=[
            scalar,
            scalar,
            whole(margin_row),
            whole(margin_col),
            whole(margin_weight),
            whole(bundle),
            whole(bundle),
            whole(bundle),
            surface_spec,
            whole(exchange_coef),
            whole(sea_mask),
        ],
        out_specs=[surface_spec, whole(partner)],
        out_shape=[jax.ShapeDtypeStruct(state.shape, jnp.float32), partner],
        scratch_shapes=[pltpu.VMEM((4 * row_count, col_count), jnp.float32)],
        input_output_aliases={8: 0},
        compiler_params=params,
        name="land",
    )(
        comp,
        margin_count,
        margin_row,
        margin_col,
        margin_weight,
        *got,
        moved,
        exchange_coef,
        sea_mask,
    )


def solution(mesh):
    in_specs = (
        P(None, None, "comp", "tile"),
        P(None, "comp"),
        P(None, "comp"),
        P("comp", "tile"),
        P("comp", "tile"),
        P("comp", "tile", None, None),
        P("comp", "tile", None, None, None),
        P("comp", "tile", None, None, None),
        P("comp", "tile", None, None, None),
    )
    out_specs = (P(None, None, "comp", "tile"), P(None, "comp", "tile"))
    return jax.shard_map(shards, mesh=mesh, in_specs=in_specs, out_specs=out_specs, check_vma=False)
```

time: 274 us -> 62.5 us (0.23)
  matrix products: 94.4 us -> 0 us
  waiting for transfers between devices: 87.3 us -> 2.56 us
  Pallas kernels: 0 us -> 40.8 us
  local copies, waits for them, and re-layouts: 37.6 us -> 4.56 us
  other arithmetic: 27.9 us -> 0 us
  starting transfers between devices: 22 us -> 13.6 us
    dot_general x24 -> x0, matrix products: 94.4 us -> none  [the longest x12 56.9 us: land_list(): lax.dot_general(spread, col_table, (((1,), (1,)), ((), ())), precision=la...]
    ppermute x4 -> x5, waiting for transfers between devices: 87.2 us -> 2.56 us  [the longest x1 2.55 us: shards(): from_west = lax.ppermute(to_east, 'tile', forward)]
    pallas_call x0 -> x4, Pallas kernels: none -> 40.8 us  [the longest x1 15.9 us: shards(): pl.pallas_call(functools.partial(land_kernel, ocean_comp), grid=(1,), in_...]
    dynamic_slice x36 -> x0, local copies, waits for them, and re-layouts: 19.5 us -> none  [shards(): unused, picked_all = lax.scan(pick_list, 0, (row_lists, col_lists, counts))]
    all_to_all x1 -> x0, starting transfers between devices: 11.2 us -> none  [shards(): lax.all_to_all(blocks, ('comp', 'tile'), split_axis=1, concat_axis=1, til...]
    lt x12 -> x0, other arithmetic: 7.81 us -> none  [pick_list(): values = jnp.where((slot_iota < count_one)[None, :], values, 0.0)]
    reshape x4 -> x0, local copies, waits for them, and re-layouts: 7.28 us -> none  [the longest x1 5.2 us: shards(): jnp.sum(spread, axis=1)]
    sub x2 -> x0, other arithmetic: 4.87 us -> none  [vertical_mix(): return field + upper - lower]
  transfers between devices with their start and end apart: 5 -> 5, of which waited for: 4 -> 1; matrix products, arithmetic and copies ran while one was open for 4% -> 3% of each run, Pallas kernels for 0% -> 12%
where the time goes in v1:
time: 62.5 us; the launch traced here: 62.2 us
  Pallas kernels  40.8 us (65%)
  starting transfers between devices  13.6 us (22%)
  local copies, waits for them, and re-layouts  4.56 us (7%)
  waiting for transfers between devices  2.56 us (4%)
  between operations  0.71 us (1%)
    pallas_call x1, Pallas kernels, shards(): pl.pallas_call(functools.partial(land_kernel, ocean_comp), grid=(1,), in_...  15.9 us
    pallas_call x1, Pallas kernels, shards(): pl.pallas_call(functools.partial(edge_kernel, ocean_comp), grid=(1,), in_...  9.72 us
    pallas_call x1, Pallas kernels, shards(): pl.pallas_call(functools.partial(transport_kernel, ocean_comp * part), gr...  7.66 us
    pallas_call x1, Pallas kernels, shards(): pl.pallas_call(functools.partial(centre_kernel, ocean_comp), grid=(1,), i...  7.53 us
    ppermute x1, starting transfers between devices, shards(): from_east = lax.ppermute(to_west, 'tile', backward)  5.75 us
    ppermute x3, starting transfers between devices, shards(): got.append(lax.ppermute(bundles[g], ('comp', 'tile'), swap))  5.75 us
    unnamed x19, local copies, waits for them, and re-layouts  4.56 us
    ppermute x1, waiting for transfers between devices, shards(): from_west = lax.ppermute(to_east, 'tile', forward)  2.55 us
  transfers between devices with their start and end apart: 5, of which 1 were waited for; matrix products, arithmetic and copies ran while one was open for 3% of the time, Pallas kernels for 12%

profile of v1, /device:TPU:9, one launch (start us, length us, event | category | flops | bytes accessed | tf_op | source)
XLA Modules:
  0.0 62.2 jit_solution(15827500372229543947)
XLA Ops:
  0.6 9.7 %edge_gather.1 = (f32[8,4096]{1,0:T(8,128)}, f32[8,4096]{1,0:T(8,128)}) custom-call(s32[1]{0:T(128)} %bitcast.comp_ref, s32[1,1,3,4,4096]{4,3,2,1,0:T(4,128)} %row_ref.5, s32[1,1,3,4,4096]{4,3,2,1,0:T(4,128)} %col_ref.5, f32[2,8,64,512]{3,2,1,0:T(8,128)} %state_ref.3, f32[2,8,64,512]{3,2,1,0:T(8,128)} %state_ref.3), custom_call_target="tpu_custom_call" | custom-call | tf_op jit(solution)/shard_map/edge_gather/pallas_call | solution.py:276
  10.4 0.0 copy-start.7
  10.4 0.0 copy-start.5
  10.4 0.0 copy-start.6
  10.4 2.1 %collective-permute-start = (f32[8,4096]{1,0:T(8,128)}, f32[8,4096]{1,0:T(8,128)S(1)}, u32[]{:S(2)}, u32[]{:S(2)}) collective-permute-start(f32[8,4096]{1,0:T(8,128)} %get-tuple-element.7), channel_id=1, source_target_pairs={{0,1},{1,2},{2,3},{3,4},{4,5},{5,6},{6,7},{7,8},{8,9},{9,10},{10,1... | collective-permute-start | bytes 393224 | tf_op jit(solution)/shard_map/ppermute | solution.py:293
  12.5 5.7 %collective-permute-start.1 = (f32[8,4096]{1,0:T(8,128)}, f32[8,4096]{1,0:T(8,128)S(1)}, u32[]{:S(2)}, u32[]{:S(2)}) collective-permute-start(f32[8,4096]{1,0:T(8,128)} %get-tuple-element.8), channel_id=1, source_target_pairs={{1,0},{2,1},{3,2},{4,3},{5,4},{6,5},{7,6},{8,7},{9,8},{10,9},{11,1... | collective-permute-start | bytes 393224 | tf_op jit(solution)/shard_map/ppermute | solution.py:294
  18.2 2.6 %collective-permute-done.from_west.west_ref = f32[8,4096]{1,0:T(8,128)S(1)} collective-permute-done((f32[8,4096]{1,0:T(8,128)}, f32[8,4096]{1,0:T(8,128)S(1)}, u32[]{:S(2)}, u32[]{:S(2)}) %collective-permute-start) | collective-permute-done | bytes 131104 | tf_op jit(solution)/shard_map/ppermute | solution.py:293
  20.8 0.0 copy-start
  20.8 0.0 collective-permute-done.1.from_east.east_ref
  20.8 0.6 %copy-done = f32[8,4096]{1,0:T(8,128)} copy-done((f32[8,4096]{1,0:T(8,128)}, f32[8,4096]{1,0:T(8,128)S(1)}, u32[]{:S(2)}) %copy-start) | copy-done | bytes 131096
  21.4 0.0 copy-start.1
  21.4 0.7 %copy-done.1 = f32[8,4096]{1,0:T(8,128)} copy-done((f32[8,4096]{1,0:T(8,128)}, f32[8,4096]{1,0:T(8,128)S(1)}, u32[]{:S(2)}) %copy-start.1) | copy-done | bytes 131096
  22.1 7.5 %centre_gather.1 = (f32[3,8,1024]{2,1,0:T(8,128)}, f32[3,8,1024]{2,1,0:T(8,128)}, f32[3,8,1024]{2,1,0:T(8,128)}) custom-call(s32[1]{0:T(128)} %bitcast.comp_ref, s32[1,1,3,4,4096]{4,3,2,1,0:T(4,128)} %row_ref.5, s32[1,1,3,4,4096]{4,3,2,1,0:T(4,128)} %col_ref.5, f32[2,8,64,512]{3,2,1,0:T(8,128)} %state_ref.3, f32[8,4096]{1,0:T(8,128)} %copy-done, ...), custom_call_target="tpu_custom_call" | custom-call | tf_op jit(solution)/shard_map/centre_gather/pallas_call | solution.py:297
  29.6 1.9 %collective-permute-start.3 = (f32[3,8,1024]{2,1,0:T(8,128)}, f32[3,8,1024]{2,1,0:T(8,128)S(1)}, u32[]{:S(2)}, u32[]{:S(2)}) collective-permute-start(f32[3,8,1024]{2,1,0:T(8,128)} %get-tuple-element.10), channel_id=1, source_target_pairs={{32,96},{96,32},{33,97},{97,33},{34,98},{98,34},{35,99},{99,35},{3... | collective-permute-start | bytes 294920 | tf_op jit(solution)/shard_map/ppermute | solution.py:319
  31.5 1.9 %collective-permute-start.4 = (f32[3,8,1024]{2,1,0:T(8,128)}, f32[3,8,1024]{2,1,0:T(8,128)S(1)}, u32[]{:S(2)}, u32[]{:S(2)}) collective-permute-start(f32[3,8,1024]{2,1,0:T(8,128)} %get-tuple-element.11), channel_id=1, source_target_pairs={{64,96},{96,64},{65,97},{97,65},{66,98},{98,66},{67,99},{99,67},{6... | collective-permute-start | bytes 294920 | tf_op jit(solution)/shard_map/ppermute | solution.py:319
  33.4 1.9 %collective-permute-start.2 = (f32[3,8,1024]{2,1,0:T(8,128)}, f32[3,8,1024]{2,1,0:T(8,128)S(1)}, u32[]{:S(2)}, u32[]{:S(2)}) collective-permute-start(f32[3,8,1024]{2,1,0:T(8,128)} %get-tuple-element.9.unused_ref), channel_id=1, source_target_pairs={{0,96},{96,0},{1,97},{97,1},{2,98},{98,2},{3,99},{99,3},{4,100},{1... | collective-permute-start | bytes 294920 | tf_op jit(solution)/shard_map/ppermute | solution.py:319
  35.4 0.0 copy-done.7
  35.4 0.6 copy.14.count_ref
  36.0 0.0 copy-done.5
  36.0 0.7 %copy.12 = f32[8,64]{0,1:T(8,128)} copy(f32[8,64]{1,0:T(8,128)S(1)} %copy-done.5) | data formatting | bytes 4096 | tf_op args[1]
  36.6 0.0 copy-done.6
  36.6 0.7 %copy.13 = f32[7,64]{0,1:T(8,128)} copy(f32[7,64]{1,0:T(8,128)S(1)} %copy-done.6) | data formatting | bytes 3584 | tf_op args[2]
  37.3 7.7 %transport.1.field_ref = f32[2,8,64,512]{3,2,1,0:T(8,128)} custom-call(f32[2,8,64,512]{3,2,1,0:T(8,128)} %state_ref.3, f32[64,8]{1,0:T(8,128)} %bitcast.3, f32[64,7]{1,0:T(8,128)} %bitcast.4, f32[8,4096]{1,0:T(8,128)} %copy-done, f32[8,4096]{1,0:T(8,128)} %copy-done.1, f32[3,8,1024]{2,1,0:T(8,128)} %get-tuple-element.9.unused_ref), custom_call_target="tpu_custom_call" | custom-call | tf_op jit(solution)/shard_map/transport/pallas_call | solution.py:322
  45.0 0.0 collective-permute-done.3.got_1
  45.0 0.0 copy-start.2
  45.0 0.0 collective-permute-done.4.got_2
  45.0 0.0 copy-start.3
  45.0 0.0 collective-permute-done.2.got_0
  45.0 0.6 copy-done.2
  45.6 0.0 copy-done.3
  45.7 0.6 %copy-done.4 = f32[3,8,1024]{2,1,0:T(8,128)} copy-done((f32[3,8,1024]{2,1,0:T(8,128)}, f32[3,8,1024]{2,1,0:T(8,128)S(1)}, u32[]{:S(2)}) %copy-start.4) | copy-done | bytes 98328
  46.3 15.9 %land.1 = (f32[2,8,64,512]{3,2,1,0:T(8,128)}, f32[2,64,512]{2,1,0:T(8,128)}) custom-call(s32[1]{0:T(128)} %bitcast.comp_ref, s32[1,1,3,4]{3,2,1,0:T(4,128)} %copy.14.count_ref, s32[1,1,3,4,4096]{4,3,2,1,0:T(4,128)} %row_ref.5, s32[1,1,3,4,4096]{4,3,2,1,0:T(4,128)} %col_ref.5, f32[1,1,3,4,4096]{4,3,2,1,0:T(4,128)} %weight_ref.1, ...), custom_call_target="tpu_custom_call", output_to_operand_aliasing={{0}: (8, {})} | custom-call | tf_op jit(solution)/shard_map/land/pallas_call | solution.py:341
  (1 shorter events, 0.0 us)
Async XLA Ops:
  10.4 25.0 %copy-start.7 = (s32[1,1,3,4]{3,1,2,0:T(1,128)S(1)}, s32[1,1,3,4]{3,1,2,0:T(1,128)}, u32[]{:S(2)}) copy-start(s32[1,1,3,4]{3,1,2,0:T(1,128)} %param.14) | copy-start | bytes 148
  10.4 25.6 %copy-start.5 = (f32[8,64]{1,0:T(8,128)S(1)}, f32[8,64]{1,0:T(8,128)}, u32[]{:S(2)}) copy-start(f32[8,64]{1,0:T(8,128)} %param.10) | copy-start | bytes 6148
  10.4 26.3 %copy-start.6 = (f32[7,64]{1,0:T(8,128)S(1)}, f32[7,64]{1,0:T(8,128)}, u32[]{:S(2)}) copy-start(f32[7,64]{1,0:T(8,128)} %param.11) | copy-start | bytes 5380
  10.4 10.4 %collective-permute-start = (f32[8,4096]{1,0:T(8,128)}, f32[8,4096]{1,0:T(8,128)S(1)}, u32[]{:S(2)}, u32[]{:S(2)}) collective-permute-start(f32[8,4096]{1,0:T(8,128)} %get-tuple-element.7), channel_id=1, source_target_pairs={{0,1},{1,2},{2,3},{3,4},{4,5},{5,6},{6,7},{7,8},{8,9},{9,10},{10,1... | collective-permute-start | bytes 393224 | tf_op jit(solution)/shard_map/ppermute | solution.py:293
  12.5 8.3 %collective-permute-start.1 = (f32[8,4096]{1,0:T(8,128)}, f32[8,4096]{1,0:T(8,128)S(1)}, u32[]{:S(2)}, u32[]{:S(2)}) collective-permute-start(f32[8,4096]{1,0:T(8,128)} %get-tuple-element.8), channel_id=1, source_target_pairs={{1,0},{2,1},{3,2},{4,3},{5,4},{6,5},{7,6},{8,7},{9,8},{10,9},{11,1... | collective-permute-start | bytes 393224 | tf_op jit(solution)/shard_map/ppermute | solution.py:294
  20.8 0.7 %copy-start = (f32[8,4096]{1,0:T(8,128)}, f32[8,4096]{1,0:T(8,128)S(1)}, u32[]{:S(2)}) copy-start(f32[8,4096]{1,0:T(8,128)S(1)} %collective-permute-done.from_west.west_ref) | copy-start | bytes 393220
  21.4 0.7 %copy-start.1 = (f32[8,4096]{1,0:T(8,128)}, f32[8,4096]{1,0:T(8,128)S(1)}, u32[]{:S(2)}) copy-start(f32[8,4096]{1,0:T(8,128)S(1)} %collective-permute-done.1.from_east.east_ref) | copy-start | bytes 393220
  29.6 15.4 %collective-permute-start.3 = (f32[3,8,1024]{2,1,0:T(8,128)}, f32[3,8,1024]{2,1,0:T(8,128)S(1)}, u32[]{:S(2)}, u32[]{:S(2)}) collective-permute-start(f32[3,8,1024]{2,1,0:T(8,128)} %get-tuple-element.10), channel_id=1, source_target_pairs={{32,96},{96,32},{33,97},{97,33},{34,98},{98,34},{35,99},{99,35},{3... | collective-permute-start | bytes 294920 | tf_op jit(solution)/shard_map/ppermute | solution.py:319
  31.5 13.5 %collective-permute-start.4 = (f32[3,8,1024]{2,1,0:T(8,128)}, f32[3,8,1024]{2,1,0:T(8,128)S(1)}, u32[]{:S(2)}, u32[]{:S(2)}) collective-permute-start(f32[3,8,1024]{2,1,0:T(8,128)} %get-tuple-element.11), channel_id=1, source_target_pairs={{64,96},{96,64},{65,97},{97,65},{66,98},{98,66},{67,99},{99,67},{6... | collective-permute-start | bytes 294920 | tf_op jit(solution)/shard_map/ppermute | solution.py:319
  33.4 11.6 %collective-permute-start.2 = (f32[3,8,1024]{2,1,0:T(8,128)}, f32[3,8,1024]{2,1,0:T(8,128)S(1)}, u32[]{:S(2)}, u32[]{:S(2)}) collective-permute-start(f32[3,8,1024]{2,1,0:T(8,128)} %get-tuple-element.9.unused_ref), channel_id=1, source_target_pairs={{0,96},{96,0},{1,97},{97,1},{2,98},{98,2},{3,99},{99,3},{4,100},{1... | collective-permute-start | bytes 294920 | tf_op jit(solution)/shard_map/ppermute | solution.py:319
  45.0 0.6 %copy-start.2 = (f32[3,8,1024]{2,1,0:T(8,128)}, f32[3,8,1024]{2,1,0:T(8,128)S(1)}, u32[]{:S(2)}) copy-start(f32[3,8,1024]{2,1,0:T(8,128)S(1)} %collective-permute-done.3.got_1) | copy-start | bytes 294916
  45.0 0.7 %copy-start.3 = (f32[3,8,1024]{2,1,0:T(8,128)}, f32[3,8,1024]{2,1,0:T(8,128)S(1)}, u32[]{:S(2)}) copy-start(f32[3,8,1024]{2,1,0:T(8,128)S(1)} %collective-permute-done.4.got_2) | copy-start | bytes 294916
  45.7 0.6 %copy-start.4 = (f32[3,8,1024]{2,1,0:T(8,128)}, f32[3,8,1024]{2,1,0:T(8,128)S(1)}, u32[]{:S(2)}) copy-start(f32[3,8,1024]{2,1,0:T(8,128)S(1)} %collective-permute-done.2.got_0) | copy-start | bytes 294916

commit v2 on v1

v2 whole, which is shorter than its diff:
```python
import functools
import jax
import jax.numpy as jnp
from jax import lax
from jax.experimental import pallas as pl
from jax.experimental.pallas import tpu as pltpu
from jax.sharding import PartitionSpec as P

SUBSTEPS = 2
LANES = 128
PARTS = 4
VMEM_LIMIT = 56 * 1024 * 1024


def split_halves(values):
    high = values.astype(jnp.bfloat16)
    low = (values - high.astype(jnp.float32)).astype(jnp.bfloat16)
    return high, low


def one_hot(index_row, size):
    n = index_row.shape[1]
    inside = (index_row >= 0) & (index_row < size)
    number = jnp.where(inside, index_row, -1).astype(jnp.float32)
    number = jnp.broadcast_to(number, (16, n)).astype(jnp.bfloat16)
    blocks = []
    iota = lax.broadcasted_iota(jnp.int32, (16, n), 0).astype(jnp.float32)
    for block in range(size // 16):
        here = (iota + float(16 * block)).astype(jnp.bfloat16)
        blocks.append(jnp.where(number == here, jnp.bfloat16(1), jnp.bfloat16(0)))
    return jnp.concatenate(blocks, axis=0)


def match_rows(total, rows):
    row_count = total.shape[0] // 2
    match = lax.broadcasted_iota(jnp.int32, (row_count, rows.shape[1]), 0) == rows
    first = jnp.sum(jnp.where(match, total[:row_count], 0.0), axis=0, keepdims=True)
    second = jnp.sum(jnp.where(match, total[row_count:], 0.0), axis=0, keepdims=True)
    return first, second


def wide_one_hot(columns, width):
    return jnp.concatenate(
        [one_hot(columns - start, min(256, width - start)) for start in range(0, width, 256)], axis=0
    )


def edge_kernel(ocean_comp, comp_ref, row_ref, col_ref, west_ref, east_ref, to_west, to_east):
    ocean = comp_ref[0] == ocean_comp
    levels = west_ref.shape[1]
    row_count = west_ref.shape[2]
    part = row_ref.shape[-1] // PARTS
    lane = lax.broadcasted_iota(jnp.int32, (row_count, LANES), 1)
    sides = ((west_ref, to_west, 0, 0), (east_ref, to_east, 2, EAST_OFFSET))
    for ref, out, shift, unused in sides:
        tile = jnp.zeros((row_count, LANES), jnp.float32)
        for k in range(2 * levels):
            moved = pltpu.roll(ref[k // levels, k % levels], (2 * k + shift) % LANES, 1)
            tile = jnp.where(lane // 2 == k, moved, tile)
        for block in range(row_count // 8):
            start = ocean_comp * part + LANES * block
            out[:, start : start + LANES] = tile[8 * block : 8 * block + 8]

    def lists(pairs):
        for ref, out, o, offset in sides:
            high, low = split_halves(ref[:, 0].reshape(2 * row_count, LANES))
            surface = jnp.concatenate([high, low], axis=1)
            for slot, h in pairs:
                for q in range(PARTS):
                    span = slice(q * part, (q + 1) * part)
                    table = one_hot(col_ref[0, 0, o, h : h + 1, span] - offset, LANES)
                    total = jnp.dot(
                        surface,
                        jnp.concatenate([table, table], axis=0),
                        preferred_element_type=jnp.float32,
                    )
                    first, second = match_rows(total, row_ref[0, 0, o, h : h + 1, span])
                    out[q : q + 1, slot * part : (slot + 1) * part] = first
                    out[q + PARTS : q + PARTS + 1, slot * part : (slot + 1) * part] = second

    @pl.when(ocean)
    def _():
        lists([(j, j) for j in range(ocean_comp)])

    @pl.when(jnp.logical_not(ocean))
    def _():
        lists([(0, ocean_comp)])


EAST_OFFSET = 384


def centre_kernel(ocean_comp, comp_ref, row_ref, col_ref, state_ref, out):
    ocean = comp_ref[0] == ocean_comp
    row_count, col_count = state_ref.shape[2:]
    part = row_ref.shape[-1] // PARTS

    def lists(pairs):
        high, low = split_halves(state_ref[:, 0].reshape(2 * row_count, col_count))
        surface = jnp.concatenate([high, low], axis=0)
        for slot, h in pairs:
            for q in range(PARTS):
                span = slice(q * part, (q + 1) * part)
                table = wide_one_hot(col_ref[0, 0, 1, h : h + 1, span], col_count)
                total = jnp.dot(surface, table, preferred_element_type=jnp.float32)
                half = 2 * row_count
                first, second = match_rows(total[:half] + total[half:], row_ref[0, 0, 1, h : h + 1, span])
                out[slot, q : q + 1] = first
                out[slot, q + PARTS : q + PARTS + 1] = second

    @pl.when(ocean)
    def _():
        lists([(j, j) for j in range(ocean_comp)])

    @pl.when(jnp.logical_not(ocean))
    def _():
        lists([(0, ocean_comp)])


def pack_kernel(ocean_comp, comp_ref, centre_ref, from_west, from_east, *outs):
    ocean = comp_ref[0] == ocean_comp
    part = centre_ref.shape[-1]

    def fill(slots):
        for slot, out in zip(slots, outs):
            span = slice(slot * part, (slot + 1) * part)
            out[0] = from_west[:, span]
            out[1] = centre_ref[slot]
            out[2] = from_east[:, span]

    @pl.when(ocean)
    def _():
        fill(range(ocean_comp))

    @pl.when(jnp.logical_not(ocean))
    def _():
        fill([0] * ocean_comp)


def transport_kernel(halo_start, state_ref, courant_ref, mixing_ref, west_ref, east_ref, unused_ref, out_ref):
    fields, levels, rows, cols = state_ref.shape
    step = pl.program_id(0)
    full = cols + LANES
    lane = lax.broadcasted_iota(jnp.int32, (8, LANES), 1)
    tiles = cols // LANES

    def advance(q, middle, ahead, behind):
        back = [pltpu.roll(t, 1, 1) for t in q]
        fore = [pltpu.roll(t, LANES - 1, 1) for t in q]
        done = []
        for i in range(len(q)):
            left = jnp.where(lane == 0, back[i - 1], back[i])
            right = jnp.where(lane == LANES - 1, fore[(i + 1) % len(q)], fore[i])
            done.append(q[i] * middle + right * ahead + left * behind)
        return done

    for block in range(rows // 8):
        span = slice(8 * block, 8 * block + 8)
        start = pl.multiple_of(halo_start + (step * (rows // 8) + block) * LANES, LANES)
        west = west_ref[:, pl.ds(start, LANES)]
        east = east_ref[:, pl.ds(start, LANES)]
        coeffs = []
        for level in range(levels):
            c = jnp.broadcast_to(courant_ref[span, level : level + 1], (8, LANES))
            half = 0.5 * c
            square = half * c
            coeffs.append((1.0 - 2.0 * square, square - half, square + half))
        mix = [jnp.broadcast_to(mixing_ref[span, level : level + 1], (8, LANES)) for level in range(levels - 1)]
        for f in range(fields):

            def source():
                for level in range(levels):
                    k = f * levels + level
                    left = pltpu.roll(west, (LANES - 2 - 2 * k) % LANES, 1)
                    right = pltpu.roll(east, (LANES - 2 * k) % LANES, 1)
                    edge = jnp.where(lane < 64, right, left)
                    yield [state_ref[f, level, span, LANES * i : LANES * i + LANES] for i in range(tiles)] + [edge]

            def substep(stream):
                before = None
                flux_below = None
                for level, q in enumerate(stream):
                    now = advance(q, *coeffs[level])
                    if before is not None:
                        flux = [mix[level - 1] * (n - b) for n, b in zip(now, before)]
                        mixed = [b + x for b, x in zip(before, flux)]
                        if flux_below is not None:
                            mixed = [m - x for m, x in zip(mixed, flux_below)]
                        yield mixed
                        flux_below = flux
                    before = now
                yield [b - x for b, x in zip(before, flux_below)]

            stream = source()
            for unused in range(SUBSTEPS):
                stream = substep(stream)
            for level, q in enumerate(stream):
                for i in range(tiles):
                    out_ref[f, level, span, LANES * i : LANES * i + LANES] = q[i]


def land_kernel(
    ocean_comp,
    comp_ref,
    count_ref,
    row_ref,
    col_ref,
    weight_ref,
    got_0,
    got_1,
    got_2,
    field_ref,
    coef_ref,
    mask_ref,
    state_out,
    partner_out,
    centre_ref,
    west_ref,
    east_ref,
):
    ocean = comp_ref[0] == ocean_comp
    row_count, col_count = coef_ref.shape
    part = row_ref.shape[-1] // PARTS
    half_rows = row_count // 2
    slot_iota = lax.broadcasted_iota(jnp.int32, (1, part), 1)
    nt = (((1,), (1,)), ((), ()))

    def land(lists):
        for o, total_ref in ((1, centre_ref), (0, west_ref), (2, east_ref)):
            total = None
            for h, got in lists:
                count = count_ref[o, h]
                for q in range(PARTS):
                    span = slice(q * part, (q + 1) * part)
                    columns = col_ref[0, 0, o, h : h + 1, span]
                    rows = row_ref[0, 0, o, h : h + 1, span]
                    weights = weight_ref[0, 0, o, h : h + 1, span]
                    live = slot_iota + q * part < count
                    if o == 1:
                        row_table = one_hot(rows, row_count)
                        table = wide_one_hot(columns, col_count)
                    else:
                        upper = rows >= half_rows
                        row_table = one_hot(jnp.where(upper, rows - half_rows, rows), half_rows)
                        offset = EAST_OFFSET if o == 2 else 0
                        columns = columns - offset
                        table = one_hot(jnp.where(upper, columns + LANES, columns), 2 * LANES)
                    on = row_table > 0
                    pieces = []
                    for f in range(2):
                        value = got[o, q + f * PARTS : q + f * PARTS + 1]
                        pieces.append(split_halves(jnp.where(live, weights * value, 0.0)))
                    left = jnp.concatenate(
                        [
                            jnp.where(on, jnp.broadcast_to(pieces[f][s], on.shape), jnp.bfloat16(0))
                            for s in range(2)
                            for f in range(2)
                        ],
                        axis=0,
                    )
                    product = lax.dot_general(left, table, nt, preferred_element_type=jnp.float32)
                    total = product if total is None else total + product
            size = total.shape[0] // 2
            total_ref[...] = total[:size] + total[size:]

    @pl.when(ocean)
    def _():
        land([(j, got) for j, got in enumerate((got_0, got_1, got_2))])

    @pl.when(jnp.logical_not(ocean))
    def _():
        land([(ocean_comp, got_0[...] + got_1[...] + got_2[...])])

    def far(f):
        centre = centre_ref[f * row_count : (f + 1) * row_count]
        sides = []
        for ref in (west_ref, east_ref):
            rows = ref[f * half_rows : (f + 1) * half_rows]
            sides.append(jnp.concatenate([rows[:, :LANES], rows[:, LANES:]], axis=0))
        return jnp.concatenate(
            [
                centre[:, :LANES] + sides[0],
                centre[:, LANES : col_count - LANES],
                centre[:, col_count - LANES :] + sides[1],
            ],
            axis=1,
        )

    first_far = far(0)
    second_far = far(1)
    partner_out[0] = first_far
    partner_out[1] = second_far
    rate = coef_ref[...] * mask_ref[...].astype(jnp.float32)
    first_own = field_ref[0, 0]
    second_own = field_ref[1, 0]
    state_out[0, 0] = first_own + rate * (first_far - first_own)
    air_second = second_own + rate * (1.2 * first_far - 0.3 * second_far - second_own)
    sea_second = second_own + rate * (1.2 * first_own - second_far)
    state_out[1, 0] = jnp.where(ocean, sea_second, air_second)


def whole(array):
    return pl.BlockSpec(array.shape, functools.partial(lambda n, *i: (0,) * n, len(array.shape)))


def shards(
    state,
    courant,
    mixing,
    exchange_coef,
    sea_mask,
    margin_count,
    margin_row,
    margin_col,
    margin_weight,
):
    fields, levels, row_count, col_count = state.shape
    slots = margin_row.shape[-1]
    ocean_comp = margin_row.shape[3] - 1
    part = slots // PARTS
    tiles = lax.axis_size("tile")
    comp = lax.axis_index("comp").astype(jnp.int32).reshape(1)
    scalar = pl.BlockSpec(memory_space=pltpu.SMEM)
    params = pltpu.CompilerParams(vmem_limit_bytes=VMEM_LIMIT)
    strip = (fields, levels, row_count, LANES)
    packet = jax.ShapeDtypeStruct((2 * PARTS, ocean_comp * part + LANES * row_count // 8), jnp.float32)
    last = col_count // LANES - 1

    to_west, to_east = pl.pallas_call(
        functools.partial(edge_kernel, ocean_comp),
        grid=(1,),
        in_specs=[
            scalar,
            whole(margin_row),
            whole(margin_col),
            pl.BlockSpec(strip, lambda i: (0, 0, 0, 0)),
            pl.BlockSpec(strip, lambda i: (0, 0, 0, last)),
        ],
        out_specs=[whole(packet)] * 2,
        out_shape=[packet] * 2,
        compiler_params=params,
        name="edge_gather",
    )(comp, margin_row, margin_col, state, state)
    forward = [(i, (i + 1) % tiles) for i in range(tiles)]
    backward = [(b, a) for a, b in forward]
    from_west = lax.ppermute(to_east, "tile", forward)
    from_east = lax.ppermute(to_west, "tile", backward)

    bundle = jax.ShapeDtypeStruct((3, 2 * PARTS, part), jnp.float32)
    centre = pl.pallas_call(
        functools.partial(centre_kernel, ocean_comp),
        grid=(1,),
        in_specs=[
            scalar,
            whole(margin_row),
            whole(margin_col),
            pl.BlockSpec((fields, 1, row_count, col_count), lambda i: (0, 0, 0, 0)),
        ],
        out_specs=whole(bundle),
        out_shape=bundle,
        compiler_params=params,
        name="centre_gather",
    )(comp, margin_row, margin_col, state)
    bundles = pl.pallas_call(
        functools.partial(pack_kernel, ocean_comp),
        grid=(1,),
        in_specs=[scalar, whole(bundle), whole(packet), whole(packet)],
        out_specs=[whole(bundle)] * ocean_comp,
        out_shape=[bundle] * ocean_comp,
        compiler_params=params,
        name="pack",
    )(comp, centre, from_west, from_east)
    got = []
    for g in range(ocean_comp):
        swap = []
        for t in range(tiles):
            swap.append((g * tiles + t, ocean_comp * tiles + t))
            swap.append((ocean_comp * tiles + t, g * tiles + t))
        got.append(lax.ppermute(bundles[g], ("comp", "tile"), swap))

    chunk = 16
    moved = pl.pallas_call(
        functools.partial(transport_kernel, ocean_comp * part),
        grid=(row_count // chunk,),
        in_specs=[
            pl.BlockSpec((fields, levels, chunk, col_count), lambda i: (0, 0, i, 0)),
            pl.BlockSpec((chunk, levels), lambda i: (i, 0)),
            pl.BlockSpec((chunk, levels - 1), lambda i: (i, 0)),
            whole(packet),
            whole(packet),
            pl.BlockSpec(memory_space=pl.ANY),
        ],
        out_specs=pl.BlockSpec((fields, levels, chunk, col_count), lambda i: (0, 0, i, 0)),
        out_shape=jax.ShapeDtypeStruct(state.shape, jnp.float32),
        compiler_params=params,
        name="transport",
    )(state, courant.T, mixing.T, from_west, from_east, bundles[0])

    surface_spec = pl.BlockSpec((fields, 1, row_count, col_count), lambda i: (0, 0, 0, 0))
    partner = jax.ShapeDtypeStruct((fields, row_count, col_count), jnp.float32)
    return pl.pallas_call(
        functools.partial(land_kernel, ocean_comp),
        grid=(1,),
        in_specs=[
            scalar,
            scalar,
            whole(margin_row),
            whole(margin_col),
            whole(margin_weight),
            whole(bundle),
            whole(bundle),
            whole(bundle),
            surface_spec,
            whole(exchange_coef),
            whole(sea_mask),
        ],
        out_specs=[surface_spec, whole(partner)],
        out_shape=[jax.ShapeDtypeStruct(state.shape, jnp.float32), partner],
        scratch_shapes=[
            pltpu.VMEM((2 * row_count, col_count), jnp.float32),
            pltpu.VMEM((row_count, 2 * LANES), jnp.float32),
            pltpu.VMEM((row_count, 2 * LANES), jnp.float32),
        ],
        input_output_aliases={8: 0},
        compiler_params=params,
        name="land",
    )(
        comp,
        margin_count.reshape(3, ocean_comp + 1),
        margin_row,
        margin_col,
        margin_weight,
        *got,
        moved,
        exchange_coef,
        sea_mask,
    )


def solution(mesh):
    in_specs = (
        P(None, None, "comp", "tile"),
        P(None, "comp"),
        P(None, "comp"),
        P("comp", "tile"),
        P("comp", "tile"),
        P("comp", "tile", None, None),
        P("comp", "tile", None, None, None),
        P("comp", "tile", None, None, None),
        P("comp", "tile", None, None, None),
    )
    out_specs = (P(None, None, "comp", "tile"), P(None, "comp", "tile"))
    return jax.shard_map(shards, mesh=mesh, in_specs=in_specs, out_specs=out_specs, check_vma=False)
```

time: 62.5 us -> 58.7 us (0.939)
  waiting for transfers between devices: 2.56 us -> 0.01 us
  Pallas kernels: 40.8 us -> 40.1 us
    pallas_call x1, Pallas kernels: 7.66 us -> 17.8 us  [shards(): pl.pallas_call(functools.partial(transport_kernel, ocean_comp * part), gr...]
    pallas_call x1, Pallas kernels: 15.9 us -> 10 us  [shards(): pl.pallas_call(functools.partial(land_kernel, ocean_comp), grid=(1,), in_...]
    pallas_call x1, Pallas kernels: 9.72 us -> 5.11 us  [shards(): pl.pallas_call(functools.partial(edge_kernel, ocean_comp), grid=(1,), in_...]
    ppermute x1, waiting for transfers between devices: 2.55 us -> 0.01 us  [shards(): from_west = lax.ppermute(to_east, 'tile', forward)]
    pallas_call x1, Pallas kernels: 7.53 us -> 5.42 us  [shards(): pl.pallas_call(functools.partial(centre_kernel, ocean_comp), grid=(1,), i...]
    pallas_call x0 -> x1, Pallas kernels: none -> 1.75 us  [shards(): pl.pallas_call(functools.partial(pack_kernel, ocean_comp), grid=(1,), in_...]
  transfers between devices with their start and end apart: 5 -> 5, of which waited for: 1 -> 0; matrix products, arithmetic and copies ran while one was open for 3% -> 3% of each run, Pallas kernels for 12% -> 40%
where the time goes in v2:
time: 58.7 us; the launch traced here: 58.4 us
  Pallas kernels  40.1 us (68%)
  starting transfers between devices  13.6 us (23%)
  local copies, waits for them, and re-layouts  3.96 us (7%)
  between operations  0.72 us (1%)
    pallas_call x1, Pallas kernels, shards(): pl.pallas_call(functools.partial(transport_kernel, ocean_comp * part), gr...  17.8 us
    pallas_call x1, Pallas kernels, shards(): pl.pallas_call(functools.partial(land_kernel, ocean_comp), grid=(1,), in_...  10 us
    ppermute x1, starting transfers between devices, shards(): from_east = lax.ppermute(to_west, 'tile', backward)  5.76 us
    ppermute x3, starting transfers between devices, shards(): got.append(lax.ppermute(bundles[g], ('comp', 'tile'), swap))  5.75 us
    pallas_call x1, Pallas kernels, shards(): pl.pallas_call(functools.partial(centre_kernel, ocean_comp), grid=(1,), i...  5.42 us
    pallas_call x1, Pallas kernels, shards(): pl.pallas_call(functools.partial(edge_kernel, ocean_comp), grid=(1,), in_...  5.11 us
    unnamed x19, local copies, waits for them, and re-layouts  3.96 us
    ppermute x1, starting transfers between devices, shards(): from_west = lax.ppermute(to_east, 'tile', forward)  2.08 us
  transfers between devices with their start and end apart: 5, of which 0 were waited for; matrix products, arithmetic and copies ran while one was open for 3% of the time, Pallas kernels for 40%

profile of v2, /device:TPU:9, one launch (start us, length us, event | category | flops | bytes accessed | tf_op | source)
XLA Modules:
  0.0 58.4 jit_solution(18030276583850075652)
XLA Ops:
  0.6 5.1 %edge_gather.1 = (f32[8,4096]{1,0:T(8,128)}, f32[8,4096]{1,0:T(8,128)}) custom-call(s32[1]{0:T(128)} %bitcast.comp_ref, s32[1,1,3,4,4096]{4,3,2,1,0:T(4,128)} %row_ref.5, s32[1,1,3,4,4096]{4,3,2,1,0:T(4,128)} %col_ref.5, f32[2,8,64,512]{3,2,1,0:T(8,128)} %state_ref.3, f32[2,8,64,512]{3,2,1,0:T(8,128)} %state_ref.3), custom_call_target="tpu_custom_call" | custom-call | tf_op jit(solution)/shard_map/edge_gather/pallas_call | solution.py:329
  5.7 0.0 copy-start.7
  5.7 0.0 copy-start.5
  5.7 2.1 %collective-permute-start = (f32[8,4096]{1,0:T(8,128)}, f32[8,4096]{1,0:T(8,128)S(1)}, u32[]{:S(2)}, u32[]{:S(2)}) collective-permute-start(f32[8,4096]{1,0:T(8,128)} %get-tuple-element.7), channel_id=1, source_target_pairs={{0,1},{1,2},{2,3},{3,4},{4,5},{5,6},{6,7},{7,8},{8,9},{9,10},{10,1... | collective-permute-start | bytes 393224 | tf_op jit(solution)/shard_map/ppermute | solution.py:346
  7.8 5.8 %collective-permute-start.1 = (f32[8,4096]{1,0:T(8,128)}, f32[8,4096]{1,0:T(8,128)S(1)}, u32[]{:S(2)}, u32[]{:S(2)}) collective-permute-start(f32[8,4096]{1,0:T(8,128)} %get-tuple-element.8), channel_id=1, source_target_pairs={{1,0},{2,1},{3,2},{4,3},{5,4},{6,5},{7,6},{8,7},{9,8},{10,9},{11,1... | collective-permute-start | bytes 393224 | tf_op jit(solution)/shard_map/ppermute | solution.py:347
  13.6 5.4 %centre_gather.1.centre_ref = f32[3,8,1024]{2,1,0:T(8,128)} custom-call(s32[1]{0:T(128)} %bitcast.comp_ref, s32[1,1,3,4,4096]{4,3,2,1,0:T(4,128)} %row_ref.5, s32[1,1,3,4,4096]{4,3,2,1,0:T(4,128)} %col_ref.5, f32[2,8,64,512]{3,2,1,0:T(8,128)} %state_ref.3), custom_call_target="tpu_custom_call" | custom-call | tf_op jit(solution)/shard_map/centre_gather/pallas_call | solution.py:350
  19.0 0.0 collective-permute-done.from_west.west_ref
  19.0 0.0 collective-permute-done.1.from_east.east_ref
  19.0 0.6 %copy-done = f32[8,4096]{1,0:T(8,128)} copy-done((f32[8,4096]{1,0:T(8,128)}, f32[8,4096]{1,0:T(8,128)S(1)}, u32[]{:S(2)}) %copy-start) | copy-done | bytes 131096
  19.7 0.0 copy-start.1
  19.7 0.7 %copy-done.1 = f32[8,4096]{1,0:T(8,128)} copy-done((f32[8,4096]{1,0:T(8,128)}, f32[8,4096]{1,0:T(8,128)S(1)}, u32[]{:S(2)}) %copy-start.1) | copy-done | bytes 131096
  20.3 1.7 %pack.1 = (f32[3,8,1024]{2,1,0:T(8,128)}, f32[3,8,1024]{2,1,0:T(8,128)}, f32[3,8,1024]{2,1,0:T(8,128)}) custom-call(s32[1]{0:T(128)} %bitcast.comp_ref, f32[3,8,1024]{2,1,0:T(8,128)} %centre_gather.1.centre_ref, f32[8,4096]{1,0:T(8,128)} %copy-done, f32[8,4096]{1,0:T(8,128)} %copy-done.1), custom_call_target="tpu_custom_call" | custom-call | tf_op jit(solution)/shard_map/pack/pallas_call | solution.py:364
  22.1 1.9 %collective-permute-start.3 = (f32[3,8,1024]{2,1,0:T(8,128)}, f32[3,8,1024]{2,1,0:T(8,128)S(1)}, u32[]{:S(2)}, u32[]{:S(2)}) collective-permute-start(f32[3,8,1024]{2,1,0:T(8,128)} %get-tuple-element.10), channel_id=1, source_target_pairs={{32,96},{96,32},{33,97},{97,33},{34,98},{98,34},{35,99},{99,35},{3... | collective-permute-start | bytes 294920 | tf_op jit(solution)/shard_map/ppermute | solution.py:379
  24.0 1.9 %collective-permute-start.4 = (f32[3,8,1024]{2,1,0:T(8,128)}, f32[3,8,1024]{2,1,0:T(8,128)S(1)}, u32[]{:S(2)}, u32[]{:S(2)}) collective-permute-start(f32[3,8,1024]{2,1,0:T(8,128)} %get-tuple-element.11), channel_id=1, source_target_pairs={{64,96},{96,64},{65,97},{97,65},{66,98},{98,66},{67,99},{99,67},{6... | collective-permute-start | bytes 294920 | tf_op jit(solution)/shard_map/ppermute | solution.py:379
  25.9 1.9 %collective-permute-start.2 = (f32[3,8,1024]{2,1,0:T(8,128)}, f32[3,8,1024]{2,1,0:T(8,128)S(1)}, u32[]{:S(2)}, u32[]{:S(2)}) collective-permute-start(f32[3,8,1024]{2,1,0:T(8,128)} %get-tuple-element.9.unused_ref), channel_id=1, source_target_pairs={{0,96},{96,0},{1,97},{97,1},{2,98},{98,2},{3,99},{99,3},{4,100},{1... | collective-permute-start | bytes 294920 | tf_op jit(solution)/shard_map/ppermute | solution.py:379
  27.8 0.0 copy-done.7
  27.8 0.6 copy.16
  28.4 0.0 copy-done.5
  28.4 0.7 %copy.12 = f32[8,64]{0,1:T(8,128)} copy(f32[8,64]{1,0:T(8,128)S(1)} %copy-done.5) | data formatting | bytes 4096 | tf_op args[1]
  29.1 0.0 copy-done.6
  29.1 0.7 %copy.13 = f32[7,64]{0,1:T(8,128)} copy(f32[7,64]{1,0:T(8,128)S(1)} %copy-done.6) | data formatting | bytes 3584 | tf_op args[2]
  29.8 17.8 %transport.1.field_ref = f32[2,8,64,512]{3,2,1,0:T(8,128)} custom-call(f32[2,8,64,512]{3,2,1,0:T(8,128)} %state_ref.3, f32[64,8]{1,0:T(8,128)} %bitcast.6, f32[64,7]{1,0:T(8,128)} %bitcast.7, f32[8,4096]{1,0:T(8,128)} %copy-done, f32[8,4096]{1,0:T(8,128)} %copy-done.1, f32[3,8,1024]{2,1,0:T(8,128)} %get-tuple-element.9.unused_ref), custom_call_target="tpu_custom_call" | custom-call | tf_op jit(solution)/shard_map/transport/pallas_call | solution.py:382
  47.7 0.0 collective-permute-done.3.got_1
  47.7 0.0 copy-start.2
  47.7 0.0 collective-permute-done.4.got_2
  47.7 0.0 copy-start.3
  47.7 0.0 collective-permute-done.2.got_0
  47.7 0.0 copy-start.4
  47.7 0.6 %copy-done.2 = f32[3,8,1024]{2,1,0:T(8,128)} copy-done((f32[3,8,1024]{2,1,0:T(8,128)}, f32[3,8,1024]{2,1,0:T(8,128)S(1)}, u32[]{:S(2)}) %copy-start.2) | copy-done | bytes 98328
  48.3 0.0 copy-done.3
  48.3 0.0 copy-done.4
  48.4 10.0 %land.1 = (f32[2,8,64,512]{3,2,1,0:T(8,128)}, f32[2,64,512]{2,1,0:T(8,128)}) custom-call(s32[1]{0:T(128)} %bitcast.comp_ref, s32[3,4]{1,0:T(4,128)} %bitcast.8, s32[1,1,3,4,4096]{4,3,2,1,0:T(4,128)} %row_ref.5, s32[1,1,3,4,4096]{4,3,2,1,0:T(4,128)} %col_ref.5, f32[1,1,3,4,4096]{4,3,2,1,0:T(4,128)} %weight_ref.1, ...), custom_call_target="tpu_custom_call", output_to_operand_aliasing={{0}: (8, {})} | custom-call | tf_op jit(solution)/shard_map/land/pallas_call | solution.py:401
  (2 shorter events, 0.0 us)
Async XLA Ops:
  5.7 22.1 %copy-start.7 = (s32[1,1,3,4]{3,1,2,0:T(1,128)S(1)}, s32[1,1,3,4]{3,1,2,0:T(1,128)}, u32[]{:S(2)}) copy-start(s32[1,1,3,4]{3,1,2,0:T(1,128)} %param.14) | copy-start | bytes 148
  5.7 22.7 %copy-start.5 = (f32[8,64]{1,0:T(8,128)S(1)}, f32[8,64]{1,0:T(8,128)}, u32[]{:S(2)}) copy-start(f32[8,64]{1,0:T(8,128)} %param.10) | copy-start | bytes 6148
  5.7 23.4 %copy-start.6 = (f32[7,64]{1,0:T(8,128)S(1)}, f32[7,64]{1,0:T(8,128)}, u32[]{:S(2)}) copy-start(f32[7,64]{1,0:T(8,128)} %param.11) | copy-start | bytes 5380
  5.7 13.3 %collective-permute-start = (f32[8,4096]{1,0:T(8,128)}, f32[8,4096]{1,0:T(8,128)S(1)}, u32[]{:S(2)}, u32[]{:S(2)}) collective-permute-start(f32[8,4096]{1,0:T(8,128)} %get-tuple-element.7), channel_id=1, source_target_pairs={{0,1},{1,2},{2,3},{3,4},{4,5},{5,6},{6,7},{7,8},{8,9},{9,10},{10,1... | collective-permute-start | bytes 393224 | tf_op jit(solution)/shard_map/ppermute | solution.py:346
  7.8 11.2 %collective-permute-start.1 = (f32[8,4096]{1,0:T(8,128)}, f32[8,4096]{1,0:T(8,128)S(1)}, u32[]{:S(2)}, u32[]{:S(2)}) collective-permute-start(f32[8,4096]{1,0:T(8,128)} %get-tuple-element.8), channel_id=1, source_target_pairs={{1,0},{2,1},{3,2},{4,3},{5,4},{6,5},{7,6},{8,7},{9,8},{10,9},{11,1... | collective-permute-start | bytes 393224 | tf_op jit(solution)/shard_map/ppermute | solution.py:347
  19.0 0.7 %copy-start = (f32[8,4096]{1,0:T(8,128)}, f32[8,4096]{1,0:T(8,128)S(1)}, u32[]{:S(2)}) copy-start(f32[8,4096]{1,0:T(8,128)S(1)} %collective-permute-done.from_west.west_ref) | copy-start | bytes 393220
  19.7 0.7 %copy-start.1 = (f32[8,4096]{1,0:T(8,128)}, f32[8,4096]{1,0:T(8,128)S(1)}, u32[]{:S(2)}) copy-start(f32[8,4096]{1,0:T(8,128)S(1)} %collective-permute-done.1.from_east.east_ref) | copy-start | bytes 393220
  22.1 25.6 %collective-permute-start.3 = (f32[3,8,1024]{2,1,0:T(8,128)}, f32[3,8,1024]{2,1,0:T(8,128)S(1)}, u32[]{:S(2)}, u32[]{:S(2)}) collective-permute-start(f32[3,8,1024]{2,1,0:T(8,128)} %get-tuple-element.10), channel_id=1, source_target_pairs={{32,96},{96,32},{33,97},{97,33},{34,98},{98,34},{35,99},{99,35},{3... | collective-permute-start | bytes 294920 | tf_op jit(solution)/shard_map/ppermute | solution.py:379
  24.0 23.7 %collective-permute-start.4 = (f32[3,8,1024]{2,1,0:T(8,128)}, f32[3,8,1024]{2,1,0:T(8,128)S(1)}, u32[]{:S(2)}, u32[]{:S(2)}) collective-permute-start(f32[3,8,1024]{2,1,0:T(8,128)} %get-tuple-element.11), channel_id=1, source_target_pairs={{64,96},{96,64},{65,97},{97,65},{66,98},{98,66},{67,99},{99,67},{6... | collective-permute-start | bytes 294920 | tf_op jit(solution)/shard_map/ppermute | solution.py:379
  25.9 21.8 %collective-permute-start.2 = (f32[3,8,1024]{2,1,0:T(8,128)}, f32[3,8,1024]{2,1,0:T(8,128)S(1)}, u32[]{:S(2)}, u32[]{:S(2)}) collective-permute-start(f32[3,8,1024]{2,1,0:T(8,128)} %get-tuple-element.9.unused_ref), channel_id=1, source_target_pairs={{0,96},{96,0},{1,97},{97,1},{2,98},{98,2},{3,99},{99,3},{4,100},{1... | collective-permute-start | bytes 294920 | tf_op jit(solution)/shard_map/ppermute | solution.py:379
  47.7 0.6 %copy-start.2 = (f32[3,8,1024]{2,1,0:T(8,128)}, f32[3,8,1024]{2,1,0:T(8,128)S(1)}, u32[]{:S(2)}) copy-start(f32[3,8,1024]{2,1,0:T(8,128)S(1)} %collective-permute-done.3.got_1) | copy-start | bytes 294916
  47.7 0.7 %copy-start.3 = (f32[3,8,1024]{2,1,0:T(8,128)}, f32[3,8,1024]{2,1,0:T(8,128)S(1)}, u32[]{:S(2)}) copy-start(f32[3,8,1024]{2,1,0:T(8,128)S(1)} %collective-permute-done.4.got_2) | copy-start | bytes 294916
  47.7 0.7 %copy-start.4 = (f32[3,8,1024]{2,1,0:T(8,128)}, f32[3,8,1024]{2,1,0:T(8,128)S(1)}, u32[]{:S(2)}) copy-start(f32[3,8,1024]{2,1,0:T(8,128)S(1)} %collective-permute-done.2.got_0) | copy-start | bytes 294916

commit v3 on v2

--- a/solution.py
+++ b/solution.py
@@ -9,7 +9,7 @@
 SUBSTEPS = 2
 LANES = 128
 PARTS = 4
-VMEM_LIMIT = 56 * 1024 * 1024
+VMEM_LIMIT = 24 * 1024 * 1024
 
 
 def split_halves(values):
@@ -117,7 +117,7 @@
         lists([(0, ocean_comp)])
 
 
-def pack_kernel(ocean_comp, comp_ref, centre_ref, from_west, from_east, *outs):
+def pack_kernel(ocean_comp, comp_ref, count_ref, centre_ref, from_west, from_east, *outs):
     ocean = comp_ref[0] == ocean_comp
     part = centre_ref.shape[-1]
 
@@ -137,66 +137,69 @@
         fill([0] * ocean_comp)
 
 
-def transport_kernel(halo_start, state_ref, courant_ref, mixing_ref, west_ref, east_ref, unused_ref, out_ref):
+def transport_kernel(
+    halo_start, state_ref, courant_ref, mixing_ref, west_ref, east_ref, unused_ref, out_ref, courant_by_row, mixing_by_row
+):
     fields, levels, rows, cols = state_ref.shape
     step = pl.program_id(0)
-    full = cols + LANES
-    lane = lax.broadcasted_iota(jnp.int32, (8, LANES), 1)
     tiles = cols // LANES
 
-    def advance(q, middle, ahead, behind):
-        back = [pltpu.roll(t, 1, 1) for t in q]
-        fore = [pltpu.roll(t, LANES - 1, 1) for t in q]
-        done = []
-        for i in range(len(q)):
-            left = jnp.where(lane == 0, back[i - 1], back[i])
-            right = jnp.where(lane == LANES - 1, fore[(i + 1) % len(q)], fore[i])
-            done.append(q[i] * middle + right * ahead + left * behind)
-        return done
-
-    for block in range(rows // 8):
-        span = slice(8 * block, 8 * block + 8)
-        start = pl.multiple_of(halo_start + (step * (rows // 8) + block) * LANES, LANES)
-        west = west_ref[:, pl.ds(start, LANES)]
-        east = east_ref[:, pl.ds(start, LANES)]
-        coeffs = []
+    @pl.when(step == 0)
+    def _():
+        courant_by_row[...] = courant_ref[...].T
+        mixing_by_row[...] = mixing_ref[...].T
+
+    def spread(ref, level):
+        here = pl.ds(pl.multiple_of(step * rows, 8), rows)
+        return jnp.broadcast_to(ref[here, level : level + 1], (rows, LANES))[None]
+
+    source = lax.broadcasted_iota(jnp.int32, (2 * LANES, 2 * LANES), 0) % LANES
+    target = lax.broadcasted_iota(jnp.int32, (2 * LANES, 2 * LANES), 1)
+    wanted = jnp.where(target < LANES, (target + LANES - 1) % LANES, (target + 1) % LANES)
+    mover = jnp.where(source == wanted, 1.0, 0.0).astype(jnp.bfloat16)
+    lane = lax.broadcasted_iota(jnp.int32, (levels, rows, LANES), 2)
+    low_end = lane == 0
+    high_end = lane == LANES - 1
+    halo_lane = lax.broadcasted_iota(jnp.int32, (8, LANES), 1)
+
+    speed = jnp.concatenate([spread(courant_by_row, level) for level in range(levels)], axis=0)
+    half = 0.5 * speed
+    square = half * speed
+    middle, ahead, behind = 1.0 - 2.0 * square, square - half, square + half
+    mix = jnp.concatenate([spread(mixing_by_row, level) for level in range(levels - 1)], axis=0)
+    for f in range(fields):
+        edges = []
         for level in range(levels):
-            c = jnp.broadcast_to(courant_ref[span, level : level + 1], (8, LANES))
-            half = 0.5 * c
-            square = half * c
-            coeffs.append((1.0 - 2.0 * square, square - half, square + half))
-        mix = [jnp.broadcast_to(mixing_ref[span, level : level + 1], (8, LANES)) for level in range(levels - 1)]
-        for f in range(fields):
-
-            def source():
-                for level in range(levels):
-                    k = f * levels + level
-                    left = pltpu.roll(west, (LANES - 2 - 2 * k) % LANES, 1)
-                    right = pltpu.roll(east, (LANES - 2 * k) % LANES, 1)
-                    edge = jnp.where(lane < 64, right, left)
-                    yield [state_ref[f, level, span, LANES * i : LANES * i + LANES] for i in range(tiles)] + [edge]
-
-            def substep(stream):
-                before = None
-                flux_below = None
-                for level, q in enumerate(stream):
-                    now = advance(q, *coeffs[level])
-                    if before is not None:
-                        flux = [mix[level - 1] * (n - b) for n, b in zip(now, before)]
-                        mixed = [b + x for b, x in zip(before, flux)]
-                        if flux_below is not None:
-                            mixed = [m - x for m, x in zip(mixed, flux_below)]
-                        yield mixed
-                        flux_below = flux
-                    before = now
-                yield [b - x for b, x in zip(before, flux_below)]
-
-            stream = source()
-            for unused in range(SUBSTEPS):
-                stream = substep(stream)
-            for level, q in enumerate(stream):
-                for i in range(tiles):
-                    out_ref[f, level, span, LANES * i : LANES * i + LANES] = q[i]
+            k = f * levels + level
+            blocks = []
+            for block in range(rows // 8):
+                start = pl.multiple_of(halo_start + (step * (rows // 8) + block) * LANES, LANES)
+                left = pltpu.roll(west_ref[:, pl.ds(start, LANES)], (LANES - 2 - 2 * k) % LANES, 1)
+                right = pltpu.roll(east_ref[:, pl.ds(start, LANES)], (LANES - 2 * k) % LANES, 1)
+                blocks.append(jnp.where(halo_lane < LANES // 2, right, left))
+            edges.append(jnp.concatenate(blocks, axis=0)[None])
+        field = [state_ref[f, :, :, LANES * i : LANES * i + LANES] for i in range(tiles)]
+        field.append(jnp.concatenate(edges, axis=0))
+        for substep in range(SUBSTEPS):
+            back, fore = [], []
+            for tile in field:
+                pair = jnp.concatenate(split_halves(tile.reshape(levels * rows, LANES)), axis=1)
+                moved = jnp.dot(pair, mover, preferred_element_type=jnp.float32)
+                back.append(moved[:, :LANES].reshape(tile.shape))
+                fore.append(moved[:, LANES:].reshape(tile.shape))
+            count = tiles if substep == SUBSTEPS - 1 else tiles + 1
+            after = []
+            for i in range(count):
+                left = jnp.where(low_end, back[i - 1], back[i])
+                right = jnp.where(high_end, fore[(i + 1) % (tiles + 1)], fore[i])
+                q = field[i] * middle + right * ahead + left * behind
+                flux = mix * (q[1:] - q[:-1])
+                after.append(
+                    jnp.concatenate([q[:1] + flux[:1], q[1:-1] + flux[1:] - flux[:-1], q[-1:] - flux[-1:]], axis=0)
+                )
+            field = after
+        for i in range(tiles):
+            out_ref[f, :, :, LANES * i : LANES * i + LANES] = field[i]
 
 
 def land_kernel(
@@ -320,6 +323,7 @@
     part = slots // PARTS
     tiles = lax.axis_size("tile")
     comp = lax.axis_index("comp").astype(jnp.int32).reshape(1)
+    counts = margin_count.reshape(3, ocean_comp + 1)
     scalar = pl.BlockSpec(memory_space=pltpu.SMEM)
     params = pltpu.CompilerParams(vmem_limit_bytes=VMEM_LIMIT)
     strip = (fields, levels, row_count, LANES)
@@ -364,12 +368,12 @@
     bundles = pl.pallas_call(
         functools.partial(pack_kernel, ocean_comp),
         grid=(1,),
-        in_specs=[scalar, whole(bundle), whole(packet), whole(packet)],
+        in_specs=[scalar, scalar, whole(bundle), whole(packet), whole(packet)],
         out_specs=[whole(bundle)] * ocean_comp,
         out_shape=[bundle] * ocean_comp,
         compiler_params=params,
         name="pack",
-    )(comp, centre, from_west, from_east)
+    )(comp, counts, centre, from_west, from_east)
     got = []
     for g in range(ocean_comp):
         swap = []
@@ -378,23 +382,27 @@
             swap.append((ocean_comp * tiles + t, g * tiles + t))
         got.append(lax.ppermute(bundles[g], ("comp", "tile"), swap))
 
-    chunk = 16
+    chunk = 32
     moved = pl.pallas_call(
         functools.partial(transport_kernel, ocean_comp * part),
         grid=(row_count // chunk,),
         in_specs=[
             pl.BlockSpec((fields, levels, chunk, col_count), lambda i: (0, 0, i, 0)),
-            pl.BlockSpec((chunk, levels), lambda i: (i, 0)),
-            pl.BlockSpec((chunk, levels - 1), lambda i: (i, 0)),
+            whole(courant),
+            whole(mixing),
             whole(packet),
             whole(packet),
             pl.BlockSpec(memory_space=pl.ANY),
         ],
         out_specs=pl.BlockSpec((fields, levels, chunk, col_count), lambda i: (0, 0, i, 0)),
         out_shape=jax.ShapeDtypeStruct(state.shape, jnp.float32),
+        scratch_shapes=[
+            pltpu.VMEM((row_count, levels), jnp.float32),
+            pltpu.VMEM((row_count, levels - 1), jnp.float32),
+        ],
         compiler_params=params,
         name="transport",
-    )(state, courant.T, mixing.T, from_west, from_east, bundles[0])
+    )(state, courant, mixing, from_west, from_east, bundles[0])
 
     surface_spec = pl.BlockSpec((fields, 1, row_count, col_count), lambda i: (0, 0, 0, 0))
     partner = jax.ShapeDtypeStruct((fields, row_count, col_count), jnp.float32)
@@ -426,7 +434,7 @@
         name="land",
     )(
         comp,
-        margin_count.reshape(3, ocean_comp + 1),
+        counts,
         margin_row,
         margin_col,
         margin_weight,

time: 58.7 us -> 39.4 us (0.67)
  Pallas kernels: 40.1 us -> 21 us
    pallas_call x1, Pallas kernels: 17.8 us -> 4.27 us  [shards(): pl.pallas_call(functools.partial(transport_kernel, ocean_comp * part), gr...]
    pallas_call x1, Pallas kernels: 5.11 us -> 2.97 us  [shards(): pl.pallas_call(functools.partial(edge_kernel, ocean_comp), grid=(1,), in_...]
    pallas_call x1, Pallas kernels: 5.42 us -> 3.65 us  [shards(): pl.pallas_call(functools.partial(centre_kernel, ocean_comp), grid=(1,), i...]
    pallas_call x1, Pallas kernels: 1.75 us -> 0.59 us  [shards(): pl.pallas_call(functools.partial(pack_kernel, ocean_comp), grid=(1,), in_...]
    unnamed x19 -> x25, local copies, waits for them, and re-layouts: 3.96 us -> 3.5 us
  transfers between devices with their start and end apart: 5 -> 5, of which waited for: 0 -> 0; matrix products, arithmetic and copies ran while one was open for 3% -> 0% of each run, Pallas kernels for 40% -> 20%
where the time goes in v3:
time: 39.4 us; the launch traced here: 39.1 us
  Pallas kernels  21 us (53%)
  starting transfers between devices  13.7 us (35%)
  local copies, waits for them, and re-layouts  3.5 us (9%)
  between operations  0.86 us (2%)
    pallas_call x1, Pallas kernels, shards(): pl.pallas_call(functools.partial(land_kernel, ocean_comp), grid=(1,), in_...  9.56 us
    ppermute x3, starting transfers between devices, shards(): got.append(lax.ppermute(bundles[g], ('comp', 'tile'), swap))  5.89 us
    ppermute x1, starting transfers between devices, shards(): from_east = lax.ppermute(to_west, 'tile', backward)  5.75 us
    pallas_call x1, Pallas kernels, shards(): pl.pallas_call(functools.partial(transport_kernel, ocean_comp * part), gr...  4.27 us
    pallas_call x1, Pallas kernels, shards(): pl.pallas_call(functools.partial(centre_kernel, ocean_comp), grid=(1,), i...  3.65 us
    unnamed x25, local copies, waits for them, and re-layouts  3.5 us
    pallas_call x1, Pallas kernels, shards(): pl.pallas_call(functools.partial(edge_kernel, ocean_comp), grid=(1,), in_...  2.97 us
    ppermute x1, starting transfers between devices, shards(): from_west = lax.ppermute(to_east, 'tile', forward)  2.09 us
  transfers between devices with their start and end apart: 5, of which 0 were waited for; matrix products, arithmetic and copies ran while one was open for 0% of the time, Pallas kernels for 20%

profile of v3, /device:TPU:9, one launch (start us, length us, event | category | flops | bytes accessed | tf_op | source)
XLA Modules:
  0.0 39.1 jit_solution(10822953582658755061)
XLA Ops:
  0.6 0.0 copy-start
  0.6 1.6 %copy-done = f32[2,8,64,512]{3,2,1,0:T(8,128)S(1)} copy-done((f32[2,8,64,512]{3,2,1,0:T(8,128)S(1)}, f32[2,8,64,512]{3,2,1,0:T(8,128)}, u32[]{:S(2)}) %copy-start) | copy-done | bytes 2097176
  2.2 0.9 %copy-done.2 = s32[1,1,3,4,4096]{4,3,2,1,0:T(4,128)S(1)} copy-done((s32[1,1,3,4,4096]{4,3,2,1,0:T(4,128)S(1)}, s32[1,1,3,4,4096]{4,3,2,1,0:T(4,128)}, u32[]{:S(2)}) %copy-start.2) | copy-done | bytes 196632
  3.2 0.9 %copy-done.4 = s32[1,1,3,4,4096]{4,3,2,1,0:T(4,128)S(1)} copy-done((s32[1,1,3,4,4096]{4,3,2,1,0:T(4,128)S(1)}, s32[1,1,3,4,4096]{4,3,2,1,0:T(4,128)}, u32[]{:S(2)}) %copy-start.4) | copy-done | bytes 196632
  4.1 3.0 %edge_gather.1 = (f32[8,4096]{1,0:T(8,128)S(1)}, f32[8,4096]{1,0:T(8,128)S(1)}) custom-call(s32[1]{0:T(128)} %bitcast.comp_ref, s32[1,1,3,4,4096]{4,3,2,1,0:T(4,128)S(1)} %copy-done.2, s32[1,1,3,4,4096]{4,3,2,1,0:T(4,128)S(1)} %copy-done.4, f32[2,8,64,512]{3,2,1,0:T(8,128)S(1)} %copy-done, f32[2,8,64,512]{3,2,1,0:T(8,128)S(1)} %copy-done), custom_call_target="tpu_custom_call" | custom-call | tf_op jit(solution)/shard_map/edge_gather/pallas_call | solution.py:333
  7.1 0.0 copy-start.11
  7.1 0.0 copy-start.1
  7.1 0.0 copy-start.9
  7.1 0.0 copy-start.10
  7.1 2.1 %collective-permute-start = (f32[8,4096]{1,0:T(8,128)S(1)}, f32[8,4096]{1,0:T(8,128)S(1)}, u32[]{:S(2)}, u32[]{:S(2)}) collective-permute-start(f32[8,4096]{1,0:T(8,128)S(1)} %get-tuple-element.7), channel_id=1, source_target_pairs={{0,1},{1,2},{2,3},{3,4},{4,5},{5,6},{6,7},{7,8},{8,9},{9,10},{10,1... | collective-permute-start | bytes 393224 | tf_op jit(solution)/shard_map/ppermute | solution.py:350
  9.2 5.7 %collective-permute-start.1 = (f32[8,4096]{1,0:T(8,128)S(1)}, f32[8,4096]{1,0:T(8,128)S(1)}, u32[]{:S(2)}, u32[]{:S(2)}) collective-permute-start(f32[8,4096]{1,0:T(8,128)S(1)} %get-tuple-element.8), channel_id=1, source_target_pairs={{1,0},{2,1},{3,2},{4,3},{5,4},{6,5},{7,6},{8,7},{9,8},{10,9},{11,1... | collective-permute-start | bytes 393224 | tf_op jit(solution)/shard_map/ppermute | solution.py:351
  14.9 3.6 %centre_gather.1.centre_ref = f32[3,8,1024]{2,1,0:T(8,128)S(1)} custom-call(s32[1]{0:T(128)} %bitcast.comp_ref, s32[1,1,3,4,4096]{4,3,2,1,0:T(4,128)S(1)} %copy-done.2, s32[1,1,3,4,4096]{4,3,2,1,0:T(4,128)S(1)} %copy-done.4, f32[2,8,64,512]{3,2,1,0:T(8,128)S(1)} %copy-done), custom_call_target="tpu_custom_call" | custom-call | tf_op jit(solution)/shard_map/centre_gather/pallas_call | solution.py:354
  18.6 0.0 collective-permute-done.from_west.west_ref
  18.6 0.0 collective-permute-done.1.from_east.east_ref
  18.6 0.6 %pack.1 = (f32[3,8,1024]{2,1,0:T(8,128)S(1)}, f32[3,8,1024]{2,1,0:T(8,128)S(1)}, f32[3,8,1024]{2,1,0:T(8,128)S(1)}) custom-call(s32[1]{0:T(128)} %bitcast.comp_ref, s32[3,4]{1,0:T(4,128)S(1)} %bitcast.4, f32[3,8,1024]{2,1,0:T(8,128)S(1)} %centre_gather.1.centre_ref, f32[8,4096]{1,0:T(8,128)S(1)} %collective-permute-done.from_west.west_ref, ...), custom_call_target="tpu_custom_call" | custom-call | tf_op jit(solution)/shard_map/pack/pallas_call | solution.py:368
  19.2 1.9 %collective-permute-start.3 = (f32[3,8,1024]{2,1,0:T(8,128)S(1)}, f32[3,8,1024]{2,1,0:T(8,128)S(1)}, u32[]{:S(2)}, u32[]{:S(2)}) collective-permute-start(f32[3,8,1024]{2,1,0:T(8,128)S(1)} %get-tuple-element.10), channel_id=1, source_target_pairs={{32,96},{96,32},{33,97},{97,33},{34,98},{98,34},{35,99},{99,35},{3... | collective-permute-start | bytes 294920 | tf_op jit(solution)/shard_map/ppermute | solution.py:383
  21.2 1.9 %collective-permute-start.4 = (f32[3,8,1024]{2,1,0:T(8,128)S(1)}, f32[3,8,1024]{2,1,0:T(8,128)S(1)}, u32[]{:S(2)}, u32[]{:S(2)}) collective-permute-start(f32[3,8,1024]{2,1,0:T(8,128)S(1)} %get-tuple-element.11), channel_id=1, source_target_pairs={{64,96},{96,64},{65,97},{97,65},{66,98},{98,66},{67,99},{99,67},{6... | collective-permute-start | bytes 294920 | tf_op jit(solution)/shard_map/ppermute | solution.py:383
  23.1 0.0 copy-start.3
  23.1 0.0 copy-start.5
  23.1 0.0 copy-start.6
  23.1 0.0 copy-start.7
  23.1 0.0 copy-start.8
  23.2 2.1 %collective-permute-start.2 = (f32[3,8,1024]{2,1,0:T(8,128)S(1)}, f32[3,8,1024]{2,1,0:T(8,128)S(1)}, u32[]{:S(2)}, u32[]{:S(2)}) collective-permute-start(f32[3,8,1024]{2,1,0:T(8,128)S(1)} %get-tuple-element.9.unused_ref), channel_id=1, source_target_pairs={{0,96},{96,0},{1,97},{97,1},{2,98},{98,2},{3,99},{99,3},{4,100},{1... | collective-permute-start | bytes 294920 | tf_op jit(solution)/shard_map/ppermute | solution.py:383
  25.2 0.0 copy-done.1
  25.2 0.0 copy-done.9
  25.2 0.0 copy-done.10
  25.3 4.3 %transport.1.field_ref = f32[2,8,64,512]{3,2,1,0:T(8,128)} custom-call(f32[2,8,64,512]{3,2,1,0:T(8,128)S(1)} %copy-done.1, f32[8,64]{1,0:T(8,128)S(1)} %copy-done.9, f32[7,64]{1,0:T(8,128)S(1)} %copy-done.10, f32[8,4096]{1,0:T(8,128)S(1)} %collective-permute-done.from_west.west_ref, f32[8,4096]{1,0:T(8,128)S(1)} %collective-permute-done.1.from_east.east_ref, ...), custom_call_target="tpu_custom_call" | custom-call | tf_op jit(solution)/shard_map/transport/pallas_call | solution.py:386
  29.5 0.0 collective-permute-done.3.got_1
  29.5 0.0 collective-permute-done.4.got_2
  29.5 0.0 collective-permute-done.2.got_0
  29.5 0.0 copy-done.3
  29.6 9.6 %land.1 = (f32[2,8,64,512]{3,2,1,0:T(8,128)}, f32[2,64,512]{2,1,0:T(8,128)}) custom-call(s32[1]{0:T(128)} %bitcast.comp_ref, s32[3,4]{1,0:T(4,128)S(1)} %bitcast.5, s32[1,1,3,4,4096]{4,3,2,1,0:T(4,128)S(1)} %copy-done.3, s32[1,1,3,4,4096]{4,3,2,1,0:T(4,128)S(1)} %copy-done.5, f32[1,1,3,4,4096]{4,3,2,1,0:T(4,128)S(1)} %copy-done.6, ...), custom_call_target="tpu_custom_call", output_to_operand_aliasing={{0}: (8, {})} | custom-call | tf_op jit(solution)/shard_map/land/pallas_call | solution.py:409
  (8 shorter events, 0.0 us)
Async XLA Ops:
  0.6 1.6 %copy-start = (f32[2,8,64,512]{3,2,1,0:T(8,128)S(1)}, f32[2,8,64,512]{3,2,1,0:T(8,128)}, u32[]{:S(2)}) copy-start(f32[2,8,64,512]{3,2,1,0:T(8,128)} %state_ref.3) | copy-start | bytes 6291460
  2.2 0.9 %copy-start.2 = (s32[1,1,3,4,4096]{4,3,2,1,0:T(4,128)S(1)}, s32[1,1,3,4,4096]{4,3,2,1,0:T(4,128)}, u32[]{:S(2)}) copy-start(s32[1,1,3,4,4096]{4,3,2,1,0:T(4,128)} %row_ref.5) | copy-start | bytes 589828
  3.2 0.9 %copy-start.4 = (s32[1,1,3,4,4096]{4,3,2,1,0:T(4,128)S(1)}, s32[1,1,3,4,4096]{4,3,2,1,0:T(4,128)}, u32[]{:S(2)}) copy-start(s32[1,1,3,4,4096]{4,3,2,1,0:T(4,128)} %col_ref.5) | copy-start | bytes 589828
  7.1 11.5 %copy-start.11 = (s32[1,1,3,4]{3,1,2,0:T(1,128)S(1)}, s32[1,1,3,4]{3,1,2,0:T(1,128)}, u32[]{:S(2)}) copy-start(s32[1,1,3,4]{3,1,2,0:T(1,128)} %param.14) | copy-start | bytes 148
  7.1 18.2 %copy-start.1 = (f32[2,8,64,512]{3,2,1,0:T(8,128)S(1)}, f32[2,8,64,512]{3,2,1,0:T(8,128)}, u32[]{:S(2)}) copy-start(f32[2,8,64,512]{3,2,1,0:T(8,128)} %state_ref.3) | copy-start | bytes 6291460
  7.1 18.1 %copy-start.9 = (f32[8,64]{1,0:T(8,128)S(1)}, f32[8,64]{1,0:T(8,128)}, u32[]{:S(2)}) copy-start(f32[8,64]{1,0:T(8,128)} %courant_ref.1) | copy-start | bytes 6148
  7.1 18.1 %copy-start.10 = (f32[7,64]{1,0:T(8,128)S(1)}, f32[7,64]{1,0:T(8,128)}, u32[]{:S(2)}) copy-start(f32[7,64]{1,0:T(8,128)} %mixing_ref.1) | copy-start | bytes 5380
  7.1 11.5 %collective-permute-start = (f32[8,4096]{1,0:T(8,128)S(1)}, f32[8,4096]{1,0:T(8,128)S(1)}, u32[]{:S(2)}, u32[]{:S(2)}) collective-permute-start(f32[8,4096]{1,0:T(8,128)S(1)} %get-tuple-element.7), channel_id=1, source_target_pairs={{0,1},{1,2},{2,3},{3,4},{4,5},{5,6},{6,7},{7,8},{8,9},{9,10},{10,1... | collective-permute-start | bytes 393224 | tf_op jit(solution)/shard_map/ppermute | solution.py:350
  9.2 9.4 %collective-permute-start.1 = (f32[8,4096]{1,0:T(8,128)S(1)}, f32[8,4096]{1,0:T(8,128)S(1)}, u32[]{:S(2)}, u32[]{:S(2)}) collective-permute-start(f32[8,4096]{1,0:T(8,128)S(1)} %get-tuple-element.8), channel_id=1, source_target_pairs={{1,0},{2,1},{3,2},{4,3},{5,4},{6,5},{7,6},{8,7},{9,8},{10,9},{11,1... | collective-permute-start | bytes 393224 | tf_op jit(solution)/shard_map/ppermute | solution.py:351
  19.2 10.3 %collective-permute-start.3 = (f32[3,8,1024]{2,1,0:T(8,128)S(1)}, f32[3,8,1024]{2,1,0:T(8,128)S(1)}, u32[]{:S(2)}, u32[]{:S(2)}) collective-permute-start(f32[3,8,1024]{2,1,0:T(8,128)S(1)} %get-tuple-element.10), channel_id=1, source_target_pairs={{32,96},{96,32},{33,97},{97,33},{34,98},{98,34},{35,99},{99,35},{3... | collective-permute-start | bytes 294920 | tf_op jit(solution)/shard_map/ppermute | solution.py:383
  21.2 8.4 %collective-permute-start.4 = (f32[3,8,1024]{2,1,0:T(8,128)S(1)}, f32[3,8,1024]{2,1,0:T(8,128)S(1)}, u32[]{:S(2)}, u32[]{:S(2)}) collective-permute-start(f32[3,8,1024]{2,1,0:T(8,128)S(1)} %get-tuple-element.11), channel_id=1, source_target_pairs={{64,96},{96,64},{65,97},{97,65},{66,98},{98,66},{67,99},{99,67},{6... | collective-permute-start | bytes 294920 | tf_op jit(solution)/shard_map/ppermute | solution.py:383
  23.1 6.4 %copy-start.3 = (s32[1,1,3,4,4096]{4,3,2,1,0:T(4,128)S(1)}, s32[1,1,3,4,4096]{4,3,2,1,0:T(4,128)}, u32[]{:S(2)}) copy-start(s32[1,1,3,4,4096]{4,3,2,1,0:T(4,128)} %row_ref.5) | copy-start | bytes 589828
  23.1 6.4 %copy-start.5 = (s32[1,1,3,4,4096]{4,3,2,1,0:T(4,128)S(1)}, s32[1,1,3,4,4096]{4,3,2,1,0:T(4,128)}, u32[]{:S(2)}) copy-start(s32[1,1,3,4,4096]{4,3,2,1,0:T(4,128)} %col_ref.5) | copy-start | bytes 589828
  23.1 6.4 %copy-start.6 = (f32[1,1,3,4,4096]{4,3,2,1,0:T(4,128)S(1)}, f32[1,1,3,4,4096]{4,3,2,1,0:T(4,128)}, u32[]{:S(2)}) copy-start(f32[1,1,3,4,4096]{4,3,2,1,0:T(4,128)} %weight_ref.1) | copy-start | bytes 589828
  23.1 6.4 %copy-start.7 = (f32[64,512]{1,0:T(8,128)S(1)}, f32[64,512]{1,0:T(8,128)}, u32[]{:S(2)}) copy-start(f32[64,512]{1,0:T(8,128)} %coef_ref.1) | copy-start | bytes 393220
  23.1 6.4 %copy-start.8 = (s32[64,512]{1,0:T(8,128)S(1)}, s32[64,512]{1,0:T(8,128)}, u32[]{:S(2)}) copy-start(s32[64,512]{1,0:T(8,128)} %mask_ref.1) | copy-start | bytes 393220
  23.2 6.4 %collective-permute-start.2 = (f32[3,8,1024]{2,1,0:T(8,128)S(1)}, f32[3,8,1024]{2,1,0:T(8,128)S(1)}, u32[]{:S(2)}, u32[]{:S(2)}) collective-permute-start(f32[3,8,1024]{2,1,0:T(8,128)S(1)} %get-tuple-element.9.unused_ref), channel_id=1, source_target_pairs={{0,96},{96,0},{1,97},{97,1},{2,98},{98,2},{3,99},{99,3},{4,100},{1... | collective-permute-start | bytes 294920 | tf_op jit(solution)/shard_map/ppermute | solution.py:383

commit v4 on v3

--- a/solution.py
+++ b/solution.py
@@ -10,6 +10,7 @@
 LANES = 128
 PARTS = 4
 VMEM_LIMIT = 24 * 1024 * 1024
+FIRST_VMEM_LIMIT = 60 * 1024 * 1024
 
 
 def split_halves(values):
@@ -45,21 +46,47 @@
     )
 
 
-def edge_kernel(ocean_comp, comp_ref, row_ref, col_ref, west_ref, east_ref, to_west, to_east):
+def edge_kernel(
+    ocean_comp,
+    comp_ref,
+    row_hbm,
+    col_hbm,
+    state_hbm,
+    to_west,
+    to_east,
+    row_ref,
+    col_ref,
+    west_top,
+    east_top,
+    west_all,
+    east_all,
+    sems,
+):
     ocean = comp_ref[0] == ocean_comp
-    levels = west_ref.shape[1]
-    row_count = west_ref.shape[2]
+    levels = west_all.shape[1]
+    row_count = west_all.shape[2]
     part = row_ref.shape[-1] // PARTS
-    lane = lax.broadcasted_iota(jnp.int32, (row_count, LANES), 1)
-    sides = ((west_ref, to_west, 0, 0), (east_ref, to_east, 2, EAST_OFFSET))
-    for ref, out, shift, unused in sides:
-        tile = jnp.zeros((row_count, LANES), jnp.float32)
-        for k in range(2 * levels):
-            moved = pltpu.roll(ref[k // levels, k % levels], (2 * k + shift) % LANES, 1)
-            tile = jnp.where(lane // 2 == k, moved, tile)
-        for block in range(row_count // 8):
-            start = ocean_comp * part + LANES * block
-            out[:, start : start + LANES] = tile[8 * block : 8 * block + 8]
+    cols = state_hbm.shape[3]
+    near = slice(0, LANES)
+    far = slice(cols - LANES, cols)
+    copies = [
+        pltpu.make_async_copy(source, target, sems.at[i])
+        for i, (source, target) in enumerate(
+            (
+                (col_hbm, col_ref),
+                (row_hbm, row_ref),
+                (state_hbm.at[:, 0:1, :, near], west_top),
+                (state_hbm.at[:, 0:1, :, far], east_top),
+                (state_hbm.at[:, :, :, near], west_all),
+                (state_hbm.at[:, :, :, far], east_all),
+            )
+        )
+    ]
+    for copy in copies:
+        copy.start()
+    sides = ((west_top, to_west, 0, 0), (east_top, to_east, 2, EAST_OFFSET))
+    for copy in copies[:4]:
+        copy.wait()
 
     def lists(pairs):
         for ref, out, o, offset in sides:
@@ -86,7 +113,23 @@
     def _():
         lists([(0, ocean_comp)])
 
-
+    for copy in copies[4:]:
+        copy.wait()
+    lane = lax.broadcasted_iota(jnp.int32, (HALO_ROWS, LANES), 1)
+    for ref, out, shift in ((west_all, to_west, 0), (east_all, to_east, 2)):
+        tile = jnp.zeros((HALO_ROWS, LANES), jnp.float32)
+        for group in range(row_count // HALO_ROWS):
+            for k in range(2 * levels):
+                at = 2 * k + group * HALO_LANES
+                rows = ref[k // levels, k % levels, group * HALO_ROWS : (group + 1) * HALO_ROWS]
+                tile = jnp.where(lane // 2 == at // 2, pltpu.roll(rows, (at + shift) % LANES, 1), tile)
+        for block in range(HALO_ROWS // 8):
+            start = ocean_comp * part + LANES * block
+            out[:, start : start + LANES] = tile[8 * block : 8 * block + 8]
+
+
+HALO_ROWS = 16
+HALO_LANES = 32
 EAST_OFFSET = 384
 
 
@@ -173,9 +216,12 @@
             k = f * levels + level
             blocks = []
             for block in range(rows // 8):
-                start = pl.multiple_of(halo_start + (step * (rows // 8) + block) * LANES, LANES)
-                left = pltpu.roll(west_ref[:, pl.ds(start, LANES)], (LANES - 2 - 2 * k) % LANES, 1)
-                right = pltpu.roll(east_ref[:, pl.ds(start, LANES)], (LANES - 2 * k) % LANES, 1)
+                inner = 8 * block % HALO_ROWS // 8
+                start = halo_start + inner * LANES
+                group = step * (rows // HALO_ROWS) + 8 * block // HALO_ROWS
+                at = 2 * k + group * HALO_LANES
+                left = pltpu.roll(west_ref[:, start : start + LANES], (2 * LANES - 2 - at) % LANES, 1)
+                right = pltpu.roll(east_ref[:, start : start + LANES], (LANES - at) % LANES, 1)
                 blocks.append(jnp.where(halo_lane < LANES // 2, right, left))
             edges.append(jnp.concatenate(blocks, axis=0)[None])
         field = [state_ref[f, :, :, LANES * i : LANES * i + LANES] for i in range(tiles)]
@@ -272,7 +318,9 @@
 
     @pl.when(jnp.logical_not(ocean))
     def _():
-        land([(ocean_comp, got_0[...] + got_1[...] + got_2[...])])
+        comp = comp_ref[0]
+        mine = jnp.where(comp == 0, got_0[...], jnp.where(comp == 1, got_1[...], got_2[...]))
+        land([(ocean_comp, mine)])
 
     def far(f):
         centre = centre_ref[f * row_count : (f + 1) * row_count]
@@ -326,25 +374,25 @@
     counts = margin_count.reshape(3, ocean_comp + 1)
     scalar = pl.BlockSpec(memory_space=pltpu.SMEM)
     params = pltpu.CompilerParams(vmem_limit_bytes=VMEM_LIMIT)
-    strip = (fields, levels, row_count, LANES)
-    packet = jax.ShapeDtypeStruct((2 * PARTS, ocean_comp * part + LANES * row_count // 8), jnp.float32)
-    last = col_count // LANES - 1
+    packet = jax.ShapeDtypeStruct((2 * PARTS, ocean_comp * part + LANES * HALO_ROWS // 8), jnp.float32)
 
     to_west, to_east = pl.pallas_call(
         functools.partial(edge_kernel, ocean_comp),
-        grid=(1,),
-        in_specs=[
-            scalar,
-            whole(margin_row),
-            whole(margin_col),
-            pl.BlockSpec(strip, lambda i: (0, 0, 0, 0)),
-            pl.BlockSpec(strip, lambda i: (0, 0, 0, last)),
+        in_specs=[scalar] + [pl.BlockSpec(memory_space=pl.ANY)] * 3,
+        out_specs=[pl.BlockSpec(memory_space=pltpu.VMEM)] * 2,
+        out_shape=[packet] * 2,
+        scratch_shapes=[
+            pltpu.VMEM(margin_row.shape, jnp.int32),
+            pltpu.VMEM(margin_col.shape, jnp.int32),
+            pltpu.VMEM((fields, 1, row_count, LANES), jnp.float32),
+            pltpu.VMEM((fields, 1, row_count, LANES), jnp.float32),
+            pltpu.VMEM((fields, levels, row_count, LANES), jnp.float32),
+            pltpu.VMEM((fields, levels, row_count, LANES), jnp.float32),
+            pltpu.SemaphoreType.DMA((6,)),
         ],
-        out_specs=[whole(packet)] * 2,
-        out_shape=[packet] * 2,
-        compiler_params=params,
+        compiler_params=pltpu.CompilerParams(vmem_limit_bytes=FIRST_VMEM_LIMIT),
         name="edge_gather",
-    )(comp, margin_row, margin_col, state, state)
+    )(comp, margin_row, margin_col, state)
     forward = [(i, (i + 1) % tiles) for i in range(tiles)]
     backward = [(b, a) for a, b in forward]
     from_west = lax.ppermute(to_east, "tile", forward)
@@ -376,11 +424,8 @@
     )(comp, counts, centre, from_west, from_east)
     got = []
     for g in range(ocean_comp):
-        swap = []
-        for t in range(tiles):
-            swap.append((g * tiles + t, ocean_comp * tiles + t))
-            swap.append((ocean_comp * tiles + t, g * tiles + t))
-        got.append(lax.ppermute(bundles[g], ("comp", "tile"), swap))
+        swap = [(i, i ^ (g ^ ocean_comp)) for i in range(ocean_comp + 1)]
+        got.append(lax.ppermute(bundles[g], "comp", swap))
 
     chunk = 32
     moved = pl.pallas_call(

time: 39.4 us -> 33.7 us (0.86)
  starting transfers between devices: 13.7 us -> 9.74 us
  local copies, waits for them, and re-layouts: 3.5 us -> 0.05 us
  Pallas kernels: 21 us -> 23 us
    ppermute x3, starting transfers between devices: 5.89 us -> 1.9 us  [shards(): got.append(lax.ppermute(bundles[g], 'comp', swap))]
    unnamed x25 -> x19, local copies, waits for them, and re-layouts: 3.5 us -> 0.05 us
    pallas_call x1, Pallas kernels: 2.97 us -> 4.9 us  [shards(): pl.pallas_call(functools.partial(edge_kernel, ocean_comp), in_specs=[scal...]
  transfers between devices with their start and end apart: 5 -> 5, of which waited for: 0 -> 0; matrix products, arithmetic and copies ran while one was open for 0% -> 0% of each run, Pallas kernels for 20% -> 24%
where the time goes in v4:
time: 33.7 us; the launch traced here: 33.6 us
  Pallas kernels  23 us (68%)
  starting transfers between devices  9.74 us (29%)
  between operations  0.81 us (2%)
    pallas_call x1, Pallas kernels, shards(): pl.pallas_call(functools.partial(land_kernel, ocean_comp), grid=(1,), in_...  9.56 us
    ppermute x1, starting transfers between devices, shards(): from_east = lax.ppermute(to_west, 'tile', backward)  5.75 us
    pallas_call x1, Pallas kernels, shards(): pl.pallas_call(functools.partial(edge_kernel, ocean_comp), in_specs=[scal...  4.9 us
    pallas_call x1, Pallas kernels, shards(): pl.pallas_call(functools.partial(transport_kernel, ocean_comp * part), gr...  4.25 us
    pallas_call x1, Pallas kernels, shards(): pl.pallas_call(functools.partial(centre_kernel, ocean_comp), grid=(1,), i...  3.65 us
    ppermute x1, starting transfers between devices, shards(): from_west = lax.ppermute(to_east, 'tile', forward)  2.09 us
    ppermute x3, starting transfers between devices, shards(): got.append(lax.ppermute(bundles[g], 'comp', swap))  1.9 us
  transfers between devices with their start and end apart: 5, of which 0 were waited for; matrix products, arithmetic and copies ran while one was open for 0% of the time, Pallas kernels for 24%

profile of v4, /device:TPU:9, one launch (start us, length us, event | category | flops | bytes accessed | tf_op | source)
XLA Modules:
  0.0 33.6 jit_solution(12734801222798485045)
XLA Ops:
  0.6 0.0 copy-start.2
  0.6 0.0 copy-start.1
  0.7 0.0 copy-start
  0.7 0.0 copy-start.8
  0.7 0.0 copy-start.6
  0.7 0.0 copy-start.7
  0.7 4.9 %edge_gather.1 = (f32[8,3328]{1,0:T(8,128)}, f32[8,3328]{1,0:T(8,128)}) custom-call(s32[1]{0:T(128)} %bitcast.comp_ref, s32[1,1,3,4,4096]{4,3,2,1,0:T(4,128)} %row_ref.3, s32[1,1,3,4,4096]{4,3,2,1,0:T(4,128)} %col_ref.3, f32[2,8,64,512]{3,2,1,0:T(8,128)} %state_ref.3), custom_call_target="tpu_custom_call" | custom-call | tf_op jit(solution)/shard_map/edge_gather/pallas_call | solution.py:379
  5.6 2.1 %collective-permute-start = (f32[8,3328]{1,0:T(8,128)}, f32[8,3328]{1,0:T(8,128)S(1)}, u32[]{:S(2)}, u32[]{:S(2)}) collective-permute-start(f32[8,3328]{1,0:T(8,128)} %get-tuple-element.7), channel_id=1, source_target_pairs={{0,1},{1,2},{2,3},{3,4},{4,5},{5,6},{6,7},{7,8},{8,9},{9,10},{10,1... | collective-permute-start | bytes 319496 | tf_op jit(solution)/shard_map/ppermute | solution.py:398
  7.7 5.7 %collective-permute-start.1 = (f32[8,3328]{1,0:T(8,128)}, f32[8,3328]{1,0:T(8,128)S(1)}, u32[]{:S(2)}, u32[]{:S(2)}) collective-permute-start(f32[8,3328]{1,0:T(8,128)} %get-tuple-element.8), channel_id=1, source_target_pairs={{1,0},{2,1},{3,2},{4,3},{5,4},{6,5},{7,6},{8,7},{9,8},{10,9},{11,1... | collective-permute-start | bytes 319496 | tf_op jit(solution)/shard_map/ppermute | solution.py:399
  13.4 0.0 copy-done.2
  13.4 0.0 copy-done.1
  13.4 0.0 copy-done
  13.5 3.7 %centre_gather.1.centre_ref = f32[3,8,1024]{2,1,0:T(8,128)S(1)} custom-call(s32[1]{0:T(128)} %bitcast.comp_ref, s32[1,1,3,4,4096]{4,3,2,1,0:T(4,128)S(1)} %copy-done.1, s32[1,1,3,4,4096]{4,3,2,1,0:T(4,128)S(1)} %copy-done.2, f32[2,8,64,512]{3,2,1,0:T(8,128)S(1)} %copy-done), custom_call_target="tpu_custom_call" | custom-call | tf_op jit(solution)/shard_map/centre_gather/pallas_call | solution.py:402
  17.1 0.0 copy-done.8
  17.1 0.0 collective-permute-done.from_west.west_ref
  17.1 0.0 collective-permute-done.1.from_east.east_ref
  17.2 0.6 %pack.1 = (f32[3,8,1024]{2,1,0:T(8,128)S(1)}, f32[3,8,1024]{2,1,0:T(8,128)S(1)}, f32[3,8,1024]{2,1,0:T(8,128)S(1)}) custom-call(s32[1]{0:T(128)} %bitcast.comp_ref, s32[3,4]{1,0:T(4,128)S(1)} %bitcast.4, f32[3,8,1024]{2,1,0:T(8,128)S(1)} %centre_gather.1.centre_ref, f32[8,3328]{1,0:T(8,128)S(1)} %collective-permute-done.from_west.west_ref, ...), custom_call_target="tpu_custom_call" | custom-call | tf_op jit(solution)/shard_map/pack/pallas_call | solution.py:416
  17.8 0.1 collective-permute-start.3
  17.8 0.1 collective-permute-start.4
  17.9 0.0 copy-start.3
  17.9 0.0 copy-start.4
  18.0 0.0 copy-start.5
  18.0 1.7 %collective-permute-start.2 = (f32[3,8,1024]{2,1,0:T(8,128)S(1)}, f32[3,8,1024]{2,1,0:T(8,128)S(1)}, u32[]{:S(2)}, u32[]{:S(2)}) collective-permute-start(f32[3,8,1024]{2,1,0:T(8,128)S(1)} %get-tuple-element.9.unused_ref), channel_id=1, source_target_pairs={{0,96},{32,64},{64,32},{96,0},{1,97},{33,65},{65,33},{97,1},{2,98}... | collective-permute-start | bytes 294920 | tf_op jit(solution)/shard_map/ppermute | solution.py:428
  19.7 0.0 copy-done.6
  19.7 0.0 copy-done.7
  19.7 4.3 %transport.1.field_ref = f32[2,8,64,512]{3,2,1,0:T(8,128)} custom-call(f32[2,8,64,512]{3,2,1,0:T(8,128)S(1)} %copy-done, f32[8,64]{1,0:T(8,128)S(1)} %copy-done.6, f32[7,64]{1,0:T(8,128)S(1)} %copy-done.7, f32[8,3328]{1,0:T(8,128)S(1)} %collective-permute-done.from_west.west_ref, f32[8,3328]{1,0:T(8,128)S(1)} %collective-permute-done.1.from_east.east_ref, ...), custom_call_target="tpu_custom_call" | custom-call | tf_op jit(solution)/shard_map/transport/pallas_call | solution.py:431
  24.0 0.0 collective-permute-done.3.got_1
  24.0 0.0 collective-permute-done.4.got_2
  24.0 0.0 collective-permute-done.2.got_0
  24.0 0.0 copy-done.3
  24.0 0.0 copy-done.4
  24.0 9.6 %land.1 = (f32[2,8,64,512]{3,2,1,0:T(8,128)}, f32[2,64,512]{2,1,0:T(8,128)}) custom-call(s32[1]{0:T(128)} %bitcast.comp_ref, s32[3,4]{1,0:T(4,128)S(1)} %bitcast.5, s32[1,1,3,4,4096]{4,3,2,1,0:T(4,128)S(1)} %copy-done.1, s32[1,1,3,4,4096]{4,3,2,1,0:T(4,128)S(1)} %copy-done.2, f32[1,1,3,4,4096]{4,3,2,1,0:T(4,128)S(1)} %copy-done.3, ...), custom_call_target="tpu_custom_call", output_to_operand_aliasing={{0}: (8, {})} | custom-call | tf_op jit(solution)/shard_map/land/pallas_call | solution.py:454
  (2 shorter events, 0.0 us)
Async XLA Ops:
  0.6 12.8 %copy-start.2 = (s32[1,1,3,4,4096]{4,3,2,1,0:T(4,128)S(1)}, s32[1,1,3,4,4096]{4,3,2,1,0:T(4,128)}, u32[]{:S(2)}) copy-start(s32[1,1,3,4,4096]{4,3,2,1,0:T(4,128)} %col_ref.3) | copy-start | bytes 589828
  0.6 12.8 %copy-start.1 = (s32[1,1,3,4,4096]{4,3,2,1,0:T(4,128)S(1)}, s32[1,1,3,4,4096]{4,3,2,1,0:T(4,128)}, u32[]{:S(2)}) copy-start(s32[1,1,3,4,4096]{4,3,2,1,0:T(4,128)} %row_ref.3) | copy-start | bytes 589828
  0.7 12.8 %copy-start = (f32[2,8,64,512]{3,2,1,0:T(8,128)S(1)}, f32[2,8,64,512]{3,2,1,0:T(8,128)}, u32[]{:S(2)}) copy-start(f32[2,8,64,512]{3,2,1,0:T(8,128)} %state_ref.3) | copy-start | bytes 6291460
  0.7 16.4 %copy-start.8 = (s32[1,1,3,4]{3,1,2,0:T(1,128)S(1)}, s32[1,1,3,4]{3,1,2,0:T(1,128)}, u32[]{:S(2)}) copy-start(s32[1,1,3,4]{3,1,2,0:T(1,128)} %param.14) | copy-start | bytes 148
  0.7 19.0 %copy-start.6 = (f32[8,64]{1,0:T(8,128)S(1)}, f32[8,64]{1,0:T(8,128)}, u32[]{:S(2)}) copy-start(f32[8,64]{1,0:T(8,128)} %courant_ref.1) | copy-start | bytes 6148
  0.7 19.0 %copy-start.7 = (f32[7,64]{1,0:T(8,128)S(1)}, f32[7,64]{1,0:T(8,128)}, u32[]{:S(2)}) copy-start(f32[7,64]{1,0:T(8,128)} %mixing_ref.1) | copy-start | bytes 5380
  5.6 11.5 %collective-permute-start = (f32[8,3328]{1,0:T(8,128)}, f32[8,3328]{1,0:T(8,128)S(1)}, u32[]{:S(2)}, u32[]{:S(2)}) collective-permute-start(f32[8,3328]{1,0:T(8,128)} %get-tuple-element.7), channel_id=1, source_target_pairs={{0,1},{1,2},{2,3},{3,4},{4,5},{5,6},{6,7},{7,8},{8,9},{9,10},{10,1... | collective-permute-start | bytes 319496 | tf_op jit(solution)/shard_map/ppermute | solution.py:398
  7.7 9.4 %collective-permute-start.1 = (f32[8,3328]{1,0:T(8,128)}, f32[8,3328]{1,0:T(8,128)S(1)}, u32[]{:S(2)}, u32[]{:S(2)}) collective-permute-start(f32[8,3328]{1,0:T(8,128)} %get-tuple-element.8), channel_id=1, source_target_pairs={{1,0},{2,1},{3,2},{4,3},{5,4},{6,5},{7,6},{8,7},{9,8},{10,9},{11,1... | collective-permute-start | bytes 319496 | tf_op jit(solution)/shard_map/ppermute | solution.py:399
  17.8 6.2 %collective-permute-start.3 = (f32[3,8,1024]{2,1,0:T(8,128)S(1)}, f32[3,8,1024]{2,1,0:T(8,128)S(1)}, u32[]{:S(2)}, u32[]{:S(2)}) collective-permute-start(f32[3,8,1024]{2,1,0:T(8,128)S(1)} %get-tuple-element.10), channel_id=1, source_target_pairs={{0,64},{32,96},{64,0},{96,32},{1,65},{33,97},{65,1},{97,33},{2,66}... | collective-permute-start | bytes 294920 | tf_op jit(solution)/shard_map/ppermute | solution.py:428
  17.8 6.1 %collective-permute-start.4 = (f32[3,8,1024]{2,1,0:T(8,128)S(1)}, f32[3,8,1024]{2,1,0:T(8,128)S(1)}, u32[]{:S(2)}, u32[]{:S(2)}) collective-permute-start(f32[3,8,1024]{2,1,0:T(8,128)S(1)} %get-tuple-element.11), channel_id=1, source_target_pairs={{0,32},{32,0},{64,96},{96,64},{1,33},{33,1},{65,97},{97,65},{2,34}... | collective-permute-start | bytes 294920 | tf_op jit(solution)/shard_map/ppermute | solution.py:428
  17.9 6.0 %copy-start.3 = (f32[1,1,3,4,4096]{4,3,2,1,0:T(4,128)S(1)}, f32[1,1,3,4,4096]{4,3,2,1,0:T(4,128)}, u32[]{:S(2)}) copy-start(f32[1,1,3,4,4096]{4,3,2,1,0:T(4,128)} %weight_ref.1) | copy-start | bytes 589828
  17.9 6.0 %copy-start.4 = (f32[64,512]{1,0:T(8,128)S(1)}, f32[64,512]{1,0:T(8,128)}, u32[]{:S(2)}) copy-start(f32[64,512]{1,0:T(8,128)} %coef_ref.1) | copy-start | bytes 393220
  18.0 6.0 %copy-start.5 = (s32[64,512]{1,0:T(8,128)S(1)}, s32[64,512]{1,0:T(8,128)}, u32[]{:S(2)}) copy-start(s32[64,512]{1,0:T(8,128)} %mask_ref.1) | copy-start | bytes 393220
  18.0 6.0 %collective-permute-start.2 = (f32[3,8,1024]{2,1,0:T(8,128)S(1)}, f32[3,8,1024]{2,1,0:T(8,128)S(1)}, u32[]{:S(2)}, u32[]{:S(2)}) collective-permute-start(f32[3,8,1024]{2,1,0:T(8,128)S(1)} %get-tuple-element.9.unused_ref), channel_id=1, source_target_pairs={{0,96},{32,64},{64,32},{96,0},{1,97},{33,65},{65,33},{97,1},{2,98}... | collective-permute-start | bytes 294920 | tf_op jit(solution)/shard_map/ppermute | solution.py:428

commit v5 on v4

--- a/solution.py
+++ b/solution.py
@@ -30,6 +30,13 @@
         here = (iota + float(16 * block)).astype(jnp.bfloat16)
         blocks.append(jnp.where(number == here, jnp.bfloat16(1), jnp.bfloat16(0)))
     return jnp.concatenate(blocks, axis=0)
+
+
+def one_hot_masks(index_row, size):
+    n = index_row.shape[1]
+    number = jnp.broadcast_to(index_row.astype(jnp.float32), (16, n)).astype(jnp.bfloat16)
+    iota = lax.broadcasted_iota(jnp.int32, (16, n), 0).astype(jnp.float32)
+    return [number == (iota + float(16 * block)).astype(jnp.bfloat16) for block in range(size // 16)]
 
 
 def match_rows(total, rows):
@@ -258,19 +265,24 @@
     got_0,
     got_1,
     got_2,
-    field_ref,
+    field_hbm,
     coef_ref,
     mask_ref,
-    state_out,
-    partner_out,
+    state_hbm,
+    partner_hbm,
     centre_ref,
     west_ref,
     east_ref,
+    field_ref,
+    state_out,
+    partner_out,
+    sems,
 ):
+    fetch = pltpu.make_async_copy(field_hbm.at[:, 0:1], field_ref, sems.at[0])
+    fetch.start()
     ocean = comp_ref[0] == ocean_comp
     row_count, col_count = coef_ref.shape
     part = row_ref.shape[-1] // PARTS
-    half_rows = row_count // 2
     slot_iota = lax.broadcasted_iota(jnp.int32, (1, part), 1)
     nt = (((1,), (1,)), ((), ()))
 
@@ -286,24 +298,21 @@
                     weights = weight_ref[0, 0, o, h : h + 1, span]
                     live = slot_iota + q * part < count
                     if o == 1:
-                        row_table = one_hot(rows, row_count)
                         table = wide_one_hot(columns, col_count)
                     else:
-                        upper = rows >= half_rows
-                        row_table = one_hot(jnp.where(upper, rows - half_rows, rows), half_rows)
-                        offset = EAST_OFFSET if o == 2 else 0
-                        columns = columns - offset
-                        table = one_hot(jnp.where(upper, columns + LANES, columns), 2 * LANES)
-                    on = row_table > 0
+                        table = one_hot(columns - (EAST_OFFSET if o == 2 else 0), LANES)
+                    masks = one_hot_masks(rows, row_count)
                     pieces = []
                     for f in range(2):
                         value = got[o, q + f * PARTS : q + f * PARTS + 1]
-                        pieces.append(split_halves(jnp.where(live, weights * value, 0.0)))
+                        value = jnp.broadcast_to(jnp.where(live, weights * value, 0.0), (16, part))
+                        pieces.append(split_halves(value))
                     left = jnp.concatenate(
                         [
-                            jnp.where(on, jnp.broadcast_to(pieces[f][s], on.shape), jnp.bfloat16(0))
+                            jnp.where(mask, pieces[f][s], jnp.bfloat16(0))
                             for s in range(2)
                             for f in range(2)
+                            for mask in masks
                         ],
                         axis=0,
                     )
@@ -326,8 +335,7 @@
         centre = centre_ref[f * row_count : (f + 1) * row_count]
         sides = []
         for ref in (west_ref, east_ref):
-            rows = ref[f * half_rows : (f + 1) * half_rows]
-            sides.append(jnp.concatenate([rows[:, :LANES], rows[:, LANES:]], axis=0))
+            sides.append(ref[f * row_count : (f + 1) * row_count])
         return jnp.concatenate(
             [
                 centre[:, :LANES] + sides[0],
@@ -341,6 +349,9 @@
     second_far = far(1)
     partner_out[0] = first_far
     partner_out[1] = second_far
+    send_partner = pltpu.make_async_copy(partner_out, partner_hbm, sems.at[1])
+    send_partner.start()
+    fetch.wait()
     rate = coef_ref[...] * mask_ref[...].astype(jnp.float32)
     first_own = field_ref[0, 0]
     second_own = field_ref[1, 0]
@@ -348,6 +359,10 @@
     air_second = second_own + rate * (1.2 * first_far - 0.3 * second_far - second_own)
     sea_second = second_own + rate * (1.2 * first_own - second_far)
     state_out[1, 0] = jnp.where(ocean, sea_second, air_second)
+    send_state = pltpu.make_async_copy(state_out, state_hbm.at[:, 0:1], sems.at[2])
+    send_state.start()
+    send_partner.wait()
+    send_state.wait()
 
 
 def whole(array):
@@ -401,23 +416,16 @@
     bundle = jax.ShapeDtypeStruct((3, 2 * PARTS, part), jnp.float32)
     centre = pl.pallas_call(
         functools.partial(centre_kernel, ocean_comp),
-        grid=(1,),
-        in_specs=[
-            scalar,
-            whole(margin_row),
-            whole(margin_col),
-            pl.BlockSpec((fields, 1, row_count, col_count), lambda i: (0, 0, 0, 0)),
-        ],
-        out_specs=whole(bundle),
+        in_specs=[scalar] + [pl.BlockSpec(memory_space=pltpu.VMEM)] * 3,
+        out_specs=pl.BlockSpec(memory_space=pltpu.VMEM),
         out_shape=bundle,
         compiler_params=params,
         name="centre_gather",
     )(comp, margin_row, margin_col, state)
     bundles = pl.pallas_call(
         functools.partial(pack_kernel, ocean_comp),
-        grid=(1,),
-        in_specs=[scalar, scalar, whole(bundle), whole(packet), whole(packet)],
-        out_specs=[whole(bundle)] * ocean_comp,
+        in_specs=[scalar, scalar] + [pl.BlockSpec(memory_space=pltpu.VMEM)] * 3,
+        out_specs=[pl.BlockSpec(memory_space=pltpu.VMEM)] * ocean_comp,
         out_shape=[bundle] * ocean_comp,
         compiler_params=params,
         name="pack",
@@ -449,30 +457,23 @@
         name="transport",
     )(state, courant, mixing, from_west, from_east, bundles[0])
 
-    surface_spec = pl.BlockSpec((fields, 1, row_count, col_count), lambda i: (0, 0, 0, 0))
+    level = (fields, 1, row_count, col_count)
     partner = jax.ShapeDtypeStruct((fields, row_count, col_count), jnp.float32)
+    local = pl.BlockSpec(memory_space=pltpu.VMEM)
+    anywhere = pl.BlockSpec(memory_space=pl.ANY)
     return pl.pallas_call(
         functools.partial(land_kernel, ocean_comp),
-        grid=(1,),
-        in_specs=[
-            scalar,
-            scalar,
-            whole(margin_row),
-            whole(margin_col),
-            whole(margin_weight),
-            whole(bundle),
-            whole(bundle),
-            whole(bundle),
-            surface_spec,
-            whole(exchange_coef),
-            whole(sea_mask),
-        ],
-        out_specs=[surface_spec, whole(partner)],
+        in_specs=[scalar, scalar] + [local] * 6 + [anywhere, local, local],
+        out_specs=[anywhere, anywhere],
         out_shape=[jax.ShapeDtypeStruct(state.shape, jnp.float32), partner],
         scratch_shapes=[
             pltpu.VMEM((2 * row_count, col_count), jnp.float32),
-            pltpu.VMEM((row_count, 2 * LANES), jnp.float32),
-            pltpu.VMEM((row_count, 2 * LANES), jnp.float32),
+            pltpu.VMEM((2 * row_count, LANES), jnp.float32),
+            pltpu.VMEM((2 * row_count, LANES), jnp.float32),
+            pltpu.VMEM(level, jnp.float32),
+            pltpu.VMEM(level, jnp.float32),
+            pltpu.VMEM(partner.shape, jnp.float32),
+            pltpu.SemaphoreType.DMA((3,)),
         ],
         input_output_aliases={8: 0},
         compiler_params=params,

time: 33.7 us -> 32.5 us (0.964)
  Pallas kernels: 23 us -> 21.7 us
    pallas_call x3, Pallas kernels: 13.8 us -> 12.5 us  [the longest x1 8.27 us: shards(): pl.pallas_call(functools.partial(land_kernel, ocean_comp), in_specs=[scal...]
where the time goes in v5:
time: 32.5 us; the launch traced here: 32.4 us
  Pallas kernels  21.7 us (67%)
  starting transfers between devices  9.75 us (30%)
  between operations  0.95 us (3%)
    pallas_call x1, Pallas kernels, shards(): pl.pallas_call(functools.partial(land_kernel, ocean_comp), in_specs=[scal...  8.27 us
    ppermute x1, starting transfers between devices, shards(): from_east = lax.ppermute(to_west, 'tile', backward)  5.75 us
    pallas_call x1, Pallas kernels, shards(): pl.pallas_call(functools.partial(edge_kernel, ocean_comp), in_specs=[scal...  4.9 us
    pallas_call x1, Pallas kernels, shards(): pl.pallas_call(functools.partial(transport_kernel, ocean_comp * part), gr...  4.25 us
    pallas_call x1, Pallas kernels, shards(): pl.pallas_call(functools.partial(centre_kernel, ocean_comp), in_specs=[sc...  3.63 us
    ppermute x1, starting transfers between devices, shards(): from_west = lax.ppermute(to_east, 'tile', forward)  2.09 us
    ppermute x3, starting transfers between devices, shards(): got.append(lax.ppermute(bundles[g], 'comp', swap))  1.92 us
  transfers between devices with their start and end apart: 5, of which 0 were waited for; matrix products, arithmetic and copies ran while one was open for 0% of the time, Pallas kernels for 24%

profile of v5, /device:TPU:9, one launch (start us, length us, event | category | flops | bytes accessed | tf_op | source)
XLA Modules:
  0.0 32.4 jit_solution(3373413350950068778)
XLA Ops:
  0.6 0.0 copy-start.2
  0.6 0.0 copy-start.1
  0.7 0.0 copy-start
  0.7 0.0 copy-start.8
  0.7 0.0 copy-start.6
  0.7 0.0 copy-start.7
  0.7 4.9 %edge_gather.1 = (f32[8,3328]{1,0:T(8,128)}, f32[8,3328]{1,0:T(8,128)}) custom-call(s32[1]{0:T(128)} %bitcast.comp_ref, s32[1,1,3,4,4096]{4,3,2,1,0:T(4,128)} %row_ref.3, s32[1,1,3,4,4096]{4,3,2,1,0:T(4,128)} %col_ref.3, f32[2,8,64,512]{3,2,1,0:T(8,128)} %state_ref.3), custom_call_target="tpu_custom_call" | custom-call | tf_op jit(solution)/shard_map/edge_gather/pallas_call | solution.py:394
  5.6 2.1 %collective-permute-start = (f32[8,3328]{1,0:T(8,128)}, f32[8,3328]{1,0:T(8,128)S(1)}, u32[]{:S(2)}, u32[]{:S(2)}) collective-permute-start(f32[8,3328]{1,0:T(8,128)} %get-tuple-element.7), channel_id=1, source_target_pairs={{0,1},{1,2},{2,3},{3,4},{4,5},{5,6},{6,7},{7,8},{8,9},{9,10},{10,1... | collective-permute-start | bytes 319496 | tf_op jit(solution)/shard_map/ppermute | solution.py:413
  7.7 5.7 %collective-permute-start.1 = (f32[8,3328]{1,0:T(8,128)}, f32[8,3328]{1,0:T(8,128)S(1)}, u32[]{:S(2)}, u32[]{:S(2)}) collective-permute-start(f32[8,3328]{1,0:T(8,128)} %get-tuple-element.8), channel_id=1, source_target_pairs={{1,0},{2,1},{3,2},{4,3},{5,4},{6,5},{7,6},{8,7},{9,8},{10,9},{11,1... | collective-permute-start | bytes 319496 | tf_op jit(solution)/shard_map/ppermute | solution.py:414
  13.4 0.0 copy-done.2
  13.4 0.0 copy-done.1
  13.4 0.0 copy-done
  13.5 3.6 %centre_gather.1.centre_ref = f32[3,8,1024]{2,1,0:T(8,128)S(1)} custom-call(s32[1]{0:T(128)} %bitcast.comp_ref, s32[1,1,3,4,4096]{4,3,2,1,0:T(4,128)S(1)} %copy-done.1, s32[1,1,3,4,4096]{4,3,2,1,0:T(4,128)S(1)} %copy-done.2, f32[2,8,64,512]{3,2,1,0:T(8,128)S(1)} %copy-done), custom_call_target="tpu_custom_call" | custom-call | tf_op jit(solution)/shard_map/centre_gather/pallas_call | solution.py:417
  17.1 0.0 copy-done.8
  17.1 0.0 collective-permute-done.from_west.west_ref
  17.1 0.0 collective-permute-done.1.from_east.east_ref
  17.1 0.6 %pack.1 = (f32[3,8,1024]{2,1,0:T(8,128)S(1)}, f32[3,8,1024]{2,1,0:T(8,128)S(1)}, f32[3,8,1024]{2,1,0:T(8,128)S(1)}) custom-call(s32[1]{0:T(128)} %bitcast.comp_ref, s32[3,4]{1,0:T(4,128)S(1)} %bitcast.4, f32[3,8,1024]{2,1,0:T(8,128)S(1)} %centre_gather.1.centre_ref, f32[8,3328]{1,0:T(8,128)S(1)} %collective-permute-done.from_west.west_ref, ...), custom_call_target="tpu_custom_call" | custom-call | tf_op jit(solution)/shard_map/pack/pallas_call | solution.py:425
  17.7 0.1 collective-permute-start.3
  17.8 0.1 collective-permute-start.4
  17.9 0.0 copy-start.3
  17.9 0.0 copy-start.5
  18.0 1.7 %collective-permute-start.2 = (f32[3,8,1024]{2,1,0:T(8,128)S(1)}, f32[3,8,1024]{2,1,0:T(8,128)S(1)}, u32[]{:S(2)}, u32[]{:S(2)}) collective-permute-start(f32[3,8,1024]{2,1,0:T(8,128)S(1)} %get-tuple-element.9.unused_ref), channel_id=1, source_target_pairs={{0,96},{32,64},{64,32},{96,0},{1,97},{33,65},{65,33},{97,1},{2,98}... | collective-permute-start | bytes 294920 | tf_op jit(solution)/shard_map/ppermute | solution.py:436
  19.7 0.0 copy-done.6
  19.7 0.0 copy-done.7
  19.7 4.3 %transport.1.field_hbm = f32[2,8,64,512]{3,2,1,0:T(8,128)} custom-call(f32[2,8,64,512]{3,2,1,0:T(8,128)S(1)} %copy-done, f32[8,64]{1,0:T(8,128)S(1)} %copy-done.6, f32[7,64]{1,0:T(8,128)S(1)} %copy-done.7, f32[8,3328]{1,0:T(8,128)S(1)} %collective-permute-done.from_west.west_ref, f32[8,3328]{1,0:T(8,128)S(1)} %collective-permute-done.1.from_east.east_ref, ...), custom_call_target="tpu_custom_call" | custom-call | tf_op jit(solution)/shard_map/transport/pallas_call | solution.py:439
  23.9 0.0 collective-permute-done.3.got_1
  23.9 0.0 collective-permute-done.4.got_2
  23.9 0.0 collective-permute-done.2.got_0
  24.0 0.0 copy-done.3
  24.0 0.0 copy-done.4
  24.0 0.0 copy-done.5
  24.0 8.3 %land.1 = (f32[2,8,64,512]{3,2,1,0:T(8,128)}, f32[2,64,512]{2,1,0:T(8,128)}) custom-call(s32[1]{0:T(128)} %bitcast.comp_ref, s32[3,4]{1,0:T(4,128)S(1)} %bitcast.5, s32[1,1,3,4,4096]{4,3,2,1,0:T(4,128)S(1)} %copy-done.1, s32[1,1,3,4,4096]{4,3,2,1,0:T(4,128)S(1)} %copy-done.2, f32[1,1,3,4,4096]{4,3,2,1,0:T(4,128)S(1)} %copy-done.3, ...), custom_call_target="tpu_custom_call", output_to_operand_aliasing={{0}: (8, {})} | custom-call | tf_op jit(solution)/shard_map/land/pallas_call | solution.py:464
  (2 shorter events, 0.0 us)
Async XLA Ops:
  0.6 12.8 %copy-start.2 = (s32[1,1,3,4,4096]{4,3,2,1,0:T(4,128)S(1)}, s32[1,1,3,4,4096]{4,3,2,1,0:T(4,128)}, u32[]{:S(2)}) copy-start(s32[1,1,3,4,4096]{4,3,2,1,0:T(4,128)} %col_ref.3) | copy-start | bytes 589828
  0.6 12.8 %copy-start.1 = (s32[1,1,3,4,4096]{4,3,2,1,0:T(4,128)S(1)}, s32[1,1,3,4,4096]{4,3,2,1,0:T(4,128)}, u32[]{:S(2)}) copy-start(s32[1,1,3,4,4096]{4,3,2,1,0:T(4,128)} %row_ref.3) | copy-start | bytes 589828
  0.7 12.8 %copy-start = (f32[2,8,64,512]{3,2,1,0:T(8,128)S(1)}, f32[2,8,64,512]{3,2,1,0:T(8,128)}, u32[]{:S(2)}) copy-start(f32[2,8,64,512]{3,2,1,0:T(8,128)} %state_ref.3) | copy-start | bytes 6291460
  0.7 16.4 %copy-start.8 = (s32[1,1,3,4]{3,1,2,0:T(1,128)S(1)}, s32[1,1,3,4]{3,1,2,0:T(1,128)}, u32[]{:S(2)}) copy-start(s32[1,1,3,4]{3,1,2,0:T(1,128)} %param.14) | copy-start | bytes 148
  0.7 19.0 %copy-start.6 = (f32[8,64]{1,0:T(8,128)S(1)}, f32[8,64]{1,0:T(8,128)}, u32[]{:S(2)}) copy-start(f32[8,64]{1,0:T(8,128)} %courant_ref.1) | copy-start | bytes 6148
  0.7 19.0 %copy-start.7 = (f32[7,64]{1,0:T(8,128)S(1)}, f32[7,64]{1,0:T(8,128)}, u32[]{:S(2)}) copy-start(f32[7,64]{1,0:T(8,128)} %mixing_ref.1) | copy-start | bytes 5380
  5.6 11.5 %collective-permute-start = (f32[8,3328]{1,0:T(8,128)}, f32[8,3328]{1,0:T(8,128)S(1)}, u32[]{:S(2)}, u32[]{:S(2)}) collective-permute-start(f32[8,3328]{1,0:T(8,128)} %get-tuple-element.7), channel_id=1, source_target_pairs={{0,1},{1,2},{2,3},{3,4},{4,5},{5,6},{6,7},{7,8},{8,9},{9,10},{10,1... | collective-permute-start | bytes 319496 | tf_op jit(solution)/shard_map/ppermute | solution.py:413
  7.7 9.4 %collective-permute-start.1 = (f32[8,3328]{1,0:T(8,128)}, f32[8,3328]{1,0:T(8,128)S(1)}, u32[]{:S(2)}, u32[]{:S(2)}) collective-permute-start(f32[8,3328]{1,0:T(8,128)} %get-tuple-element.8), channel_id=1, source_target_pairs={{1,0},{2,1},{3,2},{4,3},{5,4},{6,5},{7,6},{8,7},{9,8},{10,9},{11,1... | collective-permute-start | bytes 319496 | tf_op jit(solution)/shard_map/ppermute | solution.py:414
  17.7 6.2 %collective-permute-start.3 = (f32[3,8,1024]{2,1,0:T(8,128)S(1)}, f32[3,8,1024]{2,1,0:T(8,128)S(1)}, u32[]{:S(2)}, u32[]{:S(2)}) collective-permute-start(f32[3,8,1024]{2,1,0:T(8,128)S(1)} %get-tuple-element.10), channel_id=1, source_target_pairs={{0,64},{32,96},{64,0},{96,32},{1,65},{33,97},{65,1},{97,33},{2,66}... | collective-permute-start | bytes 294920 | tf_op jit(solution)/shard_map/ppermute | solution.py:436
  17.8 6.1 %collective-permute-start.4 = (f32[3,8,1024]{2,1,0:T(8,128)S(1)}, f32[3,8,1024]{2,1,0:T(8,128)S(1)}, u32[]{:S(2)}, u32[]{:S(2)}) collective-permute-start(f32[3,8,1024]{2,1,0:T(8,128)S(1)} %get-tuple-element.11), channel_id=1, source_target_pairs={{0,32},{32,0},{64,96},{96,64},{1,33},{33,1},{65,97},{97,65},{2,34}... | collective-permute-start | bytes 294920 | tf_op jit(solution)/shard_map/ppermute | solution.py:436
  17.9 6.0 %copy-start.3 = (f32[1,1,3,4,4096]{4,3,2,1,0:T(4,128)S(1)}, f32[1,1,3,4,4096]{4,3,2,1,0:T(4,128)}, u32[]{:S(2)}) copy-start(f32[1,1,3,4,4096]{4,3,2,1,0:T(4,128)} %weight_ref.1) | copy-start | bytes 589828
  17.9 6.0 %copy-start.4 = (f32[64,512]{1,0:T(8,128)S(1)}, f32[64,512]{1,0:T(8,128)}, u32[]{:S(2)}) copy-start(f32[64,512]{1,0:T(8,128)} %coef_ref.1) | copy-start | bytes 393220
  17.9 6.0 %copy-start.5 = (s32[64,512]{1,0:T(8,128)S(1)}, s32[64,512]{1,0:T(8,128)}, u32[]{:S(2)}) copy-start(s32[64,512]{1,0:T(8,128)} %mask_ref.1) | copy-start | bytes 393220
  18.0 6.0 %collective-permute-start.2 = (f32[3,8,1024]{2,1,0:T(8,128)S(1)}, f32[3,8,1024]{2,1,0:T(8,128)S(1)}, u32[]{:S(2)}, u32[]{:S(2)}) collective-permute-start(f32[3,8,1024]{2,1,0:T(8,128)S(1)} %get-tuple-element.9.unused_ref), channel_id=1, source_target_pairs={{0,96},{32,64},{64,32},{96,0},{1,97},{33,65},{65,33},{97,1},{2,98}... | collective-permute-start | bytes 294920 | tf_op jit(solution)/shard_map/ppermute | solution.py:436

commit v6 on v5

--- a/solution.py
+++ b/solution.py
@@ -188,20 +188,15 @@
 
 
 def transport_kernel(
-    halo_start, state_ref, courant_ref, mixing_ref, west_ref, east_ref, unused_ref, out_ref, courant_by_row, mixing_by_row
+    halo_start, state_ref, courant_ref, mixing_ref, west_ref, east_ref, unused_ref, out_hbm, out_ref, sems
 ):
     fields, levels, rows, cols = state_ref.shape
-    step = pl.program_id(0)
     tiles = cols // LANES
-
-    @pl.when(step == 0)
-    def _():
-        courant_by_row[...] = courant_ref[...].T
-        mixing_by_row[...] = mixing_ref[...].T
-
-    def spread(ref, level):
-        here = pl.ds(pl.multiple_of(step * rows, 8), rows)
-        return jnp.broadcast_to(ref[here, level : level + 1], (rows, LANES))[None]
+    courant_by_row = courant_ref[...].T
+    mixing_by_row = mixing_ref[...].T
+
+    def spread(table, level):
+        return jnp.broadcast_to(table[:, level : level + 1], (rows, LANES))[None]
 
     source = lax.broadcasted_iota(jnp.int32, (2 * LANES, 2 * LANES), 0) % LANES
     target = lax.broadcasted_iota(jnp.int32, (2 * LANES, 2 * LANES), 1)
@@ -217,6 +212,7 @@
     square = half * speed
     middle, ahead, behind = 1.0 - 2.0 * square, square - half, square + half
     mix = jnp.concatenate([spread(mixing_by_row, level) for level in range(levels - 1)], axis=0)
+    copies = []
     for f in range(fields):
         edges = []
         for level in range(levels):
@@ -225,7 +221,7 @@
             for block in range(rows // 8):
                 inner = 8 * block % HALO_ROWS // 8
                 start = halo_start + inner * LANES
-                group = step * (rows // HALO_ROWS) + 8 * block // HALO_ROWS
+                group = 8 * block // HALO_ROWS
                 at = 2 * k + group * HALO_LANES
                 left = pltpu.roll(west_ref[:, start : start + LANES], (2 * LANES - 2 - at) % LANES, 1)
                 right = pltpu.roll(east_ref[:, start : start + LANES], (LANES - at) % LANES, 1)
@@ -253,6 +249,10 @@
             field = after
         for i in range(tiles):
             out_ref[f, :, :, LANES * i : LANES * i + LANES] = field[i]
+        copies.append(pltpu.make_async_copy(out_ref.at[f : f + 1], out_hbm.at[f : f + 1], sems.at[f]))
+        copies[f].start()
+    for copy in copies:
+        copy.wait()
 
 
 def land_kernel(
@@ -435,24 +435,12 @@
         swap = [(i, i ^ (g ^ ocean_comp)) for i in range(ocean_comp + 1)]
         got.append(lax.ppermute(bundles[g], "comp", swap))
 
-    chunk = 32
     moved = pl.pallas_call(
         functools.partial(transport_kernel, ocean_comp * part),
-        grid=(row_count // chunk,),
-        in_specs=[
-            pl.BlockSpec((fields, levels, chunk, col_count), lambda i: (0, 0, i, 0)),
-            whole(courant),
-            whole(mixing),
-            whole(packet),
-            whole(packet),
-            pl.BlockSpec(memory_space=pl.ANY),
-        ],
-        out_specs=pl.BlockSpec((fields, levels, chunk, col_count), lambda i: (0, 0, i, 0)),
+        in_specs=[pl.BlockSpec(memory_space=pltpu.VMEM)] * 5 + [pl.BlockSpec(memory_space=pl.ANY)],
+        out_specs=pl.BlockSpec(memory_space=pl.ANY),
         out_shape=jax.ShapeDtypeStruct(state.shape, jnp.float32),
-        scratch_shapes=[
-            pltpu.VMEM((row_count, levels), jnp.float32),
-            pltpu.VMEM((row_count, levels - 1), jnp.float32),
-        ],
+        scratch_shapes=[pltpu.VMEM(state.shape, jnp.float32), pltpu.SemaphoreType.DMA((fields,))],
         compiler_params=params,
         name="transport",
     )(state, courant, mixing, from_west, from_east, bundles[0])

time: 32.5 us -> 32 us (0.985)
  Pallas kernels: 21.7 us -> 21.1 us
    pallas_call x1, Pallas kernels: 4.25 us -> 3.88 us  [shards(): pl.pallas_call(functools.partial(transport_kernel, ocean_comp * part), in...]
where the time goes in v6:
time: 32 us; the launch traced here: 31.9 us
  Pallas kernels  21.1 us (66%)
  starting transfers between devices  9.75 us (30%)
  between operations  0.98 us (3%)
    pallas_call x1, Pallas kernels, shards(): pl.pallas_call(functools.partial(land_kernel, ocean_comp), in_specs=[scal...  8.09 us
    ppermute x1, starting transfers between devices, shards(): from_east = lax.ppermute(to_west, 'tile', backward)  5.75 us
    pallas_call x1, Pallas kernels, shards(): pl.pallas_call(functools.partial(edge_kernel, ocean_comp), in_specs=[scal...  4.9 us
    pallas_call x1, Pallas kernels, shards(): pl.pallas_call(functools.partial(transport_kernel, ocean_comp * part), in...  3.88 us
    pallas_call x1, Pallas kernels, shards(): pl.pallas_call(functools.partial(centre_kernel, ocean_comp), in_specs=[sc...  3.63 us
    ppermute x1, starting transfers between devices, shards(): from_west = lax.ppermute(to_east, 'tile', forward)  2.09 us
    ppermute x3, starting transfers between devices, shards(): got.append(lax.ppermute(bundles[g], 'comp', swap))  1.92 us
  transfers between devices with their start and end apart: 5, of which 0 were waited for; matrix products, arithmetic and copies ran while one was open for 0% of the time, Pallas kernels for 24%

profile of v6, /device:TPU:9, one launch (start us, length us, event | category | flops | bytes accessed | tf_op | source)
XLA Modules:
  0.0 31.9 jit_solution(6045206587473885754)
XLA Ops:
  0.6 0.0 copy-start.2
  0.6 0.0 copy-start.1
  0.7 0.0 copy-start
  0.7 0.0 copy-start.8
  0.7 0.0 copy-start.6
  0.7 0.0 copy-start.7
  0.7 4.9 %edge_gather.1 = (f32[8,3328]{1,0:T(8,128)}, f32[8,3328]{1,0:T(8,128)}) custom-call(s32[1]{0:T(128)} %bitcast.comp_ref, s32[1,1,3,4,4096]{4,3,2,1,0:T(4,128)} %row_ref.3, s32[1,1,3,4,4096]{4,3,2,1,0:T(4,128)} %col_ref.3, f32[2,8,64,512]{3,2,1,0:T(8,128)} %state_ref.3), custom_call_target="tpu_custom_call" | custom-call | tf_op jit(solution)/shard_map/edge_gather/pallas_call | solution.py:394
  5.6 2.1 %collective-permute-start = (f32[8,3328]{1,0:T(8,128)}, f32[8,3328]{1,0:T(8,128)S(1)}, u32[]{:S(2)}, u32[]{:S(2)}) collective-permute-start(f32[8,3328]{1,0:T(8,128)} %get-tuple-element.7), channel_id=1, source_target_pairs={{0,1},{1,2},{2,3},{3,4},{4,5},{5,6},{6,7},{7,8},{8,9},{9,10},{10,1... | collective-permute-start | bytes 319496 | tf_op jit(solution)/shard_map/ppermute | solution.py:413
  7.7 5.7 %collective-permute-start.1 = (f32[8,3328]{1,0:T(8,128)}, f32[8,3328]{1,0:T(8,128)S(1)}, u32[]{:S(2)}, u32[]{:S(2)}) collective-permute-start(f32[8,3328]{1,0:T(8,128)} %get-tuple-element.8), channel_id=1, source_target_pairs={{1,0},{2,1},{3,2},{4,3},{5,4},{6,5},{7,6},{8,7},{9,8},{10,9},{11,1... | collective-permute-start | bytes 319496 | tf_op jit(solution)/shard_map/ppermute | solution.py:414
  13.4 0.0 copy-done.2
  13.4 0.0 copy-done.1
  13.4 0.0 copy-done
  13.5 3.6 %centre_gather.1.centre_ref = f32[3,8,1024]{2,1,0:T(8,128)S(1)} custom-call(s32[1]{0:T(128)} %bitcast.comp_ref, s32[1,1,3,4,4096]{4,3,2,1,0:T(4,128)S(1)} %copy-done.1, s32[1,1,3,4,4096]{4,3,2,1,0:T(4,128)S(1)} %copy-done.2, f32[2,8,64,512]{3,2,1,0:T(8,128)S(1)} %copy-done), custom_call_target="tpu_custom_call" | custom-call | tf_op jit(solution)/shard_map/centre_gather/pallas_call | solution.py:417
  17.1 0.0 copy-done.8
  17.1 0.0 collective-permute-done.from_west.west_ref
  17.1 0.0 collective-permute-done.1.from_east.east_ref
  17.1 0.6 %pack.1 = (f32[3,8,1024]{2,1,0:T(8,128)S(1)}, f32[3,8,1024]{2,1,0:T(8,128)S(1)}, f32[3,8,1024]{2,1,0:T(8,128)S(1)}) custom-call(s32[1]{0:T(128)} %bitcast.comp_ref, s32[3,4]{1,0:T(4,128)S(1)} %bitcast.4, f32[3,8,1024]{2,1,0:T(8,128)S(1)} %centre_gather.1.centre_ref, f32[8,3328]{1,0:T(8,128)S(1)} %collective-permute-done.from_west.west_ref, ...), custom_call_target="tpu_custom_call" | custom-call | tf_op jit(solution)/shard_map/pack/pallas_call | solution.py:425
  17.7 0.1 collective-permute-start.3
  17.8 0.1 collective-permute-start.4
  17.9 0.0 copy-start.3
  17.9 0.0 copy-start.5
  18.0 1.7 %collective-permute-start.2 = (f32[3,8,1024]{2,1,0:T(8,128)S(1)}, f32[3,8,1024]{2,1,0:T(8,128)S(1)}, u32[]{:S(2)}, u32[]{:S(2)}) collective-permute-start(f32[3,8,1024]{2,1,0:T(8,128)S(1)} %get-tuple-element.9.unused_ref), channel_id=1, source_target_pairs={{0,96},{32,64},{64,32},{96,0},{1,97},{33,65},{65,33},{97,1},{2,98}... | collective-permute-start | bytes 294920 | tf_op jit(solution)/shard_map/ppermute | solution.py:436
  19.7 0.0 copy-done.6
  19.7 0.0 copy-done.7
  19.7 3.9 %transport.1.field_hbm = f32[2,8,64,512]{3,2,1,0:T(8,128)} custom-call(f32[2,8,64,512]{3,2,1,0:T(8,128)S(1)} %copy-done, f32[8,64]{1,0:T(8,128)S(1)} %copy-done.6, f32[7,64]{1,0:T(8,128)S(1)} %copy-done.7, f32[8,3328]{1,0:T(8,128)S(1)} %collective-permute-done.from_west.west_ref, f32[8,3328]{1,0:T(8,128)S(1)} %collective-permute-done.1.from_east.east_ref, ...), custom_call_target="tpu_custom_call" | custom-call | tf_op jit(solution)/shard_map/transport/pallas_call | solution.py:438
  23.6 0.0 collective-permute-done.3.got_1
  23.6 0.0 collective-permute-done.4.got_2
  23.6 0.0 collective-permute-done.2.got_0
  23.6 0.0 copy-done.3
  23.6 0.0 copy-done.4
  23.6 0.0 copy-done.5
  23.6 8.1 %land.1 = (f32[2,8,64,512]{3,2,1,0:T(8,128)}, f32[2,64,512]{2,1,0:T(8,128)}) custom-call(s32[1]{0:T(128)} %bitcast.comp_ref, s32[3,4]{1,0:T(4,128)S(1)} %bitcast.5, s32[1,1,3,4,4096]{4,3,2,1,0:T(4,128)S(1)} %copy-done.1, s32[1,1,3,4,4096]{4,3,2,1,0:T(4,128)S(1)} %copy-done.2, f32[1,1,3,4,4096]{4,3,2,1,0:T(4,128)S(1)} %copy-done.3, ...), custom_call_target="tpu_custom_call", output_to_operand_aliasing={{0}: (8, {})} | custom-call | tf_op jit(solution)/shard_map/land/pallas_call | solution.py:452
  (2 shorter events, 0.0 us)
Async XLA Ops:
  0.6 12.8 %copy-start.2 = (s32[1,1,3,4,4096]{4,3,2,1,0:T(4,128)S(1)}, s32[1,1,3,4,4096]{4,3,2,1,0:T(4,128)}, u32[]{:S(2)}) copy-start(s32[1,1,3,4,4096]{4,3,2,1,0:T(4,128)} %col_ref.3) | copy-start | bytes 589828
  0.6 12.8 %copy-start.1 = (s32[1,1,3,4,4096]{4,3,2,1,0:T(4,128)S(1)}, s32[1,1,3,4,4096]{4,3,2,1,0:T(4,128)}, u32[]{:S(2)}) copy-start(s32[1,1,3,4,4096]{4,3,2,1,0:T(4,128)} %row_ref.3) | copy-start | bytes 589828
  0.7 12.8 %copy-start = (f32[2,8,64,512]{3,2,1,0:T(8,128)S(1)}, f32[2,8,64,512]{3,2,1,0:T(8,128)}, u32[]{:S(2)}) copy-start(f32[2,8,64,512]{3,2,1,0:T(8,128)} %state_ref.3) | copy-start | bytes 6291460
  0.7 16.4 %copy-start.8 = (s32[1,1,3,4]{3,1,2,0:T(1,128)S(1)}, s32[1,1,3,4]{3,1,2,0:T(1,128)}, u32[]{:S(2)}) copy-start(s32[1,1,3,4]{3,1,2,0:T(1,128)} %param.14) | copy-start | bytes 148
  0.7 19.0 %copy-start.6 = (f32[8,64]{1,0:T(8,128)S(1)}, f32[8,64]{1,0:T(8,128)}, u32[]{:S(2)}) copy-start(f32[8,64]{1,0:T(8,128)} %courant_ref.1) | copy-start | bytes 6148
  0.7 19.0 %copy-start.7 = (f32[7,64]{1,0:T(8,128)S(1)}, f32[7,64]{1,0:T(8,128)}, u32[]{:S(2)}) copy-start(f32[7,64]{1,0:T(8,128)} %mixing_ref.1) | copy-start | bytes 5380
  5.6 11.5 %collective-permute-start = (f32[8,3328]{1,0:T(8,128)}, f32[8,3328]{1,0:T(8,128)S(1)}, u32[]{:S(2)}, u32[]{:S(2)}) collective-permute-start(f32[8,3328]{1,0:T(8,128)} %get-tuple-element.7), channel_id=1, source_target_pairs={{0,1},{1,2},{2,3},{3,4},{4,5},{5,6},{6,7},{7,8},{8,9},{9,10},{10,1... | collective-permute-start | bytes 319496 | tf_op jit(solution)/shard_map/ppermute | solution.py:413
  7.7 9.4 %collective-permute-start.1 = (f32[8,3328]{1,0:T(8,128)}, f32[8,3328]{1,0:T(8,128)S(1)}, u32[]{:S(2)}, u32[]{:S(2)}) collective-permute-start(f32[8,3328]{1,0:T(8,128)} %get-tuple-element.8), channel_id=1, source_target_pairs={{1,0},{2,1},{3,2},{4,3},{5,4},{6,5},{7,6},{8,7},{9,8},{10,9},{11,1... | collective-permute-start | bytes 319496 | tf_op jit(solution)/shard_map/ppermute | solution.py:414
  17.7 5.8 %collective-permute-start.3 = (f32[3,8,1024]{2,1,0:T(8,128)S(1)}, f32[3,8,1024]{2,1,0:T(8,128)S(1)}, u32[]{:S(2)}, u32[]{:S(2)}) collective-permute-start(f32[3,8,1024]{2,1,0:T(8,128)S(1)} %get-tuple-element.10), channel_id=1, source_target_pairs={{0,64},{32,96},{64,0},{96,32},{1,65},{33,97},{65,1},{97,33},{2,66}... | collective-permute-start | bytes 294920 | tf_op jit(solution)/shard_map/ppermute | solution.py:436
  17.8 5.8 %collective-permute-start.4 = (f32[3,8,1024]{2,1,0:T(8,128)S(1)}, f32[3,8,1024]{2,1,0:T(8,128)S(1)}, u32[]{:S(2)}, u32[]{:S(2)}) collective-permute-start(f32[3,8,1024]{2,1,0:T(8,128)S(1)} %get-tuple-element.11), channel_id=1, source_target_pairs={{0,32},{32,0},{64,96},{96,64},{1,33},{33,1},{65,97},{97,65},{2,34}... | collective-permute-start | bytes 294920 | tf_op jit(solution)/shard_map/ppermute | solution.py:436
  17.9 5.7 %copy-start.3 = (f32[1,1,3,4,4096]{4,3,2,1,0:T(4,128)S(1)}, f32[1,1,3,4,4096]{4,3,2,1,0:T(4,128)}, u32[]{:S(2)}) copy-start(f32[1,1,3,4,4096]{4,3,2,1,0:T(4,128)} %weight_ref.1) | copy-start | bytes 589828
  17.9 5.7 %copy-start.4 = (f32[64,512]{1,0:T(8,128)S(1)}, f32[64,512]{1,0:T(8,128)}, u32[]{:S(2)}) copy-start(f32[64,512]{1,0:T(8,128)} %coef_ref.1) | copy-start | bytes 393220
  17.9 5.7 %copy-start.5 = (s32[64,512]{1,0:T(8,128)S(1)}, s32[64,512]{1,0:T(8,128)}, u32[]{:S(2)}) copy-start(s32[64,512]{1,0:T(8,128)} %mask_ref.1) | copy-start | bytes 393220
  18.0 5.6 %collective-permute-start.2 = (f32[3,8,1024]{2,1,0:T(8,128)S(1)}, f32[3,8,1024]{2,1,0:T(8,128)S(1)}, u32[]{:S(2)}, u32[]{:S(2)}) collective-permute-start(f32[3,8,1024]{2,1,0:T(8,128)S(1)} %get-tuple-element.9.unused_ref), channel_id=1, source_target_pairs={{0,96},{32,64},{64,32},{96,0},{1,97},{33,65},{65,33},{97,1},{2,98}... | collective-permute-start | bytes 294920 | tf_op jit(solution)/shard_map/ppermute | solution.py:436

commit v7 on v6

--- a/solution.py
+++ b/solution.py
@@ -80,9 +80,11 @@
         pltpu.make_async_copy(source, target, sems.at[i])
         for i, (source, target) in enumerate(
             (
-                (col_hbm, col_ref),
-                (row_hbm, row_ref),
+                (col_hbm.at[:, :, 0:1], col_ref.at[:, :, 0:1]),
+                (row_hbm.at[:, :, 0:1], row_ref.at[:, :, 0:1]),
                 (state_hbm.at[:, 0:1, :, near], west_top),
+                (col_hbm.at[:, :, 2:3], col_ref.at[:, :, 2:3]),
+                (row_hbm.at[:, :, 2:3], row_ref.at[:, :, 2:3]),
                 (state_hbm.at[:, 0:1, :, far], east_top),
                 (state_hbm.at[:, :, :, near], west_all),
                 (state_hbm.at[:, :, :, far], east_all),
@@ -92,11 +94,14 @@
     for copy in copies:
         copy.start()
     sides = ((west_top, to_west, 0, 0), (east_top, to_east, 2, EAST_OFFSET))
-    for copy in copies[:4]:
+    for copy in copies[:3]:
         copy.wait()
 
     def lists(pairs):
         for ref, out, o, offset in sides:
+            if o == 2:
+                for copy in copies[3:6]:
+                    copy.wait()
             high, low = split_halves(ref[:, 0].reshape(2 * row_count, LANES))
             surface = jnp.concatenate([high, low], axis=1)
             for slot, h in pairs:
@@ -120,7 +125,7 @@
     def _():
         lists([(0, ocean_comp)])
 
-    for copy in copies[4:]:
+    for copy in copies[6:]:
         copy.wait()
     lane = lax.broadcasted_iota(jnp.int32, (HALO_ROWS, LANES), 1)
     for ref, out, shift in ((west_all, to_west, 0), (east_all, to_east, 2)):
@@ -403,7 +408,7 @@
             pltpu.VMEM((fields, 1, row_count, LANES), jnp.float32),
             pltpu.VMEM((fields, levels, row_count, LANES), jnp.float32),
             pltpu.VMEM((fields, levels, row_count, LANES), jnp.float32),
-            pltpu.SemaphoreType.DMA((6,)),
+            pltpu.SemaphoreType.DMA((8,)),
         ],
         compiler_params=pltpu.CompilerParams(vmem_limit_bytes=FIRST_VMEM_LIMIT),
         name="edge_gather",

time: 32 us -> 32 us (level)
  no operation moved by 1% of the time
where the time goes in v7:
time: 32 us; the launch traced here: 31.9 us
  Pallas kernels  21.1 us (66%)
  starting transfers between devices  9.76 us (30%)
  between operations  0.97 us (3%)
    pallas_call x1, Pallas kernels, shards(): pl.pallas_call(functools.partial(land_kernel, ocean_comp), in_specs=[scal...  8.09 us
    ppermute x1, starting transfers between devices, shards(): from_east = lax.ppermute(to_west, 'tile', backward)  5.75 us
    pallas_call x1, Pallas kernels, shards(): pl.pallas_call(functools.partial(edge_kernel, ocean_comp), in_specs=[scal...  4.88 us
    pallas_call x1, Pallas kernels, shards(): pl.pallas_call(functools.partial(transport_kernel, ocean_comp * part), in...  3.88 us
    pallas_call x1, Pallas kernels, shards(): pl.pallas_call(functools.partial(centre_kernel, ocean_comp), in_specs=[sc...  3.63 us
    ppermute x1, starting transfers between devices, shards(): from_west = lax.ppermute(to_east, 'tile', forward)  2.09 us
    ppermute x3, starting transfers between devices, shards(): got.append(lax.ppermute(bundles[g], 'comp', swap))  1.93 us
  transfers between devices with their start and end apart: 5, of which 0 were waited for; matrix products, arithmetic and copies ran while one was open for 0% of the time, Pallas kernels for 24%

profile of v7, /device:TPU:9, one launch (start us, length us, event | category | flops | bytes accessed | tf_op | source)
XLA Modules:
  0.0 31.9 jit_solution(5439548817502944875)
XLA Ops:
  0.6 0.0 copy-start.2
  0.6 0.0 copy-start.1
  0.7 0.0 copy-start
  0.7 0.0 copy-start.8
  0.7 0.0 copy-start.6
  0.7 0.0 copy-start.7
  0.7 4.9 %edge_gather.1 = (f32[8,3328]{1,0:T(8,128)}, f32[8,3328]{1,0:T(8,128)}) custom-call(s32[1]{0:T(128)} %bitcast.comp_ref, s32[1,1,3,4,4096]{4,3,2,1,0:T(4,128)} %row_ref.3, s32[1,1,3,4,4096]{4,3,2,1,0:T(4,128)} %col_ref.3, f32[2,8,64,512]{3,2,1,0:T(8,128)} %state_ref.3), custom_call_target="tpu_custom_call" | custom-call | tf_op jit(solution)/shard_map/edge_gather/pallas_call | solution.py:399
  5.6 2.1 %collective-permute-start = (f32[8,3328]{1,0:T(8,128)}, f32[8,3328]{1,0:T(8,128)S(1)}, u32[]{:S(2)}, u32[]{:S(2)}) collective-permute-start(f32[8,3328]{1,0:T(8,128)} %get-tuple-element.7), channel_id=1, source_target_pairs={{0,1},{1,2},{2,3},{3,4},{4,5},{5,6},{6,7},{7,8},{8,9},{9,10},{10,1... | collective-permute-start | bytes 319496 | tf_op jit(solution)/shard_map/ppermute | solution.py:418
  7.7 5.7 %collective-permute-start.1 = (f32[8,3328]{1,0:T(8,128)}, f32[8,3328]{1,0:T(8,128)S(1)}, u32[]{:S(2)}, u32[]{:S(2)}) collective-permute-start(f32[8,3328]{1,0:T(8,128)} %get-tuple-element.8), channel_id=1, source_target_pairs={{1,0},{2,1},{3,2},{4,3},{5,4},{6,5},{7,6},{8,7},{9,8},{10,9},{11,1... | collective-permute-start | bytes 319496 | tf_op jit(solution)/shard_map/ppermute | solution.py:419
  13.4 0.0 copy-done.2
  13.4 0.0 copy-done.1
  13.4 0.0 copy-done
  13.4 3.6 %centre_gather.1.centre_ref = f32[3,8,1024]{2,1,0:T(8,128)S(1)} custom-call(s32[1]{0:T(128)} %bitcast.comp_ref, s32[1,1,3,4,4096]{4,3,2,1,0:T(4,128)S(1)} %copy-done.1, s32[1,1,3,4,4096]{4,3,2,1,0:T(4,128)S(1)} %copy-done.2, f32[2,8,64,512]{3,2,1,0:T(8,128)S(1)} %copy-done), custom_call_target="tpu_custom_call" | custom-call | tf_op jit(solution)/shard_map/centre_gather/pallas_call | solution.py:422
  17.1 0.0 copy-done.8
  17.1 0.0 collective-permute-done.from_west.west_ref
  17.1 0.0 collective-permute-done.1.from_east.east_ref
  17.1 0.6 %pack.1 = (f32[3,8,1024]{2,1,0:T(8,128)S(1)}, f32[3,8,1024]{2,1,0:T(8,128)S(1)}, f32[3,8,1024]{2,1,0:T(8,128)S(1)}) custom-call(s32[1]{0:T(128)} %bitcast.comp_ref, s32[3,4]{1,0:T(4,128)S(1)} %bitcast.4, f32[3,8,1024]{2,1,0:T(8,128)S(1)} %centre_gather.1.centre_ref, f32[8,3328]{1,0:T(8,128)S(1)} %collective-permute-done.from_west.west_ref, ...), custom_call_target="tpu_custom_call" | custom-call | tf_op jit(solution)/shard_map/pack/pallas_call | solution.py:430
  17.7 0.1 collective-permute-start.3
  17.8 0.1 collective-permute-start.4
  17.9 0.0 copy-start.3
  17.9 0.0 copy-start.4
  17.9 1.7 %collective-permute-start.2 = (f32[3,8,1024]{2,1,0:T(8,128)S(1)}, f32[3,8,1024]{2,1,0:T(8,128)S(1)}, u32[]{:S(2)}, u32[]{:S(2)}) collective-permute-start(f32[3,8,1024]{2,1,0:T(8,128)S(1)} %get-tuple-element.9.unused_ref), channel_id=1, source_target_pairs={{0,96},{32,64},{64,32},{96,0},{1,97},{33,65},{65,33},{97,1},{2,98}... | collective-permute-start | bytes 294920 | tf_op jit(solution)/shard_map/ppermute | solution.py:441
  19.7 0.0 copy-done.6
  19.7 0.0 copy-done.7
  19.7 3.9 %transport.1.field_hbm = f32[2,8,64,512]{3,2,1,0:T(8,128)} custom-call(f32[2,8,64,512]{3,2,1,0:T(8,128)S(1)} %copy-done, f32[8,64]{1,0:T(8,128)S(1)} %copy-done.6, f32[7,64]{1,0:T(8,128)S(1)} %copy-done.7, f32[8,3328]{1,0:T(8,128)S(1)} %collective-permute-done.from_west.west_ref, f32[8,3328]{1,0:T(8,128)S(1)} %collective-permute-done.1.from_east.east_ref, ...), custom_call_target="tpu_custom_call" | custom-call | tf_op jit(solution)/shard_map/transport/pallas_call | solution.py:443
  23.6 0.0 collective-permute-done.3.got_1
  23.6 0.0 collective-permute-done.4.got_2
  23.6 0.0 collective-permute-done.2.got_0
  23.6 0.0 copy-done.3
  23.6 0.0 copy-done.4
  23.6 0.0 copy-done.5
  23.6 8.1 %land.1 = (f32[2,8,64,512]{3,2,1,0:T(8,128)}, f32[2,64,512]{2,1,0:T(8,128)}) custom-call(s32[1]{0:T(128)} %bitcast.comp_ref, s32[3,4]{1,0:T(4,128)S(1)} %bitcast.5, s32[1,1,3,4,4096]{4,3,2,1,0:T(4,128)S(1)} %copy-done.1, s32[1,1,3,4,4096]{4,3,2,1,0:T(4,128)S(1)} %copy-done.2, f32[1,1,3,4,4096]{4,3,2,1,0:T(4,128)S(1)} %copy-done.3, ...), custom_call_target="tpu_custom_call", output_to_operand_aliasing={{0}: (8, {})} | custom-call | tf_op jit(solution)/shard_map/land/pallas_call | solution.py:457
  (2 shorter events, 0.0 us)
Async XLA Ops:
  0.6 12.8 %copy-start.2 = (s32[1,1,3,4,4096]{4,3,2,1,0:T(4,128)S(1)}, s32[1,1,3,4,4096]{4,3,2,1,0:T(4,128)}, u32[]{:S(2)}) copy-start(s32[1,1,3,4,4096]{4,3,2,1,0:T(4,128)} %col_ref.3) | copy-start | bytes 589828
  0.6 12.8 %copy-start.1 = (s32[1,1,3,4,4096]{4,3,2,1,0:T(4,128)S(1)}, s32[1,1,3,4,4096]{4,3,2,1,0:T(4,128)}, u32[]{:S(2)}) copy-start(s32[1,1,3,4,4096]{4,3,2,1,0:T(4,128)} %row_ref.3) | copy-start | bytes 589828
  0.7 12.8 %copy-start = (f32[2,8,64,512]{3,2,1,0:T(8,128)S(1)}, f32[2,8,64,512]{3,2,1,0:T(8,128)}, u32[]{:S(2)}) copy-start(f32[2,8,64,512]{3,2,1,0:T(8,128)} %state_ref.3) | copy-start | bytes 6291460
  0.7 16.4 %copy-start.8 = (s32[1,1,3,4]{3,1,2,0:T(1,128)S(1)}, s32[1,1,3,4]{3,1,2,0:T(1,128)}, u32[]{:S(2)}) copy-start(s32[1,1,3,4]{3,1,2,0:T(1,128)} %param.14) | copy-start | bytes 148
  0.7 19.0 %copy-start.6 = (f32[8,64]{1,0:T(8,128)S(1)}, f32[8,64]{1,0:T(8,128)}, u32[]{:S(2)}) copy-start(f32[8,64]{1,0:T(8,128)} %courant_ref.1) | copy-start | bytes 6148
  0.7 19.0 %copy-start.7 = (f32[7,64]{1,0:T(8,128)S(1)}, f32[7,64]{1,0:T(8,128)}, u32[]{:S(2)}) copy-start(f32[7,64]{1,0:T(8,128)} %mixing_ref.1) | copy-start | bytes 5380
  5.6 11.5 %collective-permute-start = (f32[8,3328]{1,0:T(8,128)}, f32[8,3328]{1,0:T(8,128)S(1)}, u32[]{:S(2)}, u32[]{:S(2)}) collective-permute-start(f32[8,3328]{1,0:T(8,128)} %get-tuple-element.7), channel_id=1, source_target_pairs={{0,1},{1,2},{2,3},{3,4},{4,5},{5,6},{6,7},{7,8},{8,9},{9,10},{10,1... | collective-permute-start | bytes 319496 | tf_op jit(solution)/shard_map/ppermute | solution.py:418
  7.7 9.4 %collective-permute-start.1 = (f32[8,3328]{1,0:T(8,128)}, f32[8,3328]{1,0:T(8,128)S(1)}, u32[]{:S(2)}, u32[]{:S(2)}) collective-permute-start(f32[8,3328]{1,0:T(8,128)} %get-tuple-element.8), channel_id=1, source_target_pairs={{1,0},{2,1},{3,2},{4,3},{5,4},{6,5},{7,6},{8,7},{9,8},{10,9},{11,1... | collective-permute-start | bytes 319496 | tf_op jit(solution)/shard_map/ppermute | solution.py:419
  17.7 5.8 %collective-permute-start.3 = (f32[3,8,1024]{2,1,0:T(8,128)S(1)}, f32[3,8,1024]{2,1,0:T(8,128)S(1)}, u32[]{:S(2)}, u32[]{:S(2)}) collective-permute-start(f32[3,8,1024]{2,1,0:T(8,128)S(1)} %get-tuple-element.10), channel_id=1, source_target_pairs={{0,64},{32,96},{64,0},{96,32},{1,65},{33,97},{65,1},{97,33},{2,66}... | collective-permute-start | bytes 294920 | tf_op jit(solution)/shard_map/ppermute | solution.py:441
  17.8 5.8 %collective-permute-start.4 = (f32[3,8,1024]{2,1,0:T(8,128)S(1)}, f32[3,8,1024]{2,1,0:T(8,128)S(1)}, u32[]{:S(2)}, u32[]{:S(2)}) collective-permute-start(f32[3,8,1024]{2,1,0:T(8,128)S(1)} %get-tuple-element.11), channel_id=1, source_target_pairs={{0,32},{32,0},{64,96},{96,64},{1,33},{33,1},{65,97},{97,65},{2,34}... | collective-permute-start | bytes 294920 | tf_op jit(solution)/shard_map/ppermute | solution.py:441
  17.9 5.7 %copy-start.3 = (f32[1,1,3,4,4096]{4,3,2,1,0:T(4,128)S(1)}, f32[1,1,3,4,4096]{4,3,2,1,0:T(4,128)}, u32[]{:S(2)}) copy-start(f32[1,1,3,4,4096]{4,3,2,1,0:T(4,128)} %weight_ref.1) | copy-start | bytes 589828
  17.9 5.7 %copy-start.4 = (f32[64,512]{1,0:T(8,128)S(1)}, f32[64,512]{1,0:T(8,128)}, u32[]{:S(2)}) copy-start(f32[64,512]{1,0:T(8,128)} %coef_ref.1) | copy-start | bytes 393220
  17.9 5.7 %copy-start.5 = (s32[64,512]{1,0:T(8,128)S(1)}, s32[64,512]{1,0:T(8,128)}, u32[]{:S(2)}) copy-start(s32[64,512]{1,0:T(8,128)} %mask_ref.1) | copy-start | bytes 393220
  17.9 5.6 %collective-permute-start.2 = (f32[3,8,1024]{2,1,0:T(8,128)S(1)}, f32[3,8,1024]{2,1,0:T(8,128)S(1)}, u32[]{:S(2)}, u32[]{:S(2)}) collective-permute-start(f32[3,8,1024]{2,1,0:T(8,128)S(1)} %get-tuple-element.9.unused_ref), channel_id=1, source_target_pairs={{0,96},{32,64},{64,32},{96,0},{1,97},{33,65},{65,33},{97,1},{2,98}... | collective-permute-start | bytes 294920 | tf_op jit(solution)/shard_map/ppermute | solution.py:441
